TPU v7x, 32 devices: a whole 2x2x4 slice. The times are simulated.
32 devices in a mesh: dp: 2 (over core), seq: 4 (over z), fsdp: 4 (over y, x).
Axes of the slice: x: 2, y: 2, z: 4, core: 2. Of those that a mesh axis runs over, the one named last changes fastest.
Arguments:
- hidden_in: bfloat16 [16, 512, 1024], P(('dp', 'fsdp'), 'seq'), may hold values from -6 to 6
- lengths: int32 [16], P(('dp', 'fsdp')), may hold values from 1 to 512, as said below
- norm_gain: float32 [1024], P('fsdp'), may hold values from 0.5 to 1.5
- in_weight: bfloat16 [1024, 4096], P('fsdp'), may hold values from -0.1875 to 0.1875
- conv_weight: float32 [4, 2048], P(None, 'fsdp'), may hold values from -2.5 to 2.5
- conv_bias: float32 [2048], P('fsdp'), may hold values from -0.5 to 0.5
- xproj_weight: bfloat16 [2048, 96], P('fsdp'), may hold values from -0.125 to 0.125
- dt_weight: bfloat16 [64, 2048], P(None, 'fsdp'), may hold values from -0.75 to 0.75
- dt_bias: float32 [2048], P('fsdp'), may hold values from -4.5 to -2
- a_log: float32 [16, 2048], P(None, 'fsdp'), may hold values from -4 to 2.5
- skip_gain: float32 [2048], P('fsdp'), may hold values from 0.5 to 1.5
- out_weight: bfloat16 [2048, 1024], P('fsdp'), may hold values from -0.125 to 0.125
- out_grad: bfloat16 [16, 512, 1024], P(('dp', 'fsdp'), 'seq'), may hold values from -6 to 6
Outputs:
- hidden_out: bfloat16 [16, 512, 1024], P(('dp', 'fsdp'), 'seq')
- input_grad: bfloat16 [16, 512, 1024], P(('dp', 'fsdp'), 'seq')
- grad_norm_gain: float32 [1024], P('fsdp')
- grad_in_weight: float32 [1024, 4096], P('fsdp')
- grad_conv_weight: float32 [4, 2048], P(None, 'fsdp')
- grad_conv_bias: float32 [2048], P('fsdp')
- grad_xproj_weight: float32 [2048, 96], P('fsdp')
- grad_dt_weight: float32 [64, 2048], P(None, 'fsdp')
- grad_dt_bias: float32 [2048], P('fsdp')
- grad_a_log: float32 [16, 2048], P(None, 'fsdp')
- grad_skip_gain: float32 [2048], P('fsdp')
- grad_out_weight: float32 [2048, 1024], P('fsdp')
Inputs may be any that keep to these rules, and one draw needn't show every extreme that they name: `lengths`: in each aligned run of 2 contexts (those of one group of the seq axis) one context has all 512 tokens valid; padding lies after a context's valid tokens.
All inputs are finite; a program needn't handle non-finite values.
Results may differ from a plain program's by a relative error of at most 0.012.
Values may be sent and summed in bfloat16 or wider, within the bound.
A program may use at most 256 MiB of HBM per device.

v0:
```python
import math

import jax
import jax.numpy as jnp
from jax import lax
from jax.sharding import PartitionSpec as P

EPS = 1e-05


def passed_along(value, axis, by):
    size = lax.axis_size(axis)
    pairs = [(i, i + by) for i in range(size) if 0 <= i + by < size]
    return lax.ppermute(value, axis, pairs)


def silu_grad(v):
    s = jax.nn.sigmoid(v)
    return s * (1.0 + v * (1.0 - s))


def join_carry(earlier, later):
    return (earlier[0] * later[0], later[0] * earlier[1] + later[1])


def linear_prefix(decays, inputs):
    return lax.associative_scan(join_carry, (decays, inputs), axis=0)


def body(
    hidden_in,
    lengths,
    norm_gain,
    in_weight,
    conv_weight,
    conv_bias,
    xproj_weight,
    dt_weight,
    dt_bias,
    a_log,
    skip_gain,
    out_weight,
    out_grad,
):
    seqs, ctx, width = hidden_in.shape
    taps = conv_weight.shape[0]
    reach = taps - 1
    in_matrix, proj_matrix, step_matrix, out_matrix = (
        lax.all_gather(in_weight, "fsdp", axis=0, tiled=True),
        lax.all_gather(xproj_weight, "fsdp", axis=0, tiled=True),
        lax.all_gather(dt_weight, "fsdp", axis=1, tiled=True),
        lax.all_gather(out_weight, "fsdp", axis=0, tiled=True),
    )
    gain, conv_taps, conv_shift, step_bias, log_rate, skip = (
        lax.all_gather(norm_gain, "fsdp", axis=0, tiled=True),
        lax.all_gather(conv_weight, "fsdp", axis=1, tiled=True),
        lax.all_gather(conv_bias, "fsdp", axis=0, tiled=True),
        lax.all_gather(dt_bias, "fsdp", axis=0, tiled=True),
        lax.all_gather(a_log, "fsdp", axis=1, tiled=True),
        lax.all_gather(skip_gain, "fsdp", axis=0, tiled=True),
    )
    inner = proj_matrix.shape[0]
    state = log_rate.shape[0]
    rank = step_matrix.shape[0]
    rows = ctx * seqs
    block = math.gcd(ctx, 32)
    count = ctx // block

    def split_blocks(v):
        return v.reshape((count, block) + v.shape[1:])

    x_tok = jnp.transpose(hidden_in, (1, 0, 2)).astype(jnp.float32)
    position = lax.axis_index("seq") * ctx + jnp.arange(ctx, dtype=jnp.int32)
    mask = (position[:, None] < lengths[None, :]).astype(jnp.float32)
    inverse = lax.rsqrt(jnp.mean(x_tok * x_tok, -1, keepdims=True) + EPS)
    normed = (x_tok * inverse * gain).astype(jnp.bfloat16).reshape(rows, width)
    mixed = jnp.dot(normed, in_matrix, preferred_element_type=jnp.float32).astype(jnp.bfloat16)
    stream = mixed[:, :inner].reshape(ctx, seqs, inner)
    gate_in = mixed[:, inner:].astype(jnp.float32).reshape(ctx, seqs, inner)
    before = passed_along(stream[ctx - reach :], "seq", 1)
    extended = jnp.concatenate([before, stream], 0).astype(jnp.float32)
    conv_out = conv_shift + sum((conv_taps[k] * extended[k : k + ctx] for k in range(taps)))
    u_low = jax.nn.silu(conv_out).astype(jnp.bfloat16)
    u_rows = u_low.reshape(rows, inner)
    proj = jnp.dot(u_rows, proj_matrix, preferred_element_type=jnp.float32)
    step_low = proj[:, :rank].astype(jnp.bfloat16)
    b_in = proj[:, rank : rank + state].reshape(ctx, seqs, state)
    c_in = proj[:, rank + state :].reshape(ctx, seqs, state)
    raw = (
        jnp.dot(step_low, step_matrix, preferred_element_type=jnp.float32).reshape(ctx, seqs, inner)
        + step_bias
    )
    delta = jax.nn.softplus(raw)
    rates = -jnp.exp(log_rate)
    u_float = u_low.astype(jnp.float32)
    drive = delta * u_float

    def block_terms(d, v, b):
        factors = jnp.exp(d[:, :, None, :] * rates)
        inputs = v[:, :, None, :] * b[:, :, :, None]
        return (factors, linear_prefix(factors, inputs))

    def end_block(h, item):
        _, (decay_run, local_run) = block_terms(item[0], item[1], item[2])
        return (decay_run[-1] * h + local_run[-1], None)

    zero_state = jnp.zeros((seqs, state, inner), jnp.float32)
    local_end, _ = lax.scan(
        end_block, zero_state, (split_blocks(delta), split_blocks(drive), split_blocks(b_in))
    )
    total_decay = jnp.exp(jnp.sum(delta, 0)[:, None, :] * rates)

    def relay_fwd(turn, incoming):
        return passed_along(total_decay * incoming + local_end, "seq", 1)

    start_state = lax.fori_loop(0, lax.axis_size("seq") - 1, relay_fwd, zero_state)

    def run_block(h, item):
        d, v, b, c = item
        _, (decay_run, local_run) = block_terms(d, v, b)
        states = decay_run * h[None] + local_run
        outputs = jnp.sum(c[:, :, :, None] * states, 2)
        return (states[-1], (h, outputs))

    blocked = (split_blocks(delta), split_blocks(drive), split_blocks(b_in), split_blocks(c_in))
    _, (block_starts, scanned) = lax.scan(run_block, start_state, blocked)
    y_val = scanned.reshape(ctx, seqs, inner) + skip * u_float
    gate_act = jax.nn.silu(gate_in)
    gated = (y_val * gate_act).astype(jnp.bfloat16).reshape(rows, inner)
    branch = jnp.dot(gated, out_matrix, preferred_element_type=jnp.float32).reshape(
        ctx, seqs, width
    )
    hidden_out = jnp.transpose((x_tok + mask[:, :, None] * branch).astype(jnp.bfloat16), (1, 0, 2))
    in_back, proj_back, step_back, out_back = (in_matrix, proj_matrix, step_matrix, out_matrix)
    cotangent = jnp.transpose(out_grad, (1, 0, 2)).astype(jnp.float32)
    branch_grad = (cotangent * mask[:, :, None]).astype(jnp.bfloat16).reshape(rows, width)
    out_w_grad = jnp.einsum("ri,rd->id", gated, branch_grad, preferred_element_type=jnp.float32)
    gated_grad = jnp.einsum(
        "rd,id->ri", branch_grad, out_back, preferred_element_type=jnp.float32
    ).reshape(ctx, seqs, inner)
    y_grad = gated_grad * gate_act
    z_grad = gated_grad * y_val * silu_grad(gate_in)
    skip_grad = jnp.sum(y_grad * u_float, (0, 1))

    def back_terms(d, c, dy):
        factors = jnp.exp(d[:, :, None, :] * rates)
        sources = c[:, :, :, None] * dy[:, :, None, :]
        flipped = linear_prefix(factors[::-1], (factors * sources)[::-1])
        return (factors, sources, flipped[0][::-1], flipped[1][::-1])

    def back_end(p_in, item):
        _, _, decay_run, local_run = back_terms(item[0], item[1], item[2])
        return (decay_run[0] * p_in + local_run[0], None)

    local_back, _ = lax.scan(
        back_end,
        zero_state,
        (split_blocks(delta), split_blocks(c_in), split_blocks(y_grad)),
        reverse=True,
    )

    def relay_back(turn, incoming):
        return passed_along(total_decay * incoming + local_back, "seq", -1)

    end_grad = lax.fori_loop(0, lax.axis_size("seq") - 1, relay_back, zero_state)

    def grad_block(carry, item):
        p_in, rate_acc = carry
        first, d, v, b, c, dy = item
        _, (decay_fwd, local_fwd) = block_terms(d, v, b)
        h_now = decay_fwd * first[None] + local_fwd
        h_prev = jnp.concatenate([first[None], h_now[:-1]], 0)
        factors, sources, decay_back, local_back_run = back_terms(d, c, dy)
        passed = decay_back * p_in[None] + local_back_run
        following = jnp.concatenate([passed[1:], p_in[None]], 0)
        g = sources + following
        c_grad = jnp.sum(h_now * dy[:, :, None, :], 3)
        b_grad = jnp.sum(g * v[:, :, None, :], 3)
        drive_grad = jnp.sum(g * b[:, :, :, None], 2)
        hold = g * h_prev * factors
        delta_part = jnp.sum(hold * rates, 2)
        rate_acc = rate_acc + jnp.sum(hold * d[:, :, None, :], (0, 1))
        return ((passed[0], rate_acc), (c_grad, b_grad, drive_grad, delta_part))

    start_carry = (end_grad, jnp.zeros((state, inner), jnp.float32))
    blocked_back = (
        block_starts,
        split_blocks(delta),
        split_blocks(drive),
        split_blocks(b_in),
        split_blocks(c_in),
        split_blocks(y_grad),
    )
    (_, rate_grad), (c_grad, b_grad, drive_grad, delta_part) = lax.scan(
        grad_block, start_carry, blocked_back, reverse=True
    )
    c_grad = c_grad.reshape(rows, state)
    b_grad = b_grad.reshape(rows, state)
    drive_grad = drive_grad.reshape(ctx, seqs, inner)
    delta_grad = drive_grad * u_float + delta_part.reshape(ctx, seqs, inner)
    u_grad = y_grad * skip + drive_grad * delta
    log_grad = rate_grad * rates
    raw_grad = delta_grad * jax.nn.sigmoid(raw)
    bias_grad = jnp.sum(raw_grad, (0, 1))
    raw_low = raw_grad.astype(jnp.bfloat16).reshape(rows, inner)
    step_w_grad = jnp.einsum("rk,ri->ki", step_low, raw_low, preferred_element_type=jnp.float32)
    step_grad = jnp.einsum("ri,ki->rk", raw_low, step_back, preferred_element_type=jnp.float32)
    proj_grad = jnp.concatenate([step_grad, b_grad, c_grad], 1).astype(jnp.bfloat16)
    proj_w_grad = jnp.einsum("ri,rp->ip", u_rows, proj_grad, preferred_element_type=jnp.float32)
    u_grad = u_grad + jnp.einsum(
        "rp,ip->ri", proj_grad, proj_back, preferred_element_type=jnp.float32
    ).reshape(ctx, seqs, inner)
    conv_grad = u_grad * silu_grad(conv_out)
    shift_grad = jnp.sum(conv_grad, (0, 1))
    taps_grad = jnp.stack(
        [jnp.sum(conv_grad * extended[k : k + ctx], (0, 1)) for k in range(taps)], 0
    )
    extended_grad = sum(
        (jnp.pad(conv_taps[k] * conv_grad, ((k, reach - k), (0, 0), (0, 0))) for k in range(taps))
    )
    arrived = passed_along(extended_grad[:reach], "seq", -1)
    stream_grad = extended_grad[reach:] + jnp.pad(arrived, ((ctx - reach, 0), (0, 0), (0, 0)))
    mixed_grad = jnp.concatenate(
        [stream_grad.reshape(rows, inner), z_grad.reshape(rows, inner)], 1
    ).astype(jnp.bfloat16)
    in_w_grad = jnp.einsum("rd,rj->dj", normed, mixed_grad, preferred_element_type=jnp.float32)
    normed_grad = jnp.einsum(
        "rj,dj->rd", mixed_grad, in_back, preferred_element_type=jnp.float32
    ).reshape(ctx, seqs, width)
    gain_grad = jnp.sum(normed_grad * x_tok * inverse, (0, 1))
    scaled = normed_grad * gain
    x_grad = (
        inverse * scaled
        - x_tok * inverse * inverse * inverse * jnp.mean(scaled * x_tok, -1, keepdims=True)
        + cotangent
    )
    input_grad = jnp.transpose(x_grad.astype(jnp.bfloat16), (1, 0, 2))
    shards = (
        lax.psum_scatter(gain_grad, "fsdp", scatter_dimension=0, tiled=True),
        lax.psum_scatter(in_w_grad, "fsdp", scatter_dimension=0, tiled=True),
        lax.psum_scatter(taps_grad, "fsdp", scatter_dimension=1, tiled=True),
        lax.psum_scatter(shift_grad, "fsdp", scatter_dimension=0, tiled=True),
        lax.psum_scatter(proj_w_grad, "fsdp", scatter_dimension=0, tiled=True),
        lax.psum_scatter(step_w_grad, "fsdp", scatter_dimension=1, tiled=True),
        lax.psum_scatter(bias_grad, "fsdp", scatter_dimension=0, tiled=True),
        lax.psum_scatter(log_grad, "fsdp", scatter_dimension=1, tiled=True),
        lax.psum_scatter(skip_grad, "fsdp", scatter_dimension=0, tiled=True),
        lax.psum_scatter(out_w_grad, "fsdp", scatter_dimension=0, tiled=True),
    )
    summed = lax.psum(
        (
            shards[0],
            shards[1],
            shards[2],
            shards[3],
            shards[4],
            shards[5],
            shards[6],
            shards[7],
            shards[8],
            shards[9],
        ),
        ("dp", "seq"),
    )
    return (
        hidden_out,
        input_grad,
        summed[0],
        summed[1],
        summed[2],
        summed[3],
        summed[4],
        summed[5],
        summed[6],
        summed[7],
        summed[8],
        summed[9],
    )


def solution(mesh):
    return jax.shard_map(
        body,
        mesh=mesh,
        in_specs=(
            P(("dp", "fsdp"), "seq", None),
            P(("dp", "fsdp")),
            P("fsdp"),
            P("fsdp", None),
            P(None, "fsdp"),
            P("fsdp"),
            P("fsdp", None),
            P(None, "fsdp"),
            P("fsdp"),
            P(None, "fsdp"),
            P("fsdp"),
            P("fsdp", None),
            P(("dp", "fsdp"), "seq", None),
        ),
        out_specs=(
            P(("dp", "fsdp"), "seq", None),
            P(("dp", "fsdp"), "seq", None),
            P("fsdp"),
            P("fsdp", None),
            P(None, "fsdp"),
            P("fsdp"),
            P("fsdp", None),
            P(None, "fsdp"),
            P("fsdp"),
            P(None, "fsdp"),
            P("fsdp"),
            P("fsdp", None),
        ),
        check_vma=False,
    )
```

profile of v0, /device:TPU:25, one launch (start us, length us, event | category | flops | bytes accessed | tf_op | source)
XLA Modules:
  0.0 5793.0 jit_solution(12405451351417979773)
XLA Ops:
  70.4 33.8 all-gather.7.cloned.1.call-done
  119.5 39.3 all-gather.9.cloned.1.call-done
  193.3 776.1 %while.90 = (s32[]{:T(128)}, f32[2,16,2048]{2,1,0:T(8,128)}, f32[4,32,2,2048]{3,2,1,0:T(2,128)}, f32[16,2048]{1,0:T(8,128)S(1)}, f32[4,32,2,2048]{3,2,1,0:T(2,12...) while((s32[]{:T(128)}, f32[2,16,2048]{2,1,0:T(8,128)}, ...), condition=%wide.region_3.4_spmd.clone, body=%wide.region_2.3_spmd.clone.sunk | while | flops 19988484 | bytes 287060448 | solution.py:108
  308.2 21.2 pad.1378
  502.1 21.2 pad.1378
  696.1 21.2 pad.1378
  890.0 21.2 pad.1378
  971.0 27.4 while.88
  1000.0 1098.1 %while.87 = (s32[]{:T(128)}, f32[2,16,2048]{2,1,0:T(8,128)S(1)}, f32[4,2,16,2048]{3,2,1,0:T(8,128)}, f32[4,32,2,2048]{3,1,0,2:T(8,128)}, f32[4,32,2,2048]{3,2,1,...) while((s32[]{:T(128)}, f32[2,16,2048]{2,1,0:T(8,128)S(1)}, ...), condition=%wide.region_8.9_spmd, body=%wide.region_6.8_spmd.sunk | while | flops 39124992 | bytes 406250016 | solution.py:126
  1157.4 21.2 pad.1348
  1210.8 21.2 pad.1350
  1431.8 21.2 pad.1348
  1485.2 21.2 pad.1350
  1513.0 21.2 pad.1351
  1706.2 21.2 pad.1348
  1759.6 21.2 pad.1350
  1787.4 21.2 pad.1351
  1980.6 21.2 pad.1348
  2034.0 21.2 pad.1350
  2061.7 21.2 pad.1351
  2102.6 788.0 %while.91 = (s32[]{:T(128)}, f32[2,16,2048]{2,1,0:T(8,128)}, f32[4,32,2,2048]{3,2,1,0:T(2,128)}, f32[16,2048]{1,0:T(8,128)S(1)}, f32[4,32,2,16]{3,2,1,0:T(2,128)...) while((s32[]{:T(128)}, f32[2,16,2048]{2,1,0:T(8,128)}, ...), condition=%wide.region_10.11_spmd.clone, body=%wide.region_9.10_spmd.clone.sunk | while | flops 22085636 | bytes 320483776 | solution.py:155
  2220.2 21.2 pad.1408
  2417.2 21.2 pad.1408
  2614.2 21.2 pad.1408
  2811.1 21.2 pad.1408
  2890.7 22.7 while.89
  2917.9 2337.1 %while.92 = (s32[]{:T(128)}, f32[2,16,2048]{2,1,0:T(8,128)}, f32[16,2048]{1,0:T(8,128)}, bf16[4,32,2,16]{3,2,1,0:T(2,128)(2,1)}, bf16[4,32,2,16]{3,2,1,0:T(2,128...) while((s32[]{:T(128)}, f32[2,16,2048]{2,1,0:T(8,128)}, ...), condition=%wide.region_19.20_spmd.clone, body=%wide.region_13.19_spmd.clone.sunk | while | flops 105543680 | bytes 1091199744 | solution.py:194
  3131.4 21.3 pad.1486
  3159.4 21.2 pad.1487
  3371.4 21.2 pad.1481
  3434.4 21.2 pad.1483
  3713.7 21.5 pad.1486
  3741.8 21.2 pad.1487
  3953.6 21.2 pad.1481
  4016.6 21.2 pad.1483
  4296.1 21.3 pad.1486
  4324.0 21.2 pad.1487
  4535.8 21.2 pad.1481
  4598.8 21.2 pad.1483
  4878.3 21.3 pad.1486
  4906.2 21.2 pad.1487
  5118.2 21.2 pad.1481
  5181.2 21.2 pad.1483
  5326.6 89.6 %reduce-scatter.17.cloned.1.call-done = f32[512,1024]{1,0:T(8,128)} async-done(((f32[2048,1024]{1,0:T(8,128)}), f32[512,1024]{1,0:T(8,128)}) %reduce-scatter.17.cloned.1.call-update) | async-done | bytes 2097168 | tf_op jit(solution)/shard_map/reduce_scatter | solution.py:248
  5416.2 156.8 %reduce-scatter.9.cloned.1.call-done = f32[256,4096]{1,0:T(8,128)} async-done(((f32[1024,4096]{1,0:T(8,128)}), f32[256,4096]{1,0:T(8,128)}) %reduce-scatter.9.cloned.1.call-update) | async-done | bytes 4194320 | tf_op jit(solution)/shard_map/reduce_scatter | solution.py:240
  5605.6 25.9 reduce-scatter.15.cloned.1.call-done
  5631.4 30.7 all-reduce.109
  5662.1 116.7 %all-reduce.114.cloned.1.call-done = (f32[256,4096]{1,0:T(8,128)}, f32[512,96]{0,1:T(8,128)}, f32[64,512]{1,0:T(8,128)}, f32[512,1024]{1,0:T(8,128)}) async-done(((f32[256,4096]{1,0:T(8,128)}, f32[512,96]{0,1:T(8,128)}, f32[64,512]{1,0:T(8,128)}, f32[512,1024]{1,0:T(8,128)}), (f32[256,4096]{1,0:T(8,128)}, f32[512,96]{0,1:T(8,128)}, f32[64,512]{1,0:T(8,128)}, ...) | async-done | bytes 6619152 | tf_op jit(solution)/shard_map/psum | solution.py:250
  (1915 shorter events, 4527.9 us)
Async XLA Ops:
  7.2 97.1 %all-gather.7.cloned.1.call-start = ((), (), s32[]{:S(2)}) async-start(), calls=%async_computation.6 | async-start | bytes 10485760 | tf_op jit(solution)/shard_map/all_gather | solution.py:49
  7.9 150.9 %all-gather.9.cloned.1.call-start = ((), (), s32[]{:S(2)}) async-start(), calls=%async_computation.7 | async-start | bytes 5242880 | tf_op jit(solution)/shard_map/all_gather | solution.py:52
  8.7 27.7 copy-start.129
  8.7 34.1 copy-start.126
  8.7 40.3 copy-start.116
  8.7 5304.3 %reduce-scatter.13.cloned.1.call-start = ((), (), s32[]{:S(2)}) async-start(), calls=%async_computation.10 | async-start | bytes 655360 | tf_op jit(solution)/shard_map/reduce_scatter | solution.py:244
  14.9 42.0 copy-start.112
  15.7 53.5 copy-start.137
  16.6 93.4 %copy-start.90 = (bf16[256,1024]{1,0:T(8,128)(2,1)}, bf16[256,1024]{1,0:T(8,128)(2,1)S(1)}, u32[]{:S(2)}) copy-start(bf16[256,1024]{1,0:T(8,128)(2,1)S(1)} %reshape.190) | copy-start | bytes 1572868
  29.6 157.3 %copy-start.108 = (f32[4,1,512]{2,1,0:T(1,128)}, f32[4,1,512]{2,1,0:T(1,128)S(1)}, u32[]{:S(2)}) copy-start(f32[4,1,512]{2,1,0:T(1,128)S(1)} %all-gather.2) | copy-start | bytes 24580
  56.9 115.7 %copy-start.92 = (bf16[64,2048]{1,0:T(8,128)(2,1)}, bf16[64,2048]{1,0:T(8,128)(2,1)S(1)}, u32[]{:S(2)}) copy-start(bf16[64,2048]{1,0:T(8,128)(2,1)S(1)} %all_gather.35) | copy-start | bytes 786436
  70.4 88.4 %copy-start.118 = (f32[1,2048]{1,0:T(1,128)}, f32[1,2048]{1,0:T(1,128)S(1)}, u32[]{:S(2)}) copy-start(f32[1,2048]{1,0:T(1,128)S(1)} %get-tuple-element.1039) | copy-start | bytes 24580
  111.4 7.0 collective-permute-start.2
  118.3 40.5 copy-start.96
  118.3 40.5 copy-start.120
  118.3 40.5 copy-start.122
  118.3 40.5 copy-start.124
  118.3 40.5 copy-start.131
  118.3 40.5 copy-start.132
  119.5 49.1 copy-start.57
  193.3 777.7 %copy-start.99 = (f32[2,2048]{1,0:T(2,128)S(1)}, f32[2,2048]{1,0:T(2,128)}, u32[]{:S(2)}) copy-start(f32[2,2048]{1,0:T(2,128)} %get-tuple-element.1716) | copy-start | bytes 49156
  308.2 22.1 copy-start.35
  364.7 22.9 copy-start.103
  502.1 22.1 copy-start.35
  558.6 22.9 copy-start.103
  752.6 22.9 copy-start.103
  946.5 22.9 copy-start.103
  972.0 9.1 collective-permute-start
  982.1 8.1 collective-permute-start
  991.2 7.1 collective-permute-start
  1026.9 23.9 copy-start.15
  1301.3 23.9 copy-start.15
  1575.7 23.9 copy-start.15
  1850.1 23.9 copy-start.15
  2102.6 788.0 %copy-start.100 = (f32[2,2048]{1,0:T(2,128)S(1)}, f32[2,2048]{1,0:T(2,128)}, u32[]{:S(2)}) copy-start(f32[2,2048]{1,0:T(2,128)} %get-tuple-element.1716) | copy-start | bytes 49156
  2417.2 22.1 copy-start.36
  2891.7 5.5 collective-permute-start.1
  2898.1 7.1 collective-permute-start.1
  2906.3 7.1 collective-permute-start.1
  2917.9 2337.1 %copy-start.109 = (f32[4,1,512]{2,1,0:T(1,128)S(1)}, f32[4,1,512]{2,1,0:T(1,128)}, u32[]{:S(2)}) copy-start(f32[4,1,512]{2,1,0:T(1,128)} %copy-done.108) | copy-start | bytes 24580
  2917.9 2337.1 %copy-start.113 = (f32[4,1,512]{2,1,0:T(1,128)S(1)}, f32[4,1,512]{2,1,0:T(1,128)}, u32[]{:S(2)}) copy-start(f32[4,1,512]{2,1,0:T(1,128)} %all-gather.3) | copy-start | bytes 24580
  5265.5 61.1 %reduce-scatter.11.cloned.1.call-start = ((), (), s32[]{:S(2)}) async-start(), calls=%async_computation.9 | async-start | bytes 983040 | tf_op jit(solution)/shard_map/reduce_scatter | solution.py:243
  5269.1 147.2 %reduce-scatter.17.cloned.1.call-start = ((), (), s32[]{:S(2)}) async-start(), calls=%async_computation.12 | async-start | bytes 10485760 | tf_op jit(solution)/shard_map/reduce_scatter | solution.py:248
  5273.8 299.2 %reduce-scatter.9.cloned.1.call-start = ((), (), s32[]{:S(2)}) async-start(), calls=%async_computation.8 | async-start | bytes 20971520 | tf_op jit(solution)/shard_map/reduce_scatter | solution.py:240
  5287.6 9.5 collective-permute-start.3
  5310.8 293.7 %reduce-scatter.19.cloned.1.call-start = ((), (), s32[]{:S(2)}) async-start(), calls=%async_computation.13 | async-start | bytes 1310720
  5312.2 319.2 %reduce-scatter.15.cloned.1.call-start = ((), (), s32[]{:S(2)}) async-start(), calls=%async_computation.11 | async-start | bytes 163840 | tf_op jit(solution)/shard_map/reduce_scatter | solution.py:246
  5313.0 465.8 %all-reduce.114.cloned.1.call-start = ((), (), s32[]{:S(2)}) async-start(), calls=%async_computation.14 | async-start | bytes 13238272 | tf_op jit(solution)/shard_map/psum | solution.py:250
  (354 other events, 2453.4 us)
Sparse Core Ops, SparseCore 0:
  9.9 94.3 all-gather.6
  106.1 52.6 all-gather.8
  5265.6 31.7 reduce-scatter.12
  5300.4 26.1 reduce-scatter.10
  5329.8 86.3 reduce-scatter.16
  5419.2 153.8 reduce-scatter.8
  5576.5 27.9 reduce-scatter.18
  5608.0 23.3 reduce-scatter.14
  5634.1 144.7 all-reduce.113
where the time goes:
time: 5860 us; the launch traced here: 5790 us
  local copies, waits for them, and re-layouts  3270 us (56%)
  other arithmetic  1810 us (31%)
  waiting for transfers between devices  511 us (9%)
  blocking collectives  101 us (2%)
    pad x288, local copies, waits for them, and re-layouts, linear_prefix(): return lax.associative_scan(join_carry, (decays, inputs), axis=0)  2510 us
    mul x144, other arithmetic, join_carry(): return (earlier[0] * later[0], later[0] * earlier[1] + later[1])  625 us
    add x168, other arithmetic, linear_prefix(): return lax.associative_scan(join_carry, (decays, inputs), axis=0)  591 us
    while x608, local copies, waits for them, and re-layouts  430 us
    concatenate x144, other arithmetic, linear_prefix(): return lax.associative_scan(join_carry, (decays, inputs), axis=0)  209 us
    slice x128, local copies, waits for them, and re-layouts, linear_prefix(): return lax.associative_scan(join_carry, (decays, inputs), axis=0)  167 us
    reduce_scatter x1, waiting for transfers between devices, body(): lax.psum_scatter(in_w_grad, 'fsdp', scatter_dimension=0, tiled=True)  157 us
  transfers between devices with their start and end apart: 17, of which 14 were waited for; matrix products, arithmetic and copies ran while one was open for 1% of the time, Pallas kernels for 0%

commit v1 on v0

v1 whole, which is shorter than its diff:
```python
import functools
import math

import jax
import jax.numpy as jnp
import numpy as np
from jax import lax
from jax.experimental import pallas as pl
from jax.experimental.pallas import tpu as pltpu
from jax.sharding import PartitionSpec as P

EPS = 1e-05
LOG2E = math.log2(math.e)
LANES = 128
GROUP = 16
F32 = jnp.float32
BF16 = jnp.bfloat16
MESH = pl.DeviceIdType.MESH
HR = 128
CHUNK = 512
SLACK = 1


def passed_along(value, axis, by):
    size = lax.axis_size(axis)
    pairs = [(i, i + by) for i in range(size) if 0 <= i + by < size]
    return lax.ppermute(value, axis, pairs)


def silu_grad(v):
    s = jax.nn.sigmoid(v)
    return s * (1.0 + v * (1.0 - s))


def ends_kernel(d_ref, v_ref, dy_ref, b_ref, c_ref, a_ref, h_ref, p_ref):
    state, width = a_ref.shape
    groups = d_ref.shape[1]
    cuts = [slice(j, j + LANES) for j in range(0, width, LANES)]
    rates = [a_ref[:, s] for s in cuts]

    def step(i, carry):
        h, run, p = (list(v) for v in carry)
        for k in range(GROUP):
            b = b_ref[0, i * GROUP + k]
            c = c_ref[0, i * GROUP + k]
            for j, s in enumerate(cuts):
                row = lambda ref: jnp.broadcast_to(ref[0, i, k : k + 1, s], (state, LANES))
                factor = jnp.exp2(row(d_ref) * rates[j])
                h[j] = factor * h[j] + row(v_ref) * b
                run[j] = run[j] * factor
                p[j] = p[j] + run[j] * (c * row(dy_ref))
        return tuple(h), tuple(run), tuple(p)

    zero = tuple(jnp.zeros((state, LANES), F32) for _ in cuts)
    one = tuple(jnp.ones((state, LANES), F32) for _ in cuts)
    h, _, p = lax.fori_loop(0, groups, step, (zero, one, zero))
    for j, s in enumerate(cuts):
        h_ref[0, :, s] = h[j]
        p_ref[0, :, s] = p[j]


def sweep_kernel(
    d_ref, v_ref, dy_ref, b_ref, c_ref, a_ref, h0_ref, p0_ref, cbd_ref, bbd_ref, one_ref,
    y_ref, dg_ref, dp_ref, cacc_ref, bacc_ref, racc_ref, h_s, a_s, g_s, w_s,
):
    state, width = a_ref.shape
    groups = d_ref.shape[1]
    cuts = [slice(j, j + LANES) for j in range(0, width, LANES)]
    rates = [a_ref[:, s] for s in cuts]
    across = (((1,), (1,)), ((), ()))

    @pl.when(pl.program_id(1) == 0)
    def _():
        cacc_ref[...] = jnp.zeros_like(cacc_ref)
        bacc_ref[...] = jnp.zeros_like(bacc_ref)

    h_s[0] = h0_ref[0]

    def forward(i, h):
        h = list(h)
        for k in range(GROUP):
            t = i * GROUP + k
            b = b_ref[0, t]
            for j, s in enumerate(cuts):
                row = lambda ref: jnp.broadcast_to(ref[0, i, k : k + 1, s], (state, LANES))
                factor = jnp.exp2(row(d_ref) * rates[j])
                h[j] = factor * h[j] + row(v_ref) * b
                h_s[t + 1, :, s] = h[j]
                a_s[t, :, s] = factor
        held = h_s[pl.ds(i * GROUP + 1, GROUP)].reshape(GROUP * state, width).astype(BF16)
        y_ref[0, i] = jnp.dot(cbd_ref[0, i], held, preferred_element_type=F32)
        cacc_ref[0, i] += lax.dot_general(
            dy_ref[0, i].astype(BF16), held, across, preferred_element_type=F32
        )
        return tuple(h)

    lax.fori_loop(0, groups, forward, tuple(h0_ref[0, :, s] for s in cuts))

    def backward(turn, carry):
        i = groups - 1 - turn
        p, total = (list(v) for v in carry)
        for k in reversed(range(GROUP)):
            t = i * GROUP + k
            c = c_ref[0, t]
            for j, s in enumerate(cuts):
                row = lambda ref: jnp.broadcast_to(ref[0, i, k : k + 1, s], (state, LANES))
                g = c * row(dy_ref) + p[j]
                p[j] = a_s[t, :, s] * g
                w = p[j] * h_s[t, :, s]
                total[j] = total[j] + w * row(d_ref)
                g_s[k, :, s] = g.astype(BF16)
                w_s[k, :, s] = (w * rates[j]).astype(BF16)
        g_all = g_s[...].reshape(GROUP * state, width)
        dg_ref[0, i] = jnp.dot(bbd_ref[0, i], g_all, preferred_element_type=F32)
        dp_ref[0, i] = jnp.dot(
            one_ref[...], w_s[...].reshape(GROUP * state, width), preferred_element_type=F32
        )
        bacc_ref[0, i] += lax.dot_general(
            v_ref[0, i].astype(BF16), g_all, across, preferred_element_type=F32
        )
        return tuple(p), tuple(total)

    zero = tuple(jnp.zeros((state, LANES), F32) for _ in cuts)
    start = tuple(p0_ref[0, :, s] for s in cuts)
    _, total = lax.fori_loop(0, groups, backward, (start, zero))
    for j, s in enumerate(cuts):
        racc_ref[0, :, s] = total[j]


def gather_kernel(plan, *refs):
    n = 5
    srcs, dsts = refs[:n], refs[n:2*n]
    send, recv, local = refs[2*n:]
    d, f = lax.axis_index("dp"), lax.axis_index("fsdp")
    fx, fy, fd = f ^ 1, f ^ 2, f ^ 3
    sib = {"dp": 1 - d}
    tox, toy = {"fsdp": fx}, {"fsdp": fy}
    barrier = pltpu.get_barrier_semaphore()
    for who in (tox, toy, sib):
        pl.semaphore_signal(barrier, inc=1, device_id=who, device_id_type=MESH)
    pl.semaphore_wait(barrier, 3)

    def window(p, owner, half, q):
        k, dim, cols = plan[p]
        rows = srcs[k].shape[0]
        part = rows // 4
        at = (half * 2 + q) * part
        c = cols or (0, srcs[k].shape[1])
        if dim == 0:
            return dsts[k].at[pl.ds(pl.multiple_of(owner * rows + at, part), part), c[0]:c[1]]
        w = c[1] - c[0]
        return dsts[k].at[pl.ds(pl.multiple_of(at, part), part), pl.ds(pl.multiple_of(owner * w, w), w)]

    def own(p, half, q):
        k, dim, cols = plan[p]
        part = srcs[k].shape[0] // 4
        c = cols or (0, srcs[k].shape[1])
        return srcs[k].at[pl.ds(pl.multiple_of((half * 2 + q) * part, part), part), c[0]:c[1]]

    def copy(src, dst, p, kind, who):
        return pltpu.make_async_remote_copy(src_ref=src, dst_ref=dst, send_sem=send.at[p, kind], recv_sem=recv.at[p, kind], device_id=who, device_id_type=MESH)

    locals_ = []
    started = []
    for p in range(len(plan)):
        for q in (0, 1):
            a = copy(own(p, d, q), window(p, f, d, q), p, q, tox); a.start()
            b = copy(own(p, d, 1 - q), window(p, f, d, 1 - q), p, 3 - q, toy); b.start()
            started += [a, b]
    for p in range(len(plan)):
        for half in (0, 1):
            for q in (0, 1):
                c = pltpu.make_async_copy(own(p, half, q), window(p, f, half, q), local.at[p, half * 2 + q]); c.start(); locals_.append(c)
    def arrived(p, kind, owner, half, q):
        w = window(p, owner, half, q)
        copy(w, w, p, kind, sib).wait_recv()
        return w
    for p in range(len(plan)):
        for kind, owner, q in ((0, fx, 0), (3, fy, 1), (1, fx, 1), (2, fy, 0)):
            w = arrived(p, kind, owner, d, q)
            if kind == 0:
                c = copy(w, w, p, 4, toy); c.start(); started.append(c)
            if kind == 3:
                c = copy(w, w, p, 5, tox); c.start(); started.append(c)
            c = copy(w, w, p, 6 + kind, sib); c.start(); started.append(c)
    for p in range(len(plan)):
        for kind, q in ((4, 0), (5, 1)):
            w = arrived(p, kind, fd, d, q)
            c = copy(w, w, p, 6 + kind, sib); c.start(); started.append(c)
    for p in range(len(plan)):
        for kind, owner, q in ((0, fx, 0), (3, fy, 1), (1, fx, 1), (2, fy, 0), (4, fd, 0), (5, fd, 1)):
            arrived(p, 6 + kind, owner, 1 - d, q)
    for c in started: c.wait_send()
    for c in locals_: c.wait()

def gather(in_w, out_w, xp, dt, small):
    ops = (in_w, out_w, xp, dt, small)
    dims = (0, 0, 0, 1, 1)
    half = in_w.shape[1] // 2
    plan = ((0, 0, (0, half)), (2, 0, None), (3, 1, None), (4, 1, None), (0, 0, (half, 2 * half)), (1, 0, None))
    def full(v, dim):
        s = list(v.shape); s[dim] *= 4
        return jax.ShapeDtypeStruct(tuple(s), v.dtype)
    m = len(plan)
    return pl.pallas_call(functools.partial(gather_kernel, plan),
        in_specs=[pl.BlockSpec(memory_space=pltpu.VMEM)] * 5,
        out_specs=[pl.BlockSpec(memory_space=pl.ANY)] * 5,
        out_shape=[full(v, dm) for v, dm in zip(ops, dims)],
        scratch_shapes=[pltpu.SemaphoreType.DMA((m, 12)), pltpu.SemaphoreType.DMA((m, 12)), pltpu.SemaphoreType.DMA((m, 4))],
        compiler_params=pltpu.CompilerParams(collective_id=0, has_side_effects=True, vmem_limit_bytes=40<<20), name="gather")(*ops)


def reduce_kernel(span, made, sets, lhs, rhs, pre, out, g, ra, rx, ry, mine, zlo, zhi, zout, send, recv):
    d, s, f = (lax.axis_index(a) for a in ("dp", "seq", "fsdp"))
    fx, fy, fd = f ^ 1, f ^ 2, f ^ 3
    chunks = out.shape[0]
    q = HR // 2
    root = (span - 1) // 2
    tox, toy, sib = {"fsdp": fx}, {"fsdp": fy}, {"dp": 1 - d}
    up, down = {"seq": jnp.minimum(s + 1, span - 1)}, {"seq": jnp.maximum(s - 1, 0)}
    barrier = pltpu.get_barrier_semaphore()
    for who in (tox, toy, sib):
        pl.semaphore_signal(barrier, inc=1, device_id=who, device_id_type=MESH)
    @pl.when(s > 0)
    def _(): pl.semaphore_signal(barrier, inc=1, device_id=down, device_id_type=MESH)
    @pl.when(s < span - 1)
    def _(): pl.semaphore_signal(barrier, inc=1, device_id=up, device_id_type=MESH)
    ends = (s == 0) | (s == span - 1)
    pl.semaphore_wait(barrier, jnp.where(ends, 4, 5) if span > 1 else 3)

    def copy(kind, c, src, dst, who):
        return pltpu.make_async_remote_copy(src_ref=src, dst_ref=dst, send_sem=send.at[kind, c], recv_sem=recv.at[kind, c], device_id=who, device_id_type=MESH)
    lo, hi = slice(0, q), slice(q, HR)
    A = lambda c: copy(0, c, g.at[c, :, 1 - d], ra.at[c], sib)
    X = lambda c: (copy(1, c, ra.at[c, fd, lo], rx.at[c, 0], tox), copy(2, c, ra.at[c, fx, lo], rx.at[c, 1], tox))
    XV = lambda c: copy(3, c, ra.at[c, fx, hi], rx.at[c, 2], tox)
    Y = lambda c: (copy(4, c, ra.at[c, fd, hi], ry.at[c, 0], toy), copy(5, c, ra.at[c, fy, hi], ry.at[c, 2], toy))
    YV = lambda c: copy(6, c, ra.at[c, fy, lo], ry.at[c, 1], toy)
    ZU = lambda c: copy(7, c, zout.at[c], zlo.at[c], up)
    ZD = lambda c: copy(8, c, zout.at[c], zhi.at[c], down)
    TU = lambda c: copy(9, c, out.at[c, d], out.at[c, d], up)
    TD = lambda c: copy(10, c, out.at[c, d], out.at[c, d], down)
    D = lambda c: copy(11, c, out.at[c, d], out.at[c, d], sib)
    below, above = s < root, s > root
    spot = jnp.where(below, s, jnp.where(above, span - 1 - s, 0))
    far = jnp.abs(s - root)
    most = max(root, span - 1 - root)

    def stage(c, body):
        @pl.when((c >= 0) & (c < chunks))
        def _(): body(c)

    def produce(c):
        @pl.when(c < made)
        def _():
            for j in range(4):
                for h in range(2):
                    g[c, j, h] = pre[c, j, h]
        @pl.when(c >= made)
        def _():
            k = 0
            for first in sets[1:]:
                k = k + (c >= first).astype(jnp.int32)
            right = rhs[c - made]
            for j in range(4):
                t = jnp.dot(lhs[k, pl.ds(j * 2 * HR, 2 * HR)], right, preferred_element_type=F32).astype(BF16)
                g[c, j, 0] = t[:HR]
                g[c, j, 1] = t[HR:]
        A(c).start()

    def first_sum(c):
        A(c).wait_recv()
        for j in range(4):
            ra[c, j] = (ra[c, j].astype(F32) + g[c, j, d].astype(F32)).astype(BF16)
        for t in X(c) + Y(c):
            t.start()

    def second_sum(c):
        X(c)[0].wait_recv()
        ra[c, fy, lo] = (ra[c, fy, lo].astype(F32) + rx[c, 0].astype(F32)).astype(BF16)
        YV(c).start()
        Y(c)[0].wait_recv()
        ra[c, fx, hi] = (ra[c, fx, hi].astype(F32) + ry[c, 0].astype(F32)).astype(BF16)
        XV(c).start()

    def third_sum(c):
        X(c)[1].wait_recv(); Y(c)[1].wait_recv(); XV(c).wait_recv(); YV(c).wait_recv()
        for k, rows in enumerate((lo, hi)):
            mine[c, rows] = ra[c, f, rows].astype(F32) + rx[c, 1 + k].astype(F32) + ry[c, 1 + k].astype(F32)

    def inward(c):
        @pl.when(below & (s > 0))
        def _():
            ZU(c).wait_recv()
            zout[c] = (mine[c] + zlo[c].astype(F32)).astype(BF16)
        @pl.when(above & (s < span - 1))
        def _():
            ZD(c).wait_recv()
            zout[c] = (mine[c] + zhi[c].astype(F32)).astype(BF16)
        @pl.when((s != root) & ((s == 0) | (s == span - 1)))
        def _():
            zout[c] = mine[c].astype(BF16)
        pl.when(below)(lambda: ZU(c).start())
        pl.when(above)(lambda: ZD(c).start())

    def at_root(c):
        total = mine[c]
        if root > 0:
            ZU(c).wait_recv()
            total = total + zlo[c].astype(F32)
        if span - 1 > root:
            ZD(c).wait_recv()
            total = total + zhi[c].astype(F32)
        out[c, d] = total.astype(BF16)
        if root > 0: TD(c).start()
        if span - 1 > root: TU(c).start()
        D(c).start()

    def outward(c):
        @pl.when(above)
        def _():
            TU(c).wait_recv()
            pl.when(s < span - 1)(lambda: TU(c).start())
        @pl.when(below)
        def _():
            TD(c).wait_recv()
            pl.when(s > 0)(lambda: TD(c).start())
        D(c).start()

    base = 1 + 2 * SLACK + 1
    def step(i, carry):
        stage(i, produce)
        stage(i - 1, first_sum)
        stage(i - 1 - SLACK, second_sum)
        stage(i - 1 - 2 * SLACK, third_sum)
        pl.when(s != root)(lambda: stage(i - base - SLACK * spot, inward))
        pl.when(s == root)(lambda: stage(i - base - SLACK * most, at_root))
        pl.when(s != root)(lambda: stage(i - base - SLACK * most - SLACK * far, outward))
        return carry
    lax.fori_loop(0, chunks + base + 2 * SLACK * most + 1, step, 0)

    def finish(c, carry):
        D(c).wait_recv()
        A(c).wait_send()
        for t in X(c) + Y(c) + (XV(c), YV(c)): t.wait_send()
        pl.when(below)(lambda: ZU(c).wait_send())
        pl.when(above)(lambda: ZD(c).wait_send())
        if root > 0: pl.when((s <= root) & (s > 0))(lambda: TD(c).wait_send())
        if span - 1 > root: pl.when((s >= root) & (s < span - 1))(lambda: TU(c).wait_send())
        D(c).wait_send()
        return carry
    lax.fori_loop(0, chunks, finish, 0)

def reduce_grads(lhs, rhs, pre, sets):
    made, nb, cw = pre.shape[0], rhs.shape[0], rhs.shape[2]
    n = made + nb
    span = lax.axis_size("seq")
    v = pltpu.VMEM
    return pl.pallas_call(functools.partial(reduce_kernel, span, made, sets),
        in_specs=[pl.BlockSpec(memory_space=v)] * 3, out_specs=pl.BlockSpec(memory_space=v),
        out_shape=jax.ShapeDtypeStruct((n, 2, HR, cw), BF16),
        scratch_shapes=[v((n, 4, 2, HR, cw), BF16), v((n, 4, HR, cw), BF16), v((n, 3, HR // 2, cw), BF16), v((n, 3, HR // 2, cw), BF16), v((n, HR, cw), F32), v((n, HR, cw), BF16), v((n, HR, cw), BF16), v((n, HR, cw), BF16),
            pltpu.SemaphoreType.DMA((12, n)), pltpu.SemaphoreType.DMA((12, n))],
        compiler_params=pltpu.CompilerParams(collective_id=1, has_side_effects=True, vmem_limit_bytes=60 << 20), name="reduce")(lhs, rhs, pre)


def block_diagonal(v):
    seqs, ctx, state = v.shape
    eye = jnp.eye(GROUP, dtype=F32)[None, None, :, :, None]
    spread = v.reshape(seqs, ctx // GROUP, GROUP, 1, state) * eye
    return spread.reshape(seqs, ctx // GROUP, GROUP, GROUP * state).astype(BF16)


def diagonal_blocks(v):
    seqs, groups, _, wide = v.shape
    state = wide // GROUP
    eye = jnp.eye(GROUP, dtype=F32)[None, None, :, :, None]
    picked = jnp.sum(v.reshape(seqs, groups, GROUP, GROUP, state) * eye, 3)
    return picked.reshape(seqs * groups * GROUP, state)


def local_specs(seqs, ctx, inner, state, width):
    groups = ctx // GROUP
    tok = pl.BlockSpec((1, groups, GROUP, width), lambda c, j: (c, 0, 0, j))
    wide = pl.BlockSpec((1, ctx, state, LANES), lambda c, j: (c, 0, 0, 0))
    rate = pl.BlockSpec((state, width), lambda c, j: (0, j))
    end = pl.BlockSpec((1, state, width), lambda c, j: (c, 0, j))
    diag = pl.BlockSpec((1, groups, GROUP, GROUP * state), lambda c, j: (c, 0, 0, 0))
    return tok, wide, rate, end, diag


def local_ends(delta, drive, dy, b_wide, c_wide, rates):
    seqs, groups, _, inner = delta.shape
    state = rates.shape[0]
    width = 512
    tok, wide, rate, end, _ = local_specs(seqs, groups * GROUP, inner, state, width)
    return pl.pallas_call(
        ends_kernel,
        grid=(seqs, inner // width),
        in_specs=[tok, tok, tok, wide, wide, rate],
        out_specs=[end, end],
        out_shape=[jax.ShapeDtypeStruct((seqs, state, inner), F32)] * 2,
        compiler_params=pltpu.CompilerParams(vmem_limit_bytes=56 << 20),
        name="ends",
    )(delta, drive, dy, b_wide, c_wide, rates)


def sweep(delta, drive, dy, b_in, c_in, b_wide, c_wide, rates, start, final):
    seqs, groups, _, inner = delta.shape
    ctx = groups * GROUP
    state = rates.shape[0]
    width = 512
    tok, wide, rate, end, diag = local_specs(seqs, ctx, inner, state, width)
    ones = block_diagonal(jnp.ones((1, GROUP, state), F32))[0, 0]
    token_shape = jax.ShapeDtypeStruct(delta.shape, F32)
    diag_shape = jax.ShapeDtypeStruct((seqs, groups, GROUP, GROUP * state), F32)
    return pl.pallas_call(
        sweep_kernel,
        grid=(seqs, inner // width),
        in_specs=[tok, tok, tok, wide, wide, rate, end, end, diag, diag]
        + [pl.BlockSpec(ones.shape, lambda c, j: (0, 0))],
        out_specs=[tok, tok, tok, diag, diag, end],
        out_shape=[token_shape] * 3
        + [diag_shape] * 2
        + [jax.ShapeDtypeStruct((seqs, state, inner), F32)],
        scratch_shapes=[
            pltpu.VMEM((ctx + 1, state, width), F32),
            pltpu.VMEM((ctx, state, width), F32),
            pltpu.VMEM((GROUP, state, width), BF16),
            pltpu.VMEM((GROUP, state, width), BF16),
        ],
        compiler_params=pltpu.CompilerParams(vmem_limit_bytes=56 << 20),
        name="sweep",
    )(
        delta, drive, dy, b_wide, c_wide, rates, start, final,
        block_diagonal(c_in), block_diagonal(b_in), ones,
    )


def body(
    hidden_in, lengths, norm_gain, in_weight, conv_weight, conv_bias, xproj_weight,
    dt_weight, dt_bias, a_log, skip_gain, out_weight, out_grad,
):
    seqs, ctx, width = hidden_in.shape
    taps, share = conv_weight.shape
    state = a_log.shape[0]
    rank = dt_weight.shape[0]
    reach = taps - 1
    rows = ctx * seqs
    groups = ctx // GROUP
    small = jnp.concatenate(
        [conv_weight, a_log, conv_bias[None], dt_bias[None], skip_gain[None]]
        + [jnp.pad(norm_gain, (0, share - norm_gain.shape[0]))[None]],
        0,
    )
    used = small.shape[0]
    small = jnp.pad(small, ((0, -used % 32), (0, 0)))
    in_matrix, out_matrix, proj_matrix, step_matrix, small = gather(
        in_weight, out_weight, xproj_weight, dt_weight, small
    )
    gain = small[used - 1].reshape(-1, share)[:, : norm_gain.shape[0]].reshape(-1)
    conv_taps, log_rate = small[:taps], small[taps : taps + state]
    conv_shift, step_bias, skip = (small[taps + state + i] for i in range(3))
    inner = proj_matrix.shape[0]
    dot = lambda a, b: jnp.dot(a, b, preferred_element_type=F32)

    x_tok = hidden_in.astype(F32)
    position = lax.axis_index("seq") * ctx + jnp.arange(ctx, dtype=jnp.int32)
    mask = (position[None, :] < lengths[:, None]).astype(F32)[:, :, None]

    def normalised(x):
        inverse = lax.rsqrt(jnp.mean(x * x, -1, keepdims=True) + EPS)
        return inverse, (x * inverse * gain).astype(BF16)

    inverse, normed = normalised(x_tok)
    normed = normed.reshape(rows, width)
    mixed = dot(normed, in_matrix).astype(BF16)
    stream = mixed[:, :inner].reshape(seqs, ctx, inner)
    gate_in = mixed[:, inner:].astype(F32).reshape(seqs, ctx, inner)
    before = passed_along(stream[:, ctx - reach :], "seq", 1)
    extended = jnp.concatenate([before, stream], 1).astype(F32)
    conv_out = conv_shift + sum(conv_taps[k] * extended[:, k : k + ctx] for k in range(taps))
    u_low = jax.nn.silu(conv_out).astype(BF16)
    u_rows = u_low.reshape(rows, inner)
    proj = dot(u_rows, proj_matrix)
    step_low = proj[:, :rank].astype(BF16)
    b_in = proj[:, rank : rank + state].reshape(seqs, ctx, state)
    c_in = proj[:, rank + state :].reshape(seqs, ctx, state)
    raw = dot(step_low, step_matrix).reshape(seqs, ctx, inner) + step_bias
    delta = jax.nn.softplus(raw)
    rates = -jnp.exp(log_rate)
    rates2 = rates * LOG2E
    u_float = u_low.astype(F32)
    drive = delta * u_float

    cotangent = out_grad.astype(F32)
    branch_grad = (cotangent * mask).astype(BF16).reshape(rows, width)
    gated_grad = lax.dot_general(
        branch_grad, out_matrix, (((1,), (1,)), ((), ())), preferred_element_type=F32
    ).reshape(seqs, ctx, inner)
    gate_act = jax.nn.silu(gate_in)
    y_grad = gated_grad * gate_act

    grouped = lambda v: v.reshape(seqs, groups, GROUP, inner)
    b_wide = jnp.broadcast_to(b_in[..., None], (seqs, ctx, state, LANES))
    c_wide = jnp.broadcast_to(c_in[..., None], (seqs, ctx, state, LANES))
    scan_args = (grouped(delta), grouped(drive), grouped(y_grad))
    local_end, local_back = local_ends(*scan_args, b_wide, c_wide, rates2)

    blocks = lax.axis_size("seq")
    me = lax.axis_index("seq")
    ends = lax.all_gather(jnp.stack([local_end, local_back]).astype(BF16), "seq")
    sums = lax.all_gather(jnp.sum(delta, 1), "seq")
    start = jnp.zeros((seqs, state, inner), F32)
    final = jnp.zeros((seqs, state, inner), F32)
    for k in range(blocks):
        decay = jnp.exp2(sums[k][:, None, :] * rates2)
        start = jnp.where(k < me, decay * start + ends[k, 0].astype(F32), start)
        r = blocks - 1 - k
        decay = jnp.exp2(sums[r][:, None, :] * rates2)
        final = jnp.where(r > me, decay * final + ends[r, 1].astype(F32), final)

    y, drive_grad, delta_part, c_acc, b_acc, rate_grad = sweep(
        *scan_args, b_in, c_in, b_wide, c_wide, rates2, start, final
    )
    ungrouped = lambda v: v.reshape(seqs, ctx, inner)
    y_val = ungrouped(y) + skip * u_float
    drive_grad = ungrouped(drive_grad)
    c_grad, b_grad = diagonal_blocks(c_acc), diagonal_blocks(b_acc)
    log_grad = jnp.sum(rate_grad, 0) * rates

    gated = (y_val * gate_act).astype(BF16).reshape(rows, inner)
    branch = dot(gated, out_matrix).reshape(seqs, ctx, width)
    hidden_out = (x_tok + mask * branch).astype(BF16)
    contract = lambda a, b: lax.dot_general(
        a, b, (((0,), (0,)), ((), ())), preferred_element_type=F32
    )
    out_w_grad = contract(gated, branch_grad)
    z_grad = gated_grad * y_val * silu_grad(gate_in)
    skip_grad = jnp.sum(y_grad * u_float, (0, 1))
    delta_grad = drive_grad * u_float + ungrouped(delta_part) * (1.0 / LOG2E)
    u_grad = y_grad * skip + drive_grad * delta
    raw_grad = delta_grad * jax.nn.sigmoid(raw)
    bias_grad = jnp.sum(raw_grad, (0, 1))
    raw_low = raw_grad.astype(BF16).reshape(rows, inner)
    step_w_grad = contract(step_low, raw_low)
    step_grad = lax.dot_general(
        raw_low, step_matrix, (((1,), (1,)), ((), ())), preferred_element_type=F32
    )
    proj_grad = jnp.concatenate([step_grad, b_grad, c_grad], 1).astype(BF16)
    proj_w_grad = contract(proj_grad, u_rows)
    u_grad = u_grad + lax.dot_general(
        proj_grad, proj_matrix, (((1,), (1,)), ((), ())), preferred_element_type=F32
    ).reshape(seqs, ctx, inner)
    conv_grad = u_grad * silu_grad(conv_out)
    shift_grad = jnp.sum(conv_grad, (0, 1))
    taps_grad = jnp.stack(
        [jnp.sum(conv_grad * extended[:, k : k + ctx], (0, 1)) for k in range(taps)], 0
    )
    after = passed_along(conv_grad[:, :reach], "seq", -1)
    later = jnp.concatenate([conv_grad, after], 1)
    stream_grad = sum(conv_taps[k] * later[:, reach - k : reach - k + ctx] for k in range(taps))
    mixed_grad = jnp.concatenate(
        [stream_grad.reshape(rows, inner), z_grad.reshape(rows, inner)], 1
    ).astype(BF16)
    in_w_grad = contract(normed, mixed_grad)
    normed_grad = lax.dot_general(
        mixed_grad, in_matrix, (((1,), (1,)), ((), ())), preferred_element_type=F32
    ).reshape(seqs, ctx, width)
    gain_grad = jnp.sum(normed_grad * x_tok * inverse, (0, 1))
    scaled = normed_grad * gain
    x_grad = (
        inverse * scaled
        - x_tok * inverse * inverse * inverse * jnp.mean(scaled * x_tok, -1, keepdims=True)
        + cotangent
    )
    input_grad = x_grad.astype(BF16)

    shards = lax.axis_size("fsdp")
    gain_rows = jnp.pad(gain_grad.reshape(shards, -1), ((0, 0), (0, share - width // shards)))
    rest = jnp.concatenate(
        [taps_grad, log_grad, shift_grad[None], bias_grad[None], skip_grad[None]]
        + [gain_rows.reshape(1, inner), step_w_grad, proj_w_grad],
        0,
    )
    rest = jnp.pad(rest, ((0, 2 * HR - rest.shape[0]), (0, 0))).astype(BF16)
    pre = rest.reshape(2, HR, shards, share // CHUNK, CHUNK).transpose(3, 2, 0, 1, 4)
    tall = gated.T.reshape(shards, 2, 2, HR, rows).transpose(2, 0, 1, 3, 4)
    lhs = jnp.concatenate([tall.reshape(2, -1, rows), normed.T[None]], 0)
    right = branch_grad.reshape(rows, -1, CHUNK).transpose(1, 0, 2)
    mixed_right = mixed_grad.reshape(rows, -1, CHUNK).transpose(1, 0, 2)
    made, part = pre.shape[0], right.shape[0]
    sums = reduce_grads(
        lhs, jnp.concatenate([right, right, mixed_right], 0), pre, (made, made + part, made + 2 * part)
    ).astype(F32)
    rest = sums[:made].transpose(1, 2, 0, 3).reshape(2 * HR, share)
    out_w = sums[made : made + 2 * part].reshape(2, part, 2, HR, CHUNK).transpose(2, 0, 3, 1, 4)
    out_w = out_w.reshape(-1, width)
    in_w = sums[made + 2 * part :].transpose(1, 2, 0, 3).reshape(2 * HR, 2 * inner)
    at = taps + state
    return (
        hidden_out, input_grad, rest[at + 3, : width // shards], in_w, rest[:taps], rest[at],
        rest[at + 4 + rank : at + 4 + rank + proj_matrix.shape[1]].T, rest[at + 4 : at + 4 + rank],
        rest[at + 1], rest[taps:at], rest[at + 2], out_w,
    )


def solution(mesh):
    tokens = P(("dp", "fsdp"), "seq", None)
    return jax.shard_map(
        body,
        mesh=mesh,
        in_specs=(
            tokens, P(("dp", "fsdp")), P("fsdp"), P("fsdp", None), P(None, "fsdp"), P("fsdp"),
            P("fsdp", None), P(None, "fsdp"), P("fsdp"), P(None, "fsdp"), P("fsdp"),
            P("fsdp", None), tokens,
        ),
        out_specs=(
            tokens, tokens, P("fsdp"), P("fsdp", None), P(None, "fsdp"), P("fsdp"),
            P("fsdp", None), P(None, "fsdp"), P("fsdp"), P(None, "fsdp"), P("fsdp"),
            P("fsdp", None),
        ),
        check_vma=False,
    )
```

time: 5860 us -> 398 us (0.07); the launches traced: 5790 us -> 394 us
  local copies, waits for them, and re-layouts: 3270 us -> 73.6 us
  other arithmetic: 1810 us -> 42.5 us
  waiting for transfers between devices: 511 us -> 0.73 us
  Pallas kernels: 0 us -> 219 us
  blocking collectives: 101 us -> 11.1 us
    pad x288 -> x3, local copies, waits for them, and re-layouts: 2510 us -> 1.77 us  [the longest x1 1.08 us: body(): rest = jnp.pad(rest, ((0, 2 * HR - rest.shape[0]), (0, 0))).astype(BF16)]
    add x195 -> x0, other arithmetic: 707 us -> none  [the longest x168 591 us: linear_prefix(): return lax.associative_scan(join_carry, (decays, inputs), axis=0)]
    mul x158 -> x2, other arithmetic: 661 us -> 2.61 us  [the longest x1 1.93 us: body(): delta_grad = drive_grad * u_float + ungrouped(delta_part) * (1.0 / LOG2E)]
    while x610 -> x0, local copies, waits for them, and re-layouts: 431 us -> none
    reduce_scatter x5 -> x0, waiting for transfers between devices: 286 us -> none  [the longest x1 157 us: body(): lax.psum_scatter(in_w_grad, 'fsdp', scatter_dimension=0, tiled=True)]
    pallas_call x0 -> x4, Pallas kernels: none -> 219 us  [the longest x1 94.6 us: reduce_grads(): pl.pallas_call(functools.partial(reduce_kernel, span, made, sets), in_spe...]
    concatenate x144 -> x2, other arithmetic: 209 us -> 3.26 us  [the longest x1 1.94 us: body(): jnp.concatenate([right, right, mixed_right], 0)]
    slice x151 -> x13, local copies, waits for them, and re-layouts: 192 us -> 4.33 us  [the longest x1 0.66 us: body(): rest[at + 4:at + 4 + rank]]
  transfers between devices with their start and end apart: 17 -> 3, of which waited for: 14 -> 1; matrix products, arithmetic and copies ran while one was open for 1% -> 8% of each run, Pallas kernels for 0% -> 0%
where the time goes in v1:
time: 398 us; the launch traced here: 394 us
  Pallas kernels  219 us (55%)
  local copies, waits for them, and re-layouts  73.6 us (18%)
  other arithmetic  42.5 us (11%)
  matrix products  27.5 us (7%)
  between operations  15.2 us (4%)
  blocking collectives  11.1 us (3%)
  starting transfers between devices  4.11 us (1%)
    pallas_call x1, Pallas kernels, reduce_grads(): pl.pallas_call(functools.partial(reduce_kernel, span, made, sets), in_spe...  94.6 us
    pallas_call x1, Pallas kernels, gather(): pl.pallas_call(functools.partial(gather_kernel, plan), in_specs=[pl.Block...  61.9 us
    pallas_call x1, Pallas kernels, sweep(): pl.pallas_call(sweep_kernel, grid=(seqs, inner // width), in_specs=[tok,...  49 us
    unnamed x119, local copies, waits for them, and re-layouts  20.8 us
    pallas_call x1, Pallas kernels, local_ends(): pl.pallas_call(ends_kernel, grid=(seqs, inner // width), in_specs=[tok, t...  13.9 us
    dot_general x4, matrix products, body(): dot = lambda a, b: jnp.dot(a, b, preferred_element_type=F32)  11.3 us
    all_gather x1, blocking collectives, body(): sums = lax.all_gather(jnp.sum(delta, 1), 'seq')  11.1 us
    mul x6, local copies, waits for them, and re-layouts, block_diagonal(): spread = v.reshape(seqs, ctx // GROUP, GROUP, 1, state) * eye  9.47 us
  transfers between devices with their start and end apart: 3, of which 1 were waited for; matrix products, arithmetic and copies ran while one was open for 8% of the time, Pallas kernels for 0%

profile of v1, /device:TPU:25, one launch (start us, length us, event | category | flops | bytes accessed | tf_op | source)
XLA Modules:
  0.0 394.1 jit_solution(18358437895689375886)
XLA Ops:
  8.9 2.3 concatenate.43
  11.2 1.6 copy-done
  14.9 61.9 %gather.1 = (bf16[1024,4096]{1,0:T(8,128)(2,1)}, bf16[2048,1024]{1,0:T(8,128)(2,1)S(1)}, bf16[2048,96]{1,0:T(8,128)(2,1)S(1)}, bf16[64,2048]{1,0:T(8,128)(2,1)S(1)}, f32[32,2048]{1,0:T(8,128)S(1)}) custom-call(bf16[256,4096]{1,0:T(8,128)(2,1)S(1)} %copy-done, bf16[512,1024]{1,0:T(8,128)(2,1)S(1)} %copy-done.1, bf16[512,96]{1,0:T(8,128)(2,1)S(1)} %copy.46.refs_2_, ...), custom_call_target="tpu_custom_call" | custom-call | tf_op jit(solution)/shard_map/gather/pallas_call | solution.py:205
  76.8 2.0 copy-done.3
  79.6 5.7 %convolution_convert_fusion = bf16[256,4096]{1,0:T(8,128)(2,1)S(1)} fusion(bf16[256,1024]{1,0:T(8,128)(2,1)S(1)} %bitcast.212, bf16[1024,4096]{1,0:T(8,128)(2,1)} %get-tuple-element.26), kind=kOutput, calls=%fused_computation.2 | convolution fusion | flops 2148532224 | bytes 11010048 | tf_op jit(solution)/shard_map/dot_general | solution.py:465
  85.6 1.8 collective-permute-start
  88.2 1.3 fusion.45
  90.7 5.4 %fusion.22 = (bf16[2048]{0:T(1024)(128)(2,1)}, f32[2,128,2048]{2,1,0:T(8,128)}, bf16[2,128,2048]{2,1,0:T(8,128)(2,1)S(1)}, f32[2,128,2048]{2,1,0:T(8,128)}, f32[2,128,2048]{2,1,0:T(8,128)}) fusion(bf16[2,128,2048]{2,1,0:T(8,128)(2,1)S(1)} %bitcast.210, f32[2,131,2048]{2,1,0:T(8,128)S(1)} %maximum_convert_fusion, f32[2048]{0:T(1024)S(1)} %bitcast.239, ...), kind=kOutput, calls=%fused_computation.40 | convolution fusion | flops 1085274112 | bytes 21540864 | tf_op jit(solution)/shard_map/dot_general | solution.py:498
  99.0 3.3 fusion.67
  102.3 2.5 compare_select_fusion.1.d_ref
  104.8 1.9 broadcast_in_dim.64.b_ref
  106.7 2.0 broadcast_in_dim.66.c_ref
  108.7 13.9 %ends.1 = (f32[2,16,2048]{2,1,0:T(8,128)}, f32[2,16,2048]{2,1,0:T(8,128)}) custom-call(f32[2,8,16,2048]{3,2,1,0:T(8,128)} %compare_select_fusion.1.d_ref, f32[2,8,16,2048]{3,2,1,0:T(8,128)} %bitcast.192, f32[2,8,16,2048]{3,2,1,0:T(8,128)} %bitcast.190, f32[2,128,16,128]{3,2,1,0:T(8,128)} %broadcast_in_dim.64.b_ref, ...), custom_call_target="tpu_custom_call" | custom-call | tf_op jit(solution)/shard_map/ends/pallas_call | solution.py:397
  124.4 2.2 reshape_reshape.2
  126.7 2.0 copy.62
  131.4 1.9 copy.76
  133.3 1.6 mul.467
  134.9 2.5 mul.468
  137.3 1.6 mul.474
  138.9 3.1 mul.475
  143.3 11.1 %all-gather.1 = f32[4,2,2048]{2,1,0:T(2,128)S(1)} all-gather(f32[1,2,2048]{2,1,0:T(2,128)} %bitcast.238), channel_id=2, replica_groups=mesh['dp'=2,'seq'=4,'fsdp'=4] {'seq'}, dimensions={0}, use_global_device_ids=true | all-gather | bytes 81920 | tf_op jit(solution)/shard_map/all_gather | solution.py:513
  154.3 1.7 multiply_convert_fusion.2
  156.1 2.1 fusion.52.p0_ref
  158.2 2.1 fusion.56.h0_ref
  160.3 49.0 %sweep.1 = (f32[2,8,16,2048]{3,2,1,0:T(8,128)}, f32[2,8,16,2048]{3,2,1,0:T(8,128)}, f32[2,8,16,2048]{3,2,1,0:T(8,128)}, f32[2,8,16,256]{3,2,1,0:T(8,128)}, f32[2...) custom-call(f32[2,8,16,2048]{3,2,1,0:T(8,128)} %compare_select_fusion.1.d_ref, f32[2,8,16,2048]{3,2,1,0:T(8,128)} %bitcast.193, ...), custom_call_target="tpu_custom_call" | custom-call | tf_op jit(solution)/shard_map/sweep/pallas_call | solution.py:417
  209.3 1.9 broadcast_multiply_fusion
  212.1 4.9 %fusion.69 = (bf16[2048]{0:T(1024)(128)(2,1)}, bf16[2,128,2048]{2,1,0:T(8,128)(2,1)S(1)}, bf16[2,128,2048]{2,1,0:T(8,128)(2,1)}, bf16[2,128,2048]{2,1,0:T(8,128)(2,1)}) fusion(f32[2048]{0:T(1024)S(1)} %bitcast.231, f32[2,8,16,2048]{3,2,1,0:T(8,128)S(1)} %broadcast_multiply_fusion, bf16[2,128,2048]{2,1,0:T(8,128)(2,1)S(1)} %copy-done.10, ...), kind=kLoop, calls=%fused_computation.148 | loop fusion | flops 13629440 | bytes 15749120 | tf_op jit(solution)/shard_map/reduce_sum | solution.py:544
  218.4 2.0 reshape.273
  220.4 2.0 reshape.275
  222.4 3.3 multiply_reduce_fusion.5
  225.8 2.5 convolution_convert_fusion.1
  228.8 5.7 %multiply_reduce_fusion = (bf16[2048]{0:T(1024)(128)(2,1)}, bf16[2048]{0:T(1024)(128)(2,1)}, bf16[2048]{0:T(1024)(128)(2,1)S(1)}, bf16[2048]{0:T(1024)(128)(2,1)...) fusion(f32[2,131,2048]{2,1,0:T(8,128)S(1)} %copy-done.6, f32[2,128,2048]{2,1,0:T(8,128)} %get-tuple-element.50, ...), kind=kLoop, calls=%fused_computation.52 | loop fusion | flops 14669824 | bytes 21008384 | tf_op jit(solution)/shard_map/reduce_sum | solution.py:558
  236.5 2.3 collective-permute-start.1
  238.8 4.6 %fusion.36 = bf16[2,128,1024]{2,1,0:T(8,128)(2,1)} fusion(bf16[2,128,2048]{2,1,0:T(8,128)(2,1)} %get-tuple-element.58, bf16[2048,1024]{1,0:T(8,128)(2,1)} %copy-done.3, bf16[2,128,1024]{2,1,0:T(8,128)(2,1)S(1)} %copy-done.15, f32[2,128]{1,0:T(2,128)S(1)} %copy-done.54), kind=kOutput, calls=%fused_computation.71 | convolution fusion | flops 1074790400 | bytes 6292480 | tf_op jit(solution)/shard_map/dot_general | solution.py:465
  244.5 1.3 pad_maximum_fusion.2.lhs
  246.0 1.6 concatenate.50
  247.6 2.4 copy.58
  252.0 6.4 %fusion.24 = f32[256,1024]{1,0:T(8,128)S(1)} fusion(bf16[1024,4096]{1,0:T(8,128)(2,1)} %get-tuple-element.26, bf16[256,2048]{1,0:T(8,128)(2,1)} %bitcast.204, bf16[256,2048]{1,0:T(8,128)(2,1)} %bitcast.207), kind=kOutput, calls=%fused_computation.43 | convolution fusion | flops 2151677952 | bytes 11534336 | tf_op jit(solution)/shard_map/dot_general | solution.py:567
  259.1 3.1 concatenate.53
  263.4 2.6 reshape.286
  266.0 2.5 copy.75
  269.7 1.9 pad_maximum_fusion.rhs
  271.7 94.6 %reduce.5 = bf16[13,2,128,512]{3,2,1,0:T(8,128)(2,1)} custom-call(bf16[3,1024,256]{2,1,0:T(8,128)(2,1)} %pad_maximum_fusion.2.lhs, bf16[12,256,512]{2,1,0:T(8,128)(2,1)} %pad_maximum_fusion.rhs, bf16[1,4,2,128,512]{4,3,2,1,0:T(8,128)(2,1)} %bitcast.206), custom_call_target="tpu_custom_call" | custom-call | tf_op jit(solution)/shard_map/reduce/pallas_call | solution.py:359
  366.3 3.1 convert_element_type.178
  374.1 2.4 copy.60
  376.5 5.8 %copy.71 = f32[32,8,8,512]{3,1,2,0:T(8,128)} copy(f32[32,8,8,512]{3,2,1,0:T(8,128)S(1)} %bitcast.196) | data formatting | bytes 8388608
  382.3 1.6 copy.61
  383.9 1.8 copy.72
  (180 shorter events, 32.0 us)
Async XLA Ops:
  7.2 148.9 %all-gather.4.cloned.1.call-start = ((), (), s32[]{:S(2)}) async-start(), calls=%async_computation | async-start | bytes 1310720 | tf_op jit(solution)/shard_map/all_gather | solution.py:512
  11.2 1.6 copy-start
  14.9 64.1 %copy-start.14 = (bf16[2,128,1024]{2,1,0:T(8,128)(2,1)S(1)}, bf16[2,128,1024]{2,1,0:T(8,128)(2,1)}, u32[]{:S(2)}) copy-start(bf16[2,128,1024]{2,1,0:T(8,128)(2,1)} %param.13) | copy-start | bytes 1572868
  76.8 2.0 copy-start.3
  78.9 11.7 %copy-start.39 = (f32[1,2048]{1,0:T(1,128)}, f32[1,2048]{1,0:T(1,128)S(1)}, u32[]{:S(2)}) copy-start(f32[1,2048]{1,0:T(1,128)S(1)} %get-tuple-element.65) | copy-start | bytes 24580
  78.9 11.7 %copy-start.41 = (f32[1,2048]{1,0:T(1,128)}, f32[1,2048]{1,0:T(1,128)S(1)}, u32[]{:S(2)}) copy-start(f32[1,2048]{1,0:T(1,128)S(1)} %get-tuple-element.66) | copy-start | bytes 24580
  78.9 11.7 %copy-start.43 = (f32[1,2048]{1,0:T(1,128)}, f32[1,2048]{1,0:T(1,128)S(1)}, u32[]{:S(2)}) copy-start(f32[1,2048]{1,0:T(1,128)S(1)} %get-tuple-element.67) | copy-start | bytes 24580
  78.9 11.7 %copy-start.45 = (f32[1,2048]{1,0:T(1,128)}, f32[1,2048]{1,0:T(1,128)S(1)}, u32[]{:S(2)}) copy-start(f32[1,2048]{1,0:T(1,128)S(1)} %get-tuple-element.69) | copy-start | bytes 24580
  79.2 6.1 %copy-start.48 = (f32[2,128]{1,0:T(2,128)}, f32[2,128]{1,0:T(2,128)S(1)}, u32[]{:S(2)}) copy-start(f32[2,128]{1,0:T(2,128)S(1)} %add_rsqrt_fusion) | copy-start | bytes 3076
  79.4 5.9 %copy-start.25 = (bf16[2,128,1024]{2,1,0:T(8,128)(2,1)}, bf16[2,128,1024]{2,1,0:T(8,128)(2,1)S(1)}, u32[]{:S(2)}) copy-start(bf16[2,128,1024]{2,1,0:T(8,128)(2,1)S(1)} %fusion.41) | copy-start | bytes 1572868
  85.3 2.8 copy-start.55
  85.6 5.1 %copy-start.20 = (bf16[256,2048]{1,0:T(8,128)(2,1)}, bf16[256,2048]{1,0:T(8,128)(2,1)S(1)}, u32[]{:S(2)}) copy-start(bf16[256,2048]{1,0:T(8,128)(2,1)S(1)} %get-tuple-element.57) | copy-start | bytes 3145732
  85.6 4.7 %collective-permute-start = (bf16[2,3,2048]{2,1,0:T(4,128)(2,1)S(1)}, bf16[2,3,2048]{2,1,0:T(4,128)(2,1)S(1)}, u32[]{:S(2)}, u32[]{:S(2)}) collective-permute-start(bf16[2,3,2048]{2,1,0:T(4,128)(2,1)S(1)} %slice.216), channel_id=1, source_target_pairs={{0,4},{4,8},{8,12},{1,5},{5,9},{9,13},{2,6},{6,10},{10,14},{3,7},{... | collective-permute-start | bytes 73736 | tf_op jit(solution)/shard_map/ppermute | solution.py:27
  88.2 2.4 copy-start.53
  88.2 2.5 copy-start.4
  89.6 6.6 %copy-start.26 = (bf16[2,128,1024]{2,1,0:T(8,128)(2,1)}, bf16[2,128,1024]{2,1,0:T(8,128)(2,1)S(1)}, u32[]{:S(2)}) copy-start(bf16[2,128,1024]{2,1,0:T(8,128)(2,1)S(1)} %fusion.45) | copy-start | bytes 1572868
  90.6 5.5 %copy-start.5 = (f32[2,131,2048]{2,1,0:T(8,128)}, f32[2,131,2048]{2,1,0:T(8,128)S(1)}, u32[]{:S(2)}) copy-start(f32[2,131,2048]{2,1,0:T(8,128)S(1)} %maximum_convert_fusion) | copy-start | bytes 6438916
  97.5 4.8 %copy-start.30 = (f32[256,96]{0,1:T(8,128)}, f32[256,96]{0,1:T(8,128)S(1)}, u32[]{:S(2)}) copy-start(f32[256,96]{0,1:T(8,128)S(1)} %fusion.76) | copy-start | bytes 294916
  138.9 17.2 %copy-start.23 = (f32[16,2048]{1,0:T(8,128)S(1)}, f32[16,2048]{1,0:T(8,128)}, u32[]{:S(2)}) copy-start(f32[16,2048]{1,0:T(8,128)} %fusion.60.a_ref) | copy-start | bytes 393220
  160.2 51.0 %copy-start.24 = (f32[2,128,2048]{2,1,0:T(8,128)S(1)}, f32[2,128,2048]{2,1,0:T(8,128)}, u32[]{:S(2)}) copy-start(f32[2,128,2048]{2,1,0:T(8,128)} %get-tuple-element.81) | copy-start | bytes 6291460
  209.2 2.0 copy-start.10
  209.3 2.5 copy-start.13
  209.3 2.8 copy-start.21
  212.1 5.3 %copy-start.31 = (f32[256,96]{0,1:T(8,128)S(1)}, f32[256,96]{0,1:T(8,128)}, u32[]{:S(2)}) copy-start(f32[256,96]{0,1:T(8,128)} %copy-done.30) | copy-start | bytes 294916
  216.9 1.5 copy-start.33
  217.4 3.0 copy-start.32
  218.4 4.0 %copy-start.36 = (f32[16,16]{1,0:T(8,128)S(1)}, f32[16,16]{1,0:T(8,128)}, u32[]{:S(2)}) copy-start(f32[16,16]{1,0:T(8,128)} %copy-done.35) | copy-start | bytes 3076
  225.8 2.9 copy-start.6
  228.8 10.0 %copy-start.34 = (f32[2,16,2048]{2,1,0:T(8,128)S(1)}, f32[2,16,2048]{2,1,0:T(8,128)}, u32[]{:S(2)}) copy-start(f32[2,16,2048]{2,1,0:T(8,128)} %get-tuple-element.37) | copy-start | bytes 786436
  228.8 10.0 %copy-start.15 = (bf16[2,128,1024]{2,1,0:T(8,128)(2,1)S(1)}, bf16[2,128,1024]{2,1,0:T(8,128)(2,1)}, u32[]{:S(2)}) copy-start(bf16[2,128,1024]{2,1,0:T(8,128)(2,1)} %param.13) | copy-start | bytes 1572868
  228.8 10.0 %copy-start.54 = (f32[2,128]{1,0:T(2,128)S(1)}, f32[2,128]{1,0:T(2,128)}, u32[]{:S(2)}) copy-start(f32[2,128]{1,0:T(2,128)} %copy-done.53) | copy-start | bytes 3076
  236.5 13.5 %collective-permute-start.1 = (f32[2,3,2048]{2,1,0:T(4,128)}, f32[2,3,2048]{2,1,0:T(4,128)S(1)}, u32[]{:S(2)}, u32[]{:S(2)}) collective-permute-start(f32[2,3,2048]{2,1,0:T(4,128)} %slice.237), channel_id=1, source_target_pairs={{4,0},{8,4},{12,8},{5,1},{9,5},{13,9},{6,2},{10,6},{14,10},{7,3},{... | collective-permute-start | bytes 147464 | tf_op jit(solution)/shard_map/ppermute | solution.py:27
  238.8 4.7 %copy-start.18 = (bf16[2,128,2048]{2,1,0:T(8,128)(2,1)S(1)}, bf16[2,128,2048]{2,1,0:T(8,128)(2,1)}, u32[]{:S(2)}) copy-start(bf16[2,128,2048]{2,1,0:T(8,128)(2,1)} %get-tuple-element.58) | copy-start | bytes 3145732
  244.1 1.8 copy-start.52
  244.1 1.8 copy-start.51
  244.1 1.8 copy-start.50
  244.1 1.8 copy-start.17
  246.0 4.0 %copy-start.12 = (f32[2,128,2048]{2,1,0:T(8,128)S(1)}, f32[2,128,2048]{2,1,0:T(8,128)}, u32[]{:S(2)}) copy-start(f32[2,128,2048]{2,1,0:T(8,128)} %copy-done.11) | copy-start | bytes 6291460
  246.0 4.0 %copy-start.40 = (f32[1,2048]{1,0:T(1,128)S(1)}, f32[1,2048]{1,0:T(1,128)}, u32[]{:S(2)}) copy-start(f32[1,2048]{1,0:T(1,128)} %copy-done.39) | copy-start | bytes 24580
  246.0 4.0 %copy-start.42 = (f32[1,2048]{1,0:T(1,128)S(1)}, f32[1,2048]{1,0:T(1,128)}, u32[]{:S(2)}) copy-start(f32[1,2048]{1,0:T(1,128)} %copy-done.41) | copy-start | bytes 24580
  246.0 4.0 %copy-start.44 = (f32[1,2048]{1,0:T(1,128)S(1)}, f32[1,2048]{1,0:T(1,128)}, u32[]{:S(2)}) copy-start(f32[1,2048]{1,0:T(1,128)} %copy-done.43) | copy-start | bytes 24580
  246.0 4.0 %copy-start.46 = (f32[1,2048]{1,0:T(1,128)S(1)}, f32[1,2048]{1,0:T(1,128)}, u32[]{:S(2)}) copy-start(f32[1,2048]{1,0:T(1,128)} %copy-done.45) | copy-start | bytes 24580
  252.0 6.5 %copy-start.16 = (bf16[2,128,1024]{2,1,0:T(8,128)(2,1)S(1)}, bf16[2,128,1024]{2,1,0:T(8,128)(2,1)}, u32[]{:S(2)}) copy-start(bf16[2,128,1024]{2,1,0:T(8,128)(2,1)} %param.13) | copy-start | bytes 1572868
  252.0 6.5 %copy-start.38 = (f32[1,2,4,128]{3,1,2,0:T(2,128)S(1)}, f32[1,2,4,128]{3,1,2,0:T(2,128)}, u32[]{:S(2)}) copy-start(f32[1,2,4,128]{3,1,2,0:T(2,128)} %copy-done.37) | copy-start | bytes 12292
  252.0 6.5 %copy-start.49 = (f32[2,128]{1,0:T(2,128)S(1)}, f32[2,128]{1,0:T(2,128)}, u32[]{:S(2)}) copy-start(f32[2,128]{1,0:T(2,128)} %copy-done.48) | copy-start | bytes 3076
  266.0 2.7 copy-start.22
  366.3 3.1 copy-start.7
  383.9 1.8 copy-start.27
  (11 other events, 10.5 us)
Sparse Core Ops, SparseCore 0:
  124.5 27.3 all-gather.3

commit v2 on v1

--- a/solution.py
+++ b/solution.py
@@ -19,6 +19,7 @@
 HR = 128
 CHUNK = 512
 SLACK = 1
+TAPS = 4
 
 
 def passed_along(value, axis, by):
@@ -59,14 +60,23 @@
         p_ref[0, :, s] = p[j]
 
 
+def silu_parts(v):
+    s = jax.nn.sigmoid(v)
+    return v * s, s * (1.0 + v * (1.0 - s))
+
+
 def sweep_kernel(
-    d_ref, v_ref, dy_ref, b_ref, c_ref, a_ref, h0_ref, p0_ref, cbd_ref, bbd_ref, one_ref,
-    y_ref, dg_ref, dp_ref, cacc_ref, bacc_ref, racc_ref, h_s, a_s, g_s, w_s,
+    d_ref, u_ref, dy_ref, gg_ref, z_ref, raw_ref, b_ref, c_ref, small_ref, h0_ref, p0_ref,
+    cbd_ref, bbd_ref, one_ref,
+    gated_ref, zg_ref, ug_ref, rl_ref, cacc_ref, bacc_ref, racc_ref, sums_ref,
+    v_s, y_s, h_s, a_s, g_s, w_s,
 ):
-    state, width = a_ref.shape
-    groups = d_ref.shape[1]
+    groups, width = d_ref.shape[1], d_ref.shape[3]
+    state = b_ref.shape[2]
     cuts = [slice(j, j + LANES) for j in range(0, width, LANES)]
-    rates = [a_ref[:, s] for s in cuts]
+    all_rates = -jnp.exp(small_ref[TAPS : TAPS + state]) * LOG2E
+    rates = [all_rates[:, s] for s in cuts]
+    skip = small_ref[TAPS + state + 2 : TAPS + state + 3]
     across = (((1,), (1,)), ((), ()))
 
     @pl.when(pl.program_id(1) == 0)
@@ -78,27 +88,31 @@
 
     def forward(i, h):
         h = list(h)
+        u = u_ref[0, i].astype(F32)
+        v_s[i] = d_ref[0, i] * u
         for k in range(GROUP):
             t = i * GROUP + k
             b = b_ref[0, t]
             for j, s in enumerate(cuts):
-                row = lambda ref: jnp.broadcast_to(ref[0, i, k : k + 1, s], (state, LANES))
-                factor = jnp.exp2(row(d_ref) * rates[j])
-                h[j] = factor * h[j] + row(v_ref) * b
+                factor = jnp.exp2(jnp.broadcast_to(d_ref[0, i, k : k + 1, s], (state, LANES)) * rates[j])
+                h[j] = factor * h[j] + jnp.broadcast_to(v_s[i, k : k + 1, s], (state, LANES)) * b
                 h_s[t + 1, :, s] = h[j]
                 a_s[t, :, s] = factor
         held = h_s[pl.ds(i * GROUP + 1, GROUP)].reshape(GROUP * state, width).astype(BF16)
-        y_ref[0, i] = jnp.dot(cbd_ref[0, i], held, preferred_element_type=F32)
+        y = jnp.dot(cbd_ref[0, i], held, preferred_element_type=F32) + skip * u
         cacc_ref[0, i] += lax.dot_general(
             dy_ref[0, i].astype(BF16), held, across, preferred_element_type=F32
         )
+        gate, slope = silu_parts(z_ref[0, i].astype(F32))
+        gated_ref[0, i] = (y * gate).astype(BF16)
+        zg_ref[0, 0, i] = (gg_ref[0, i] * y * slope).astype(BF16)
         return tuple(h)
 
     lax.fori_loop(0, groups, forward, tuple(h0_ref[0, :, s] for s in cuts))
 
     def backward(turn, carry):
         i = groups - 1 - turn
-        p, total = (list(v) for v in carry)
+        p, total, sums = (list(v) for v in carry)
         for k in reversed(range(GROUP)):
             t = i * GROUP + k
             c = c_ref[0, t]
@@ -111,20 +125,29 @@
                 g_s[k, :, s] = g.astype(BF16)
                 w_s[k, :, s] = (w * rates[j]).astype(BF16)
         g_all = g_s[...].reshape(GROUP * state, width)
-        dg_ref[0, i] = jnp.dot(bbd_ref[0, i], g_all, preferred_element_type=F32)
-        dp_ref[0, i] = jnp.dot(
+        drive_grad = jnp.dot(bbd_ref[0, i], g_all, preferred_element_type=F32)
+        delta_part = jnp.dot(
             one_ref[...], w_s[...].reshape(GROUP * state, width), preferred_element_type=F32
         )
         bacc_ref[0, i] += lax.dot_general(
-            v_ref[0, i].astype(BF16), g_all, across, preferred_element_type=F32
+            v_s[i].astype(BF16), g_all, across, preferred_element_type=F32
         )
-        return tuple(p), tuple(total)
+        u, dy, delta = u_ref[0, i].astype(F32), dy_ref[0, i], d_ref[0, i]
+        raw_grad = (drive_grad * u + delta_part * (1.0 / LOG2E)) * jax.nn.sigmoid(raw_ref[0, i])
+        rl_ref[0, i] = raw_grad.astype(BF16)
+        ug_ref[0, i] = dy * skip + drive_grad * delta
+        sums[0] = sums[0] + (dy * u)[:8] + (dy * u)[8:]
+        sums[1] = sums[1] + raw_grad[:8] + raw_grad[8:]
+        return tuple(p), tuple(total), tuple(sums)
 
     zero = tuple(jnp.zeros((state, LANES), F32) for _ in cuts)
     start = tuple(p0_ref[0, :, s] for s in cuts)
-    _, total = lax.fori_loop(0, groups, backward, (start, zero))
+    none = jnp.zeros((8, width), F32)
+    _, total, sums = lax.fori_loop(0, groups, backward, (start, zero, (none, none)))
     for j, s in enumerate(cuts):
         racc_ref[0, :, s] = total[j]
+    sums_ref[0, 0] = sums[0]
+    sums_ref[0, 1] = sums[1]
 
 
 def gather_kernel(plan, *refs):
@@ -210,110 +233,169 @@
         compiler_params=pltpu.CompilerParams(collective_id=0, has_side_effects=True, vmem_limit_bytes=40<<20), name="gather")(*ops)
 
 
-def reduce_kernel(span, made, sets, lhs, rhs, pre, out, g, ra, rx, ry, mine, zlo, zhi, zout, send, recv):
+def back_kernel(
+    span, state, rank,
+    gated, zg, ug, rl, u, conv, lead, step_low, cacc, bacc, normed, x, og, bg, mask,
+    in_w, out_w, xp, dt, small, racc, sums,
+    hidden_out, input_grad, out_sum, in_sum, rest_sum,
+    pg, mixed, cg, ng, rest, g, ra, rx, ry, zlo, zhi, tot, send, recv, halo, local,
+):
     d, s, f = (lax.axis_index(a) for a in ("dp", "seq", "fsdp"))
     fx, fy, fd = f ^ 1, f ^ 2, f ^ 3
-    chunks = out.shape[0]
+    chunks = tot.shape[0]
+    rows, width = x.shape
+    inner = gated.shape[1]
+    seqs = cg.shape[0]
+    ctx = rows // seqs
+    parts = inner // CHUNK
+    out_chunks = 2 * width // CHUNK
+    in_chunks = 2 * parts
+    last = out_chunks + in_chunks
+    slots = g.shape[0]
     q = HR // 2
     root = (span - 1) // 2
     tox, toy, sib = {"fsdp": fx}, {"fsdp": fy}, {"dp": 1 - d}
     up, down = {"seq": jnp.minimum(s + 1, span - 1)}, {"seq": jnp.maximum(s - 1, 0)}
+    contract = (((0,), (0,)), ((), ()))
+    across = (((1,), (1,)), ((), ()))
+    dot = lambda a, b, dims=(((1,), (0,)), ((), ())): lax.dot_general(
+        a, b, dims, preferred_element_type=F32
+    )
+
+    cg[:, ctx:] = jnp.zeros((seqs, cg.shape[1] - ctx, inner), F32)
     barrier = pltpu.get_barrier_semaphore()
     for who in (tox, toy, sib):
         pl.semaphore_signal(barrier, inc=1, device_id=who, device_id_type=MESH)
+
     @pl.when(s > 0)
-    def _(): pl.semaphore_signal(barrier, inc=1, device_id=down, device_id_type=MESH)
+    def _():
+        pl.semaphore_signal(barrier, inc=1, device_id=down, device_id_type=MESH)
+
     @pl.when(s < span - 1)
-    def _(): pl.semaphore_signal(barrier, inc=1, device_id=up, device_id_type=MESH)
+    def _():
+        pl.semaphore_signal(barrier, inc=1, device_id=up, device_id_type=MESH)
+
     ends = (s == 0) | (s == span - 1)
     pl.semaphore_wait(barrier, jnp.where(ends, 4, 5) if span > 1 else 3)
 
     def copy(kind, c, src, dst, who):
-        return pltpu.make_async_remote_copy(src_ref=src, dst_ref=dst, send_sem=send.at[kind, c], recv_sem=recv.at[kind, c], device_id=who, device_id_type=MESH)
+        return pltpu.make_async_remote_copy(
+            src_ref=src, dst_ref=dst, send_sem=send.at[kind, c], recv_sem=recv.at[kind, c],
+            device_id=who, device_id_type=MESH,
+        )
+
     lo, hi = slice(0, q), slice(q, HR)
-    A = lambda c: copy(0, c, g.at[c, :, 1 - d], ra.at[c], sib)
-    X = lambda c: (copy(1, c, ra.at[c, fd, lo], rx.at[c, 0], tox), copy(2, c, ra.at[c, fx, lo], rx.at[c, 1], tox))
-    XV = lambda c: copy(3, c, ra.at[c, fx, hi], rx.at[c, 2], tox)
-    Y = lambda c: (copy(4, c, ra.at[c, fd, hi], ry.at[c, 0], toy), copy(5, c, ra.at[c, fy, hi], ry.at[c, 2], toy))
-    YV = lambda c: copy(6, c, ra.at[c, fy, lo], ry.at[c, 1], toy)
-    ZU = lambda c: copy(7, c, zout.at[c], zlo.at[c], up)
-    ZD = lambda c: copy(8, c, zout.at[c], zhi.at[c], down)
-    TU = lambda c: copy(9, c, out.at[c, d], out.at[c, d], up)
-    TD = lambda c: copy(10, c, out.at[c, d], out.at[c, d], down)
-    D = lambda c: copy(11, c, out.at[c, d], out.at[c, d], sib)
+    A = lambda c: copy(0, c, g.at[lax.rem(c, slots), :, 1 - d], ra.at[c], sib)
+    X0 = lambda c: copy(1, c, ra.at[c, fd, lo], rx.at[c, 0], tox)
+    X1 = lambda c: copy(2, c, ra.at[c, fx, lo], rx.at[c, 1], tox)
+    X2 = lambda c: copy(3, c, ra.at[c, fx, hi], rx.at[c, 2], tox)
+    Y0 = lambda c: copy(4, c, ra.at[c, fd, hi], ry.at[c, 0], toy)
+    Y2 = lambda c: copy(5, c, ra.at[c, fy, hi], ry.at[c, 2], toy)
+    Y1 = lambda c: copy(6, c, ra.at[c, fy, lo], ry.at[c, 1], toy)
+    ZU = lambda c: copy(7, c, ra.at[c, f], zlo.at[c], up)
+    ZD = lambda c: copy(8, c, ra.at[c, f], zhi.at[c], down)
+    TU = lambda c: copy(9, c, tot.at[c, d], tot.at[c, d], up)
+    TD = lambda c: copy(10, c, tot.at[c, d], tot.at[c, d], down)
+    D = lambda c: copy(11, c, tot.at[c, d], tot.at[c, d], sib)
     below, above = s < root, s > root
     spot = jnp.where(below, s, jnp.where(above, span - 1 - s, 0))
     far = jnp.abs(s - root)
     most = max(root, span - 1 - root)
 
-    def stage(c, body):
+    def stage(c, run):
         @pl.when((c >= 0) & (c < chunks))
-        def _(): body(c)
+        def _():
+            run(c)
 
     def produce(c):
-        @pl.when(c < made)
+        slot = lax.rem(c, slots)
+
+        @pl.when(c >= slots)
+        def _():
+            A(c - slots).wait_send()
+
+        @pl.when(c < out_chunks)
+        def _():
+            r = c // (width // CHUNK)
+            col = lax.rem(c, width // CHUNK) * CHUNK
+            right = bg[:, pl.ds(pl.multiple_of(col, CHUNK), CHUNK)]
+            for j in range(4):
+                for h in range(2):
+                    at = j * (inner // 4) + h * (inner // 8) + r * HR
+                    left = gated[:, pl.ds(pl.multiple_of(at, HR), HR)]
+                    g[slot, j, h] = dot(left, right, contract).astype(BF16)
+
+        @pl.when((c >= out_chunks) & (c < last))
+        def _():
+            right = mixed[c - out_chunks]
+            for j in range(4):
+                t = dot(normed[:, j * 2 * HR : (j + 1) * 2 * HR], right, contract).astype(BF16)
+                g[slot, j, 0] = t[:HR]
+                g[slot, j, 1] = t[HR:]
+
+        @pl.when(c == last)
         def _():
             for j in range(4):
                 for h in range(2):
-                    g[c, j, h] = pre[c, j, h]
-        @pl.when(c >= made)
-        def _():
-            k = 0
-            for first in sets[1:]:
-                k = k + (c >= first).astype(jnp.int32)
-            right = rhs[c - made]
-            for j in range(4):
-                t = jnp.dot(lhs[k, pl.ds(j * 2 * HR, 2 * HR)], right, preferred_element_type=F32).astype(BF16)
-                g[c, j, 0] = t[:HR]
-                g[c, j, 1] = t[HR:]
+                    cols = slice(j * CHUNK, (j + 1) * CHUNK)
+                    g[slot, j, h] = rest[h * HR : (h + 1) * HR, cols].astype(BF16)
+
         A(c).start()
 
     def first_sum(c):
         A(c).wait_recv()
         for j in range(4):
-            ra[c, j] = (ra[c, j].astype(F32) + g[c, j, d].astype(F32)).astype(BF16)
-        for t in X(c) + Y(c):
-            t.start()
+            own = g[lax.rem(c, slots), j, d]
+            ra[c, j] = (ra[c, j].astype(F32) + own.astype(F32)).astype(BF16)
+        X0(c).start()
+        Y0(c).start()
+        X1(c).start()
+        Y2(c).start()
 
     def second_sum(c):
-        X(c)[0].wait_recv()
+        X0(c).wait_recv()
         ra[c, fy, lo] = (ra[c, fy, lo].astype(F32) + rx[c, 0].astype(F32)).astype(BF16)
-        YV(c).start()
-        Y(c)[0].wait_recv()
+        Y1(c).start()
+        Y0(c).wait_recv()
         ra[c, fx, hi] = (ra[c, fx, hi].astype(F32) + ry[c, 0].astype(F32)).astype(BF16)
-        XV(c).start()
+        X2(c).start()
 
     def third_sum(c):
-        X(c)[1].wait_recv(); Y(c)[1].wait_recv(); XV(c).wait_recv(); YV(c).wait_recv()
-        for k, rows in enumerate((lo, hi)):
-            mine[c, rows] = ra[c, f, rows].astype(F32) + rx[c, 1 + k].astype(F32) + ry[c, 1 + k].astype(F32)
+        X1(c).wait_recv()
+        Y2(c).wait_recv()
+        X2(c).wait_recv()
+        Y1(c).wait_recv()
+        for k, part in enumerate((lo, hi)):
+            total = ra[c, f, part].astype(F32) + rx[c, 1 + k].astype(F32) + ry[c, 1 + k].astype(F32)
+            ra[c, f, part] = total.astype(BF16)
 
     def inward(c):
         @pl.when(below & (s > 0))
         def _():
             ZU(c).wait_recv()
-            zout[c] = (mine[c] + zlo[c].astype(F32)).astype(BF16)
+            ra[c, f] = (ra[c, f].astype(F32) + zlo[c].astype(F32)).astype(BF16)
+
         @pl.when(above & (s < span - 1))
         def _():
             ZD(c).wait_recv()
-            zout[c] = (mine[c] + zhi[c].astype(F32)).astype(BF16)
-        @pl.when((s != root) & ((s == 0) | (s == span - 1)))
-        def _():
-            zout[c] = mine[c].astype(BF16)
+            ra[c, f] = (ra[c, f].astype(F32) + zhi[c].astype(F32)).astype(BF16)
+
         pl.when(below)(lambda: ZU(c).start())
         pl.when(above)(lambda: ZD(c).start())
 
     def at_root(c):
-        total = mine[c]
+        total = ra[c, f].astype(F32)
         if root > 0:
             ZU(c).wait_recv()
             total = total + zlo[c].astype(F32)
         if span - 1 > root:
             ZD(c).wait_recv()
             total = total + zhi[c].astype(F32)
-        out[c, d] = total.astype(BF16)
-        if root > 0: TD(c).start()
-        if span - 1 > root: TU(c).start()
+        tot[c, d] = total.astype(BF16)
+        if root > 0:
+            TD(c).start()
+        if span - 1 > root:
+            TU(c).start()
         D(c).start()
 
     def outward(c):
@@ -321,13 +403,161 @@
         def _():
             TU(c).wait_recv()
             pl.when(s < span - 1)(lambda: TU(c).start())
+
         @pl.when(below)
         def _():
             TD(c).wait_recv()
             pl.when(s > 0)(lambda: TD(c).start())
+
         D(c).start()
 
+    tile = 2 * LANES
+
+    def columns(t, size=tile):
+        return pl.ds(pl.multiple_of(t * size, size), size)
+
+    def proj_work():
+        step_grad = dot(rl[...], dt[...], across)
+        r = lax.broadcasted_iota(jnp.int32, (rows, GROUP * state), 0)
+        k = lax.broadcasted_iota(jnp.int32, (rows, GROUP * state), 1)
+        own = lax.rem(r, GROUP) == k // state
+        pick = lambda v: jnp.where(own, v[...], 0.0).astype(BF16)
+        at = lax.rem(lax.broadcasted_iota(jnp.int32, (GROUP * state, LANES), 0), state)
+        col = lax.broadcasted_iota(jnp.int32, (GROUP * state, LANES), 1)
+        fold = lambda first: (col == at + first).astype(F32).astype(BF16)
+        grads = jnp.concatenate([step_grad, jnp.zeros((rows, LANES - rank), F32)], 1)
+        grads = grads + dot(pick(bacc), fold(rank)) + dot(pick(cacc), fold(rank + state))
+        pg[...] = grads.astype(BF16)
+        rest[...] = jnp.zeros(rest.shape, F32)
+        first = TAPS + state + 4
+        used = rank + 2 * state
+
+        def weights(t, carry):
+            cols = columns(t)
+            rest[first : first + rank, cols] = dot(step_low[...], rl[:, cols], contract)
+            rest[first + rank : first + rank + used, cols] = dot(pg[...], u[:, cols], contract)[:used]
+            logs = racc[0, :, cols]
+            kept = sums[0, :, :, cols]
+            for c in range(1, seqs):
+                logs = logs + racc[c, :, cols]
+                kept = kept + sums[c, :, :, cols]
+            rest[TAPS : TAPS + state, cols] = -logs * jnp.exp(small[TAPS : TAPS + state, cols])
+            at = TAPS + state
+            rest[at + 1 : at + 2, cols] = jnp.sum(kept[1], 0, keepdims=True)
+            rest[at + 2 : at + 3, cols] = jnp.sum(kept[0], 0, keepdims=True)
+            return carry
+
+        lax.fori_loop(0, inner // tile, weights, 0)
+
+    def conv_work(first, count):
+        def one(t, carry):
+            cols = columns(t)
+            shift = jnp.zeros((1, tile), F32)
+            taps = [jnp.zeros((1, tile), F32) for _ in range(TAPS)]
+            for c in range(seqs):
+                tok = slice(c * ctx, (c + 1) * ctx)
+                weight = xp[columns(t)]
+                back = dot(pg[tok, : weight.shape[1]], weight, across)
+                _, slope = silu_parts(conv[tok, cols])
+                grad = (ug[tok, cols] + back) * slope
+                cg[c, :ctx, cols] = grad
+                before = lead[c, :, cols].astype(F32)
+                shift = shift + jnp.sum(grad, 0, keepdims=True)
+                for k in range(TAPS):
+                    at = GROUP - TAPS + 1 + k
+                    taps[k] = taps[k] + jnp.sum(grad * before[at : at + ctx], 0, keepdims=True)
+            for k in range(TAPS):
+                rest[k : k + 1, cols] = taps[k]
+            rest[TAPS + state : TAPS + state + 1, cols] = shift
+            return carry
+
+        lax.fori_loop(first, first + count, one, 0)
+
+    edge = cg.shape[1] - ctx
+    H = lambda: pltpu.make_async_remote_copy(
+        src_ref=cg.at[:, :edge], dst_ref=cg.at[:, ctx:], send_sem=halo.at[0],
+        recv_sem=halo.at[1], device_id=down, device_id_type=MESH,
+    )
+
+    def halo_send():
+        pl.when(s > 0)(lambda: H().start())
+
+    def stream_work():
+        pl.when(s < span - 1)(lambda: H().wait_recv())
+
+        def one(t, carry):
+            cols = columns(t)
+            for c in range(seqs):
+                total = 0.0
+                for k in range(TAPS):
+                    at = TAPS - 1 - k
+                    total = total + small[k : k + 1, cols] * cg[c, at : at + ctx, cols]
+                half = pl.ds(pl.multiple_of(lax.rem(t, 2) * tile, tile), tile)
+                mixed[parts + t // 2, c * ctx : (c + 1) * ctx, half] = total.astype(BF16)
+            return carry
+
+        lax.fori_loop(0, inner // tile, one, 0)
+        pl.when(s > 0)(lambda: H().wait_send())
+
+    def hidden_work():
+        def one(t, carry):
+            cols = columns(t)
+            branch = dot(gated[...], out_w[:, cols])
+            keep = mask[...]
+            keep = jnp.concatenate([keep] * (tile // LANES), 1)
+            hidden_out[:, cols] = (x[:, cols].astype(F32) + keep * branch).astype(BF16)
+            return carry
+
+        lax.fori_loop(0, width // tile, one, 0)
+
+    def norm_work(first, count):
+        def one(k, carry):
+            cols = columns(lax.rem(k + parts, 2 * parts), CHUNK)
+            ng[...] += dot(mixed[k], in_w[:, cols], across)
+            return carry
+
+        if first == 0:
+            ng[...] = jnp.zeros(ng.shape, F32)
+        lax.fori_loop(first, first + count, one, 0)
+
+    def input_work():
+        share = width // 4
+        at = TAPS + state + 3
+        gain = jnp.concatenate(
+            [small[at : at + 1, j * CHUNK : j * CHUNK + share] for j in range(4)], 1
+        )
+
+        def one(r, total):
+            tok = pl.ds(pl.multiple_of(r * GROUP, GROUP), GROUP)
+            xs = x[tok].astype(F32)
+            inverse = lax.rsqrt(jnp.mean(xs * xs, -1, keepdims=True) + EPS)
+            grad = ng[tok]
+            scaled = grad * gain
+            slope = jnp.mean(scaled * xs, -1, keepdims=True)
+            out = inverse * scaled - xs * (inverse * inverse * inverse * slope)
+            input_grad[tok] = (out + og[tok].astype(F32)).astype(BF16)
+            return total + grad * (xs * inverse)
+
+        total = lax.fori_loop(0, rows // GROUP, one, jnp.zeros((GROUP, width), F32))
+        total = jnp.sum(total, 0, keepdims=True)
+        for j in range(4):
+            rest[at : at + 1, j * CHUNK : j * CHUNK + share] = total[:, j * share : (j + 1) * share]
+
+    mixed[:parts] = zg[...]
+    tiles = inner // tile
+    work = {
+        0: proj_work,
+        1: lambda: conv_work(0, tiles // 2),
+        2: lambda: conv_work(tiles // 2, tiles // 2),
+        3: halo_send,
+        4: hidden_work,
+        5: stream_work,
+        last - 4: lambda: norm_work(0, parts),
+        last - 3: lambda: norm_work(parts, parts),
+        last - 2: input_work,
+    }
     base = 1 + 2 * SLACK + 1
+
     def step(i, carry):
         stage(i, produce)
         stage(i - 1, first_sum)
@@ -336,32 +566,95 @@
         pl.when(s != root)(lambda: stage(i - base - SLACK * spot, inward))
         pl.when(s == root)(lambda: stage(i - base - SLACK * most, at_root))
         pl.when(s != root)(lambda: stage(i - base - SLACK * most - SLACK * far, outward))
+        for at, run in work.items():
+            pl.when(i == at)(run)
         return carry
+
     lax.fori_loop(0, chunks + base + 2 * SLACK * most + 1, step, 0)
 
     def finish(c, carry):
-        D(c).wait_recv()
-        A(c).wait_send()
-        for t in X(c) + Y(c) + (XV(c), YV(c)): t.wait_send()
+        pl.when(c >= chunks - slots)(lambda: A(c).wait_send())
+        for t in (X0, X1, X2, Y0, Y1, Y2):
+            t(c).wait_send()
         pl.when(below)(lambda: ZU(c).wait_send())
         pl.when(above)(lambda: ZD(c).wait_send())
-        if root > 0: pl.when((s <= root) & (s > 0))(lambda: TD(c).wait_send())
-        if span - 1 > root: pl.when((s >= root) & (s < span - 1))(lambda: TU(c).wait_send())
+        if root > 0:
+            pl.when((s <= root) & (s > 0))(lambda: TD(c).wait_send())
+        if span - 1 > root:
+            pl.when((s >= root) & (s < span - 1))(lambda: TU(c).wait_send())
         D(c).wait_send()
+        D(c).wait_recv()
         return carry
+
     lax.fori_loop(0, chunks, finish, 0)
-
-def reduce_grads(lhs, rhs, pre, sets):
-    made, nb, cw = pre.shape[0], rhs.shape[0], rhs.shape[2]
-    n = made + nb
+    copies = []
+    for c in range(chunks):
+        for h in range(2):
+            if c < out_chunks:
+                r, col = c // (width // CHUNK), c % (width // CHUNK)
+                first = h * (inner // 8) + r * HR
+                to = out_sum.at[first : first + HR, col * CHUNK : (col + 1) * CHUNK]
+            elif c < last:
+                col = (c - out_chunks + parts) % (2 * parts)
+                to = in_sum.at[h * HR : (h + 1) * HR, col * CHUNK : (col + 1) * CHUNK]
+            else:
+                to = rest_sum.at[h * HR : (h + 1) * HR]
+            copies.append(pltpu.make_async_copy(tot.at[c, h], to, local.at[c, h]))
+    for one in copies:
+        one.start()
+    for one in copies:
+        one.wait()
+
+
+def back(*args):
+    gated, zg, _, _, _, _, _, step_low, cacc, _, _, x = args[:12]
+    in_w, out_w = args[15:17]
+    rows, inner = gated.shape
+    width = x.shape[1]
+    state = cacc.shape[1] // GROUP
+    rank = step_low.shape[1]
+    seqs = args[20].shape[0]
     span = lax.axis_size("seq")
-    v = pltpu.VMEM
-    return pl.pallas_call(functools.partial(reduce_kernel, span, made, sets),
-        in_specs=[pl.BlockSpec(memory_space=v)] * 3, out_specs=pl.BlockSpec(memory_space=v),
-        out_shape=jax.ShapeDtypeStruct((n, 2, HR, cw), BF16),
-        scratch_shapes=[v((n, 4, 2, HR, cw), BF16), v((n, 4, HR, cw), BF16), v((n, 3, HR // 2, cw), BF16), v((n, 3, HR // 2, cw), BF16), v((n, HR, cw), F32), v((n, HR, cw), BF16), v((n, HR, cw), BF16), v((n, HR, cw), BF16),
-            pltpu.SemaphoreType.DMA((12, n)), pltpu.SemaphoreType.DMA((12, n))],
-        compiler_params=pltpu.CompilerParams(collective_id=1, has_side_effects=True, vmem_limit_bytes=60 << 20), name="reduce")(lhs, rhs, pre)
+    out_chunks, in_chunks = 2 * width // CHUNK, 2 * inner // CHUNK
+    n = out_chunks + in_chunks + 1
+    vmem, dma = pltpu.VMEM, pltpu.SemaphoreType.DMA
+    any_space = pl.BlockSpec(memory_space=pl.ANY)
+    whole = pl.BlockSpec(memory_space=vmem)
+    shape = jax.ShapeDtypeStruct
+    return pl.pallas_call(
+        functools.partial(back_kernel, span, state, rank),
+        in_specs=[whole] * len(args),
+        out_specs=[whole, whole, any_space, any_space, any_space],
+        out_shape=[
+            shape((rows, width), BF16),
+            shape((rows, width), BF16),
+            shape((inner // 4, width), BF16),
+            shape((width // 4, 2 * inner), BF16),
+            shape((2 * HR, CHUNK), BF16),
+        ],
+        scratch_shapes=[
+            vmem((rows, LANES), BF16),
+            vmem((in_chunks, rows, CHUNK), BF16),
+            vmem((seqs, rows // seqs + 8, inner), F32),
+            vmem((rows, width), F32),
+            vmem((2 * HR, inner), F32),
+            vmem((4, 4, 2, HR, CHUNK), BF16),
+            vmem((n, 4, HR, CHUNK), BF16),
+            vmem((n, 3, HR // 2, CHUNK), BF16),
+            vmem((n, 3, HR // 2, CHUNK), BF16),
+            vmem((n, HR, CHUNK), BF16),
+            vmem((n, HR, CHUNK), BF16),
+            vmem((n, 2, HR, CHUNK), BF16),
+            dma((12, n)),
+            dma((12, n)),
+            dma((2,)),
+            dma((n, 2)),
+        ],
+        compiler_params=pltpu.CompilerParams(
+            collective_id=1, has_side_effects=True, vmem_limit_bytes=63 << 20
+        ),
+        name="back",
+    )(*args)
 
 
 def block_diagonal(v):
@@ -369,14 +662,6 @@
     eye = jnp.eye(GROUP, dtype=F32)[None, None, :, :, None]
     spread = v.reshape(seqs, ctx // GROUP, GROUP, 1, state) * eye
     return spread.reshape(seqs, ctx // GROUP, GROUP, GROUP * state).astype(BF16)
-
-
-def diagonal_blocks(v):
-    seqs, groups, _, wide = v.shape
-    state = wide // GROUP
-    eye = jnp.eye(GROUP, dtype=F32)[None, None, :, :, None]
-    picked = jnp.sum(v.reshape(seqs, groups, GROUP, GROUP, state) * eye, 3)
-    return picked.reshape(seqs * groups * GROUP, state)
 
 
 def local_specs(seqs, ctx, inner, state, width):
@@ -405,34 +690,42 @@
     )(delta, drive, dy, b_wide, c_wide, rates)
 
 
-def sweep(delta, drive, dy, b_in, c_in, b_wide, c_wide, rates, start, final):
+def sweep(delta, u, dy, gated_grad, gate_in, raw, b_in, c_in, b_wide, c_wide, small, start, final):
     seqs, groups, _, inner = delta.shape
     ctx = groups * GROUP
-    state = rates.shape[0]
-    width = 512
-    tok, wide, rate, end, diag = local_specs(seqs, ctx, inner, state, width)
+    state = b_in.shape[2]
+    width = CHUNK
+    tok, wide, _, end, diag = local_specs(seqs, ctx, inner, state, width)
     ones = block_diagonal(jnp.ones((1, GROUP, state), F32))[0, 0]
-    token_shape = jax.ShapeDtypeStruct(delta.shape, F32)
+    token = lambda t: jax.ShapeDtypeStruct(delta.shape, t)
     diag_shape = jax.ShapeDtypeStruct((seqs, groups, GROUP, GROUP * state), F32)
+    chunked = pl.BlockSpec((1, 1, groups, GROUP, width), lambda c, j: (j, c, 0, 0, 0))
+    chunked_shape = jax.ShapeDtypeStruct((inner // width, seqs, groups, GROUP, width), BF16)
+    vmem = pltpu.VMEM
     return pl.pallas_call(
         sweep_kernel,
         grid=(seqs, inner // width),
-        in_specs=[tok, tok, tok, wide, wide, rate, end, end, diag, diag]
-        + [pl.BlockSpec(ones.shape, lambda c, j: (0, 0))],
-        out_specs=[tok, tok, tok, diag, diag, end],
-        out_shape=[token_shape] * 3
+        in_specs=[tok] * 6
+        + [wide, wide, pl.BlockSpec((small.shape[0], width), lambda c, j: (0, j)), end, end]
+        + [diag, diag, pl.BlockSpec(ones.shape, lambda c, j: (0, 0))],
+        out_specs=[tok, chunked, tok, tok, diag, diag, end]
+        + [pl.BlockSpec((1, 2, 8, width), lambda c, j: (c, 0, 0, j))],
+        out_shape=[token(BF16), chunked_shape, token(F32), token(BF16)]
         + [diag_shape] * 2
-        + [jax.ShapeDtypeStruct((seqs, state, inner), F32)],
+        + [jax.ShapeDtypeStruct((seqs, state, inner), F32)]
+        + [jax.ShapeDtypeStruct((seqs, 2, 8, inner), F32)],
         scratch_shapes=[
-            pltpu.VMEM((ctx + 1, state, width), F32),
-            pltpu.VMEM((ctx, state, width), F32),
-            pltpu.VMEM((GROUP, state, width), BF16),
-            pltpu.VMEM((GROUP, state, width), BF16),
+            vmem((groups, GROUP, width), F32),
+            vmem((groups, GROUP, width), F32),
+            vmem((ctx + 1, state, width), F32),
+            vmem((ctx, state, width), F32),
+            vmem((GROUP, state, width), BF16),
+            vmem((GROUP, state, width), BF16),
         ],
         compiler_params=pltpu.CompilerParams(vmem_limit_bytes=56 << 20),
         name="sweep",
     )(
-        delta, drive, dy, b_wide, c_wide, rates, start, final,
+        delta, u, dy, gated_grad, gate_in, raw, b_wide, c_wide, small, start, final,
         block_diagonal(c_in), block_diagonal(b_in), ones,
     )
 
@@ -520,88 +813,26 @@
         decay = jnp.exp2(sums[r][:, None, :] * rates2)
         final = jnp.where(r > me, decay * final + ends[r, 1].astype(F32), final)
 
-    y, drive_grad, delta_part, c_acc, b_acc, rate_grad = sweep(
-        *scan_args, b_in, c_in, b_wide, c_wide, rates2, start, final
+    gated, z_grad, u_grad, raw_low, c_acc, b_acc, rate_grad, sums = sweep(
+        grouped(delta), grouped(u_low), grouped(y_grad), grouped(gated_grad),
+        grouped(mixed[:, inner:]), grouped(raw), b_in, c_in, b_wide, c_wide, small, start, final,
     )
-    ungrouped = lambda v: v.reshape(seqs, ctx, inner)
-    y_val = ungrouped(y) + skip * u_float
-    drive_grad = ungrouped(drive_grad)
-    c_grad, b_grad = diagonal_blocks(c_acc), diagonal_blocks(b_acc)
-    log_grad = jnp.sum(rate_grad, 0) * rates
-
-    gated = (y_val * gate_act).astype(BF16).reshape(rows, inner)
-    branch = dot(gated, out_matrix).reshape(seqs, ctx, width)
-    hidden_out = (x_tok + mask * branch).astype(BF16)
-    contract = lambda a, b: lax.dot_general(
-        a, b, (((0,), (0,)), ((), ())), preferred_element_type=F32
+    flat = lambda v: v.reshape(rows, -1)
+    lead = jnp.concatenate([jnp.zeros((seqs, GROUP - reach, inner), BF16), before, stream], 1)
+    hidden_out, input_grad, out_sum, in_sum, rest = back(
+        flat(gated), z_grad.reshape(-1, rows, CHUNK), flat(u_grad), flat(raw_low), u_rows,
+        flat(conv_out), lead, step_low, flat(c_acc), flat(b_acc), normed, flat(hidden_in),
+        flat(out_grad), branch_grad, jnp.broadcast_to(mask, (seqs, ctx, LANES)).reshape(rows, LANES),
+        in_matrix, out_matrix, proj_matrix, step_matrix, small, rate_grad, sums,
     )
-    out_w_grad = contract(gated, branch_grad)
-    z_grad = gated_grad * y_val * silu_grad(gate_in)
-    skip_grad = jnp.sum(y_grad * u_float, (0, 1))
-    delta_grad = drive_grad * u_float + ungrouped(delta_part) * (1.0 / LOG2E)
-    u_grad = y_grad * skip + drive_grad * delta
-    raw_grad = delta_grad * jax.nn.sigmoid(raw)
-    bias_grad = jnp.sum(raw_grad, (0, 1))
-    raw_low = raw_grad.astype(BF16).reshape(rows, inner)
-    step_w_grad = contract(step_low, raw_low)
-    step_grad = lax.dot_general(
-        raw_low, step_matrix, (((1,), (1,)), ((), ())), preferred_element_type=F32
-    )
-    proj_grad = jnp.concatenate([step_grad, b_grad, c_grad], 1).astype(BF16)
-    proj_w_grad = contract(proj_grad, u_rows)
-    u_grad = u_grad + lax.dot_general(
-        proj_grad, proj_matrix, (((1,), (1,)), ((), ())), preferred_element_type=F32
-    ).reshape(seqs, ctx, inner)
-    conv_grad = u_grad * silu_grad(conv_out)
-    shift_grad = jnp.sum(conv_grad, (0, 1))
-    taps_grad = jnp.stack(
-        [jnp.sum(conv_grad * extended[:, k : k + ctx], (0, 1)) for k in range(taps)], 0
-    )
-    after = passed_along(conv_grad[:, :reach], "seq", -1)
-    later = jnp.concatenate([conv_grad, after], 1)
-    stream_grad = sum(conv_taps[k] * later[:, reach - k : reach - k + ctx] for k in range(taps))
-    mixed_grad = jnp.concatenate(
-        [stream_grad.reshape(rows, inner), z_grad.reshape(rows, inner)], 1
-    ).astype(BF16)
-    in_w_grad = contract(normed, mixed_grad)
-    normed_grad = lax.dot_general(
-        mixed_grad, in_matrix, (((1,), (1,)), ((), ())), preferred_element_type=F32
-    ).reshape(seqs, ctx, width)
-    gain_grad = jnp.sum(normed_grad * x_tok * inverse, (0, 1))
-    scaled = normed_grad * gain
-    x_grad = (
-        inverse * scaled
-        - x_tok * inverse * inverse * inverse * jnp.mean(scaled * x_tok, -1, keepdims=True)
-        + cotangent
-    )
-    input_grad = x_grad.astype(BF16)
-
+    rest = rest.astype(F32)
     shards = lax.axis_size("fsdp")
-    gain_rows = jnp.pad(gain_grad.reshape(shards, -1), ((0, 0), (0, share - width // shards)))
-    rest = jnp.concatenate(
-        [taps_grad, log_grad, shift_grad[None], bias_grad[None], skip_grad[None]]
-        + [gain_rows.reshape(1, inner), step_w_grad, proj_w_grad],
-        0,
-    )
-    rest = jnp.pad(rest, ((0, 2 * HR - rest.shape[0]), (0, 0))).astype(BF16)
-    pre = rest.reshape(2, HR, shards, share // CHUNK, CHUNK).transpose(3, 2, 0, 1, 4)
-    tall = gated.T.reshape(shards, 2, 2, HR, rows).transpose(2, 0, 1, 3, 4)
-    lhs = jnp.concatenate([tall.reshape(2, -1, rows), normed.T[None]], 0)
-    right = branch_grad.reshape(rows, -1, CHUNK).transpose(1, 0, 2)
-    mixed_right = mixed_grad.reshape(rows, -1, CHUNK).transpose(1, 0, 2)
-    made, part = pre.shape[0], right.shape[0]
-    sums = reduce_grads(
-        lhs, jnp.concatenate([right, right, mixed_right], 0), pre, (made, made + part, made + 2 * part)
-    ).astype(F32)
-    rest = sums[:made].transpose(1, 2, 0, 3).reshape(2 * HR, share)
-    out_w = sums[made : made + 2 * part].reshape(2, part, 2, HR, CHUNK).transpose(2, 0, 3, 1, 4)
-    out_w = out_w.reshape(-1, width)
-    in_w = sums[made + 2 * part :].transpose(1, 2, 0, 3).reshape(2 * HR, 2 * inner)
     at = taps + state
     return (
-        hidden_out, input_grad, rest[at + 3, : width // shards], in_w, rest[:taps], rest[at],
+        hidden_out.reshape(seqs, ctx, width), input_grad.reshape(seqs, ctx, width),
+        rest[at + 3, : width // shards], in_sum.astype(F32), rest[:taps], rest[at],
         rest[at + 4 + rank : at + 4 + rank + proj_matrix.shape[1]].T, rest[at + 4 : at + 4 + rank],
-        rest[at + 1], rest[taps:at], rest[at + 2], out_w,
+        rest[at + 1], rest[taps:at], rest[at + 2], out_sum.astype(F32),
     )
 
 

time: 398 us -> 343 us (0.86)
  local copies, waits for them, and re-layouts: 73.6 us -> 29.6 us
  other arithmetic: 42.5 us -> 25.4 us
  Pallas kernels: 219 us -> 236 us
  matrix products: 27.5 us -> 15.6 us
  waiting for transfers between devices: 0.73 us -> 8.13 us
    reduce_sum x6 -> x0, other arithmetic: 17.6 us -> none  [the longest x1 5.72 us: body(): jnp.sum(conv_grad * extended[:, k:k + ctx], (0, 1))]
    pallas_call x2, Pallas kernels: 144 us -> 160 us  [the longest x1 101 us: back(): pl.pallas_call(functools.partial(back_kernel, span, state, rank), in_spec...]
    reshape x9 -> x0, local copies, waits for them, and re-layouts: 11.8 us -> none  [the longest x2 5.11 us: body(): rest.reshape(2, HR, shards, share // CHUNK, CHUNK).transpose(3, 2, 0, 1, 4)]
    dot_general x5 -> x0, matrix products: 10.8 us -> none  [the longest x1 6.43 us: body(): lax.dot_general(mixed_grad, in_matrix, (((1,), (1,)), ((), ())), preferre...]
    unnamed x119 -> x53, local copies, waits for them, and re-layouts: 20.8 us -> 10.5 us
    all_gather x1, waiting for transfers between devices: 0.01 us -> 8.11 us  [body(): lax.all_gather(jnp.stack([local_end, local_back]).astype(BF16), 'seq')]
    concatenate x5 -> x1, local copies, waits for them, and re-layouts: 8.12 us -> 0.52 us  [body(): jnp.concatenate([jnp.zeros((seqs, GROUP - reach, inner), BF16), before, s...]
    mul x6, local copies, waits for them, and re-layouts: 9.47 us -> 2.98 us  [block_diagonal(): spread = v.reshape(seqs, ctx // GROUP, GROUP, 1, state) * eye]
  transfers between devices with their start and end apart: 3 -> 2, of which waited for: 1 -> 1; matrix products, arithmetic and copies ran while one was open for 8% -> 5% of each run, Pallas kernels for 0% -> 0%
where the time goes in v2:
time: 343 us; the launch traced here: 342 us
  Pallas kernels  236 us (69%)
  local copies, waits for them, and re-layouts  29.6 us (9%)
  other arithmetic  25.4 us (7%)
  matrix products  15.6 us (5%)
  between operations  14.4 us (4%)
  blocking collectives  11 us (3%)
  waiting for transfers between devices  8.13 us (2%)
    pallas_call x1, Pallas kernels, back(): pl.pallas_call(functools.partial(back_kernel, span, state, rank), in_spec...  101 us
    pallas_call x1, Pallas kernels, gather(): pl.pallas_call(functools.partial(gather_kernel, plan), in_specs=[pl.Block...  61.9 us
    pallas_call x1, Pallas kernels, sweep(): pl.pallas_call(sweep_kernel, grid=(seqs, inner // width), in_specs=[tok]...  59.3 us
    pallas_call x1, Pallas kernels, local_ends(): pl.pallas_call(ends_kernel, grid=(seqs, inner // width), in_specs=[tok, t...  13.8 us
    all_gather x1, blocking collectives, body(): sums = lax.all_gather(jnp.sum(delta, 1), 'seq')  11 us
    unnamed x53, local copies, waits for them, and re-layouts  10.5 us
    dot_general x3, matrix products, body(): dot = lambda a, b: jnp.dot(a, b, preferred_element_type=F32)  9.76 us
    all_gather x1, waiting for transfers between devices, body(): lax.all_gather(jnp.stack([local_end, local_back]).astype(BF16), 'seq')  8.11 us
  transfers between devices with their start and end apart: 2, of which 1 were waited for; matrix products, arithmetic and copies ran while one was open for 5% of the time, Pallas kernels for 0%

profile of v2, /device:TPU:25, one launch (start us, length us, event | category | flops | bytes accessed | tf_op | source)
XLA Modules:
  0.0 341.9 jit_solution(1659621858582748243)
XLA Ops:
  7.2 1.0 copy.37.refs_2_
  8.2 0.7 pad.8
  8.9 2.3 concatenate.17
  11.2 1.6 copy-done.2
  12.8 1.2 copy-done.5
  14.0 0.8 copy-done.6
  14.9 61.9 %gather.1 = (bf16[1024,4096]{1,0:T(8,128)(2,1)}, bf16[2048,1024]{1,0:T(8,128)(2,1)S(1)}, bf16[2048,96]{1,0:T(8,128)(2,1)S(1)}, bf16[64,2048]{1,0:T(8,128)(2,1)S(1)}, f32[32,2048]{1,0:T(8,128)S(1)}) custom-call(bf16[256,4096]{1,0:T(8,128)(2,1)S(1)} %copy-done.2, bf16[512,1024]{1,0:T(8,128)(2,1)S(1)} %copy-done.5, bf16[512,96]{1,0:T(8,128)(2,1)S(1)} %copy.37.refs_2_, ...), custom_call_target="tpu_custom_call" | custom-call | tf_op jit(solution)/shard_map/gather/pallas_call | solution.py:228
  76.8 2.0 copy-done
  79.3 0.8 copy-done.10
  80.1 5.7 %convolution_convert_fusion = bf16[256,4096]{1,0:T(8,128)(2,1)S(1)} fusion(bf16[256,1024]{1,0:T(8,128)(2,1)S(1)} %bitcast.133, bf16[1024,4096]{1,0:T(8,128)(2,1)} %get-tuple-element.33.in_w), kind=kOutput, calls=%fused_computation.2 | convolution fusion | flops 2148532224 | bytes 11010048 | tf_op jit(solution)/shard_map/dot_general | solution.py:758
  86.1 1.5 collective-permute-start
  87.7 1.2 multiply_convert_fusion.1
  88.9 5.8 %fusion.5 = (f32[2,8,16,2048]{3,2,1,0:T(8,128)}, f32[2,8,16,2048]{3,2,1,0:T(8,128)}) fusion(bf16[2,8,16,2048]{3,2,1,0:T(8,128)(2,1)S(1)} %bitcast.129, bf16[2,8,16,1024]{3,2,1,0:T(8,128)(2,1)S(1)} %bitcast.135, bf16[2048,1024]{1,0:T(8,128)(2,1)} %copy-done), kind=kOutput, calls=%fused_computation.10 | convolution fusion | flops 1076887552 | bytes 9961472 | tf_op jit(solution)/shard_map/dot_general | solution.py:791
  94.8 0.7 negate_multiply_fusion.a_ref
  95.8 2.6 multiply_convert_fusion
  99.1 3.6 %fusion.13 = (f32[2,2048]{1,0:T(2,128)}, f32[2,128,2048]{2,1,0:T(8,128)}, f32[256,2048]{1,0:T(8,128)S(1)}) fusion(f32[2048]{0:T(1024)S(1)} %bitcast.148, bf16[2,128,2048]{2,1,0:T(8,128)(2,1)S(1)} %get-tuple-element.54, bf16[64,2048]{1,0:T(8,128)(2,1)S(1)} %get-tuple-element.35.dt, f32[256,96]{0,1:T(8,128)S(1)} %fusion.29), kind=kOutput, calls=%fused_computation.30 | convolution fusion | flops 72347648 | bytes 5562368 | tf_op jit(solution)/shard_map/dot_general | solution.py:758
  102.7 3.1 compare_select_fusion.1
  105.8 2.0 broadcast_in_dim.25.b_ref
  107.8 1.9 broadcast_in_dim.27.c_ref
  109.7 13.8 %ends.1 = (f32[2,16,2048]{2,1,0:T(8,128)}, f32[2,16,2048]{2,1,0:T(8,128)}) custom-call(f32[2,8,16,2048]{3,2,1,0:T(8,128)} %get-tuple-element.52.d_ref, f32[2,8,16,2048]{3,2,1,0:T(8,128)} %bitcast.127, f32[2,8,16,2048]{3,2,1,0:T(8,128)} %get-tuple-element.78.dy_ref, f32[2,128,16,128]{3,2,1,0:T(8,128)} %broadcast_in_dim.25.b_ref, ...), custom_call_target="tpu_custom_call" | custom-call | tf_op jit(solution)/shard_map/ends/pallas_call | solution.py:682
  123.5 1.1 convert_bitcast_fusion
  124.6 0.7 pad_maximum_fusion.1
  125.6 0.6 convert_element_type.156.one_ref
  126.7 0.6 compare_convert_fusion
  127.4 0.6 slice.257
  128.1 0.9 mul.300
  129.3 1.5 mul.307
  130.8 0.7 copy.48.step_low
  131.6 11.0 %all-gather.1 = f32[4,2,2048]{2,1,0:T(2,128)S(1)} all-gather(f32[1,2,2048]{2,1,0:T(2,128)S(1)} %bitcast.150), channel_id=2, replica_groups=mesh['dp'=2,'seq'=4,'fsdp'=4] {'seq'}, dimensions={0}, use_global_device_ids=true | all-gather | bytes 81920 | tf_op jit(solution)/shard_map/all_gather | solution.py:806
  142.5 1.7 multiply_convert_fusion.2
  144.3 1.4 pad_maximum_fusion.lead
  145.6 8.1 %all-gather.4.cloned.1.call-done = bf16[4,2,2,16,2048]{4,3,2,1,0:T(8,128)(2,1)} async-done(((bf16[1,2,2,16,2048]{4,3,2,1,0:T(8,128)(2,1)}), bf16[4,2,2,16,2048]{4,3,2,1,0:T(8,128)(2,1)}) %all-gather.4.cloned.1.call-update) | async-done | bytes 1048592 | tf_op jit(solution)/shard_map/all_gather | solution.py:805
  153.8 2.1 fusion.14.p0_ref
  155.8 2.1 fusion.18.h0_ref
  157.9 59.3 %sweep.1 = (bf16[2,8,16,2048]{3,2,1,0:T(8,128)(2,1)}, bf16[4,2,8,16,512]{4,3,2,1,0:T(8,128)(2,1)}, f32[2,8,16,2048]{3,2,1,0:T(8,128)}, bf16[2,8,16,2048]{3,2,1,0...) custom-call(f32[2,8,16,2048]{3,2,1,0:T(8,128)} %get-tuple-element.52, ...), custom_call_target="tpu_custom_call" | custom-call | tf_op jit(solution)/shard_map/sweep/pallas_call | solution.py:705
  217.2 0.8 broadcast_in_dim.58.mask
  218.0 101.1 %back.1 = (bf16[256,1024]{1,0:T(8,128)(2,1)}, bf16[256,1024]{1,0:T(8,128)(2,1)}, bf16[512,1024]{1,0:T(8,128)(2,1)}, bf16[256,4096]{1,0:T(8,128)(2,1)}, bf16[256,512]{1,0:T(8,128)(2,1)}) custom-call(bf16[256,2048]{1,0:T(8,128)(2,1)} %bitcast.141, bf16[4,256,512]{2,1,0:T(8,128)(2,1)} %bitcast.142, f32[256,2048]{1,0:T(8,128)} %bitcast.131, ...), custom_call_target="tpu_custom_call" | custom-call | tf_op jit(solution)/shard_map/back/pallas_call | solution.py:624
  319.2 1.0 convert_element_type.158
  320.2 1.5 slice.202
  321.7 1.4 slice.204
  323.0 1.3 slice.199
  324.3 1.4 fusion.25
  325.7 1.2 slice.198
  327.0 4.2 %convert_element_type.159 = f32[256,4096]{1,0:T(8,128)} convert(bf16[256,4096]{1,0:T(8,128)(2,1)} %get-tuple-element.50) | non-fusion elementwise | flops 1048576 | bytes 6291456 | tf_op jit(solution)/shard_map/convert_element_type | solution.py:833
  331.2 1.6 convert_element_type.160
  332.7 0.7 slice_bitcast_fusion
  333.4 0.8 copy.52
  334.2 0.8 copy.53
  (70 shorter events, 3.0 us)
Async XLA Ops:
  7.2 146.6 %all-gather.4.cloned.1.call-start = ((), (), s32[]{:S(2)}) async-start(), calls=%async_computation | async-start | bytes 1310720 | tf_op jit(solution)/shard_map/all_gather | solution.py:805
  11.2 1.6 copy-start.2
  12.8 1.2 copy-start.5
  14.0 0.8 copy-start.6
  14.9 64.0 %copy-start.8 = (bf16[2,128,1024]{2,1,0:T(8,128)(2,1)S(1)}, bf16[2,128,1024]{2,1,0:T(8,128)(2,1)}, u32[]{:S(2)}) copy-start(bf16[2,128,1024]{2,1,0:T(8,128)(2,1)} %param.13) | copy-start | bytes 1572868
  76.8 2.0 copy-start
  78.8 15.9 %copy-start.3 = (f32[32,2048]{1,0:T(8,128)}, f32[32,2048]{1,0:T(8,128)S(1)}, u32[]{:S(2)}) copy-start(f32[32,2048]{1,0:T(8,128)S(1)} %get-tuple-element.32.small_ref.small) | copy-start | bytes 786436
  78.8 19.6 %copy-start.1 = (bf16[2048,96]{1,0:T(8,128)(2,1)}, bf16[2048,96]{1,0:T(8,128)(2,1)S(1)}, u32[]{:S(2)}) copy-start(bf16[2048,96]{1,0:T(8,128)(2,1)S(1)} %get-tuple-element.34.xp) | copy-start | bytes 1179652
  78.8 20.3 %copy-start.4 = (bf16[64,2048]{1,0:T(8,128)(2,1)}, bf16[64,2048]{1,0:T(8,128)(2,1)S(1)}, u32[]{:S(2)}) copy-start(bf16[64,2048]{1,0:T(8,128)(2,1)S(1)} %get-tuple-element.35.dt) | copy-start | bytes 786436
  79.3 0.8 copy-start.10
  85.8 1.8 copy-start.21
  86.1 8.7 %copy-start.9 = (bf16[256,2048]{1,0:T(8,128)(2,1)}, bf16[256,2048]{1,0:T(8,128)(2,1)S(1)}, u32[]{:S(2)}) copy-start(bf16[256,2048]{1,0:T(8,128)(2,1)S(1)} %get-tuple-element.58) | copy-start | bytes 3145732
  86.1 9.3 %collective-permute-start = (bf16[2,3,2048]{2,1,0:T(4,128)(2,1)S(1)}, bf16[2,3,2048]{2,1,0:T(4,128)(2,1)S(1)}, u32[]{:S(2)}, u32[]{:S(2)}) collective-permute-start(bf16[2,3,2048]{2,1,0:T(4,128)(2,1)S(1)} %slice.177), channel_id=1, source_target_pairs={{0,4},{4,8},{8,12},{1,5},{5,9},{9,13},{2,6},{6,10},{10,14},{3,7},{... | collective-permute-start | bytes 73736 | tf_op jit(solution)/shard_map/ppermute | solution.py:28
  88.9 5.9 %copy-start.11 = (bf16[2,128,1024]{2,1,0:T(8,128)(2,1)}, bf16[2,128,1024]{2,1,0:T(8,128)(2,1)S(1)}, u32[]{:S(2)}) copy-start(bf16[2,128,1024]{2,1,0:T(8,128)(2,1)S(1)} %multiply_convert_fusion.1) | copy-start | bytes 1572868
  95.5 3.0 copy-start.16
  98.4 4.3 %copy-start.7 = (bf16[2,128,2048]{2,1,0:T(8,128)(2,1)}, bf16[2,128,2048]{2,1,0:T(8,128)(2,1)S(1)}, u32[]{:S(2)}) copy-start(bf16[2,128,2048]{2,1,0:T(8,128)(2,1)S(1)} %get-tuple-element.54) | copy-start | bytes 3145732
  129.2 1.6 copy-start.18
  129.2 2.3 copy-start.19
  129.3 15.0 %copy-start.17 = (bf16[2,3,2048]{2,1,0:T(4,128)(2,1)S(1)}, bf16[2,3,2048]{2,1,0:T(4,128)(2,1)}, u32[]{:S(2)}) copy-start(bf16[2,3,2048]{2,1,0:T(4,128)(2,1)} %copy-done.16) | copy-start | bytes 73732
  129.3 15.0 %copy-start.22 = (bf16[144]{0:T(256)(128)(2,1)S(1)}, bf16[144]{0:T(256)(128)(2,1)}, u32[]{:S(2)}) copy-start(bf16[144]{0:T(256)(128)(2,1)} %pad.10.clone) | copy-start | bytes 868
  130.8 22.9 %copy-start.12 = (f32[16,2048]{1,0:T(8,128)S(1)}, f32[16,2048]{1,0:T(8,128)}, u32[]{:S(2)}) copy-start(f32[16,2048]{1,0:T(8,128)} %negate_multiply_fusion.a_ref) | copy-start | bytes 393220
  157.9 59.3 %copy-start.20 = (f32[256]{0:T(256)S(1)}, f32[256]{0:T(256)}, u32[]{:S(2)}) copy-start(f32[256]{0:T(256)} %compare_convert_fusion) | copy-start | bytes 3076
  327.0 4.2 %copy-start.13 = (bf16[512,1024]{1,0:T(8,128)(2,1)S(1)}, bf16[512,1024]{1,0:T(8,128)(2,1)}, u32[]{:S(2)}) copy-start(bf16[512,1024]{1,0:T(8,128)(2,1)} %get-tuple-element.51) | copy-start | bytes 3145732
  331.2 2.3 copy-start.15
  331.2 3.1 copy-start.14
Sparse Core Ops, SparseCore 0:
  125.5 28.2 all-gather.3

commit v3 on v2

--- a/solution.py
+++ b/solution.py
@@ -20,44 +20,6 @@
 CHUNK = 512
 SLACK = 1
 TAPS = 4
-
-
-def passed_along(value, axis, by):
-    size = lax.axis_size(axis)
-    pairs = [(i, i + by) for i in range(size) if 0 <= i + by < size]
-    return lax.ppermute(value, axis, pairs)
-
-
-def silu_grad(v):
-    s = jax.nn.sigmoid(v)
-    return s * (1.0 + v * (1.0 - s))
-
-
-def ends_kernel(d_ref, v_ref, dy_ref, b_ref, c_ref, a_ref, h_ref, p_ref):
-    state, width = a_ref.shape
-    groups = d_ref.shape[1]
-    cuts = [slice(j, j + LANES) for j in range(0, width, LANES)]
-    rates = [a_ref[:, s] for s in cuts]
-
-    def step(i, carry):
-        h, run, p = (list(v) for v in carry)
-        for k in range(GROUP):
-            b = b_ref[0, i * GROUP + k]
-            c = c_ref[0, i * GROUP + k]
-            for j, s in enumerate(cuts):
-                row = lambda ref: jnp.broadcast_to(ref[0, i, k : k + 1, s], (state, LANES))
-                factor = jnp.exp2(row(d_ref) * rates[j])
-                h[j] = factor * h[j] + row(v_ref) * b
-                run[j] = run[j] * factor
-                p[j] = p[j] + run[j] * (c * row(dy_ref))
-        return tuple(h), tuple(run), tuple(p)
-
-    zero = tuple(jnp.zeros((state, LANES), F32) for _ in cuts)
-    one = tuple(jnp.ones((state, LANES), F32) for _ in cuts)
-    h, _, p = lax.fori_loop(0, groups, step, (zero, one, zero))
-    for j, s in enumerate(cuts):
-        h_ref[0, :, s] = h[j]
-        p_ref[0, :, s] = p[j]
 
 
 def silu_parts(v):
@@ -150,87 +112,553 @@
     sums_ref[0, 1] = sums[1]
 
 
-def gather_kernel(plan, *refs):
-    n = 5
-    srcs, dsts = refs[:n], refs[n:2*n]
-    send, recv, local = refs[2*n:]
-    d, f = lax.axis_index("dp"), lax.axis_index("fsdp")
+def front_kernel(
+    span,
+    x, og, lengths, taps_own, log_own, cbias_own, dbias_own, skip_own, gain_own,
+    in_own, out_own, xp_own, dt_own,
+    normed_out, bg, mask, lead, conv, u, gate, raw, delta, bw, cw, bbd, cbd, gg, dy, step_low,
+    start, final, in_full, out_full, xp_full, dt_full, small_full,
+    in_w, out_w, xp, dt, small, small_own, hx, acc, zacc, normed, v, proj, ends, sums,
+    ends_in, sums_in,
+    send, recv, halo, relay_send, relay_recv, sums_send, sums_recv, local, keep,
+):
+    d, s, f = (lax.axis_index(a) for a in ("dp", "seq", "fsdp"))
     fx, fy, fd = f ^ 1, f ^ 2, f ^ 3
-    sib = {"dp": 1 - d}
-    tox, toy = {"fsdp": fx}, {"fsdp": fy}
+    tox, toy, sib = {"fsdp": fx}, {"fsdp": fy}, {"dp": 1 - d}
+    rows, width = x.shape
+    inner = u.shape[1]
+    seqs = bw.shape[0]
+    ctx = rows // seqs
+    state, rank = log_own.shape[0], dt_own.shape[0]
+    groups = ctx // GROUP
+    share = inner // 4
+    at_state, at_bias = TAPS, TAPS + state
+    across = (((1,), (1,)), ((), ()))
+    dot = lambda a, b, dims=(((1,), (0,)), ((), ())): lax.dot_general(
+        a, b, dims, preferred_element_type=F32
+    )
+
+    for c in range(seqs):
+        hx[c] = jnp.zeros((GROUP, width), BF16)
     barrier = pltpu.get_barrier_semaphore()
     for who in (tox, toy, sib):
         pl.semaphore_signal(barrier, inc=1, device_id=who, device_id_type=MESH)
-    pl.semaphore_wait(barrier, 3)
+
+    def greet(o, carry):
+        who = {"seq": lax.rem(s + o, span)}
+        pl.semaphore_signal(barrier, inc=1, device_id=who, device_id_type=MESH)
+        return carry
+
+    lax.fori_loop(1, span, greet, 0)
+    small_own[...] = jnp.zeros(small_own.shape, F32)
+    small_own[:TAPS] = taps_own[...]
+    small_own[at_state:at_bias] = log_own[...]
+    small_own[at_bias : at_bias + 1] = cbias_own[...]
+    small_own[at_bias + 1 : at_bias + 2] = dbias_own[...]
+    small_own[at_bias + 2 : at_bias + 3] = skip_own[...]
+    small_own[at_bias + 3 : at_bias + 4, : width // 4] = gain_own[...]
+    pl.semaphore_wait(barrier, 2 + span)
+
+    SMALL, STREAM, PROJ, STEP, GATE, OUT = range(6)
+    plan = (
+        (small_own, small, 1, None),
+        (in_own, in_w, 0, (0, inner)),
+        (xp_own, xp, 0, None),
+        (dt_own, dt, 1, None),
+        (in_own, in_w, 0, (inner, 2 * inner)),
+        (out_own, out_w, 0, None),
+    )
 
     def window(p, owner, half, q):
-        k, dim, cols = plan[p]
-        rows = srcs[k].shape[0]
-        part = rows // 4
+        src, dst, dim, cols = plan[p]
+        high, wide = src.shape
+        part = high // 4
         at = (half * 2 + q) * part
-        c = cols or (0, srcs[k].shape[1])
+        lo, hi = cols or (0, wide)
         if dim == 0:
-            return dsts[k].at[pl.ds(pl.multiple_of(owner * rows + at, part), part), c[0]:c[1]]
-        w = c[1] - c[0]
-        return dsts[k].at[pl.ds(pl.multiple_of(at, part), part), pl.ds(pl.multiple_of(owner * w, w), w)]
+            return dst.at[pl.ds(pl.multiple_of(owner * high + at, part), part), lo:hi]
+        col = pl.ds(pl.multiple_of(owner * wide, wide), wide)
+        return dst.at[pl.ds(pl.multiple_of(at, part), part), col]
 
     def own(p, half, q):
-        k, dim, cols = plan[p]
-        part = srcs[k].shape[0] // 4
-        c = cols or (0, srcs[k].shape[1])
-        return srcs[k].at[pl.ds(pl.multiple_of((half * 2 + q) * part, part), part), c[0]:c[1]]
+        src, _, _, cols = plan[p]
+        high, wide = src.shape
+        part = high // 4
+        lo, hi = cols or (0, wide)
+        return src.at[pl.ds(pl.multiple_of((half * 2 + q) * part, part), part), lo:hi]
 
     def copy(src, dst, p, kind, who):
-        return pltpu.make_async_remote_copy(src_ref=src, dst_ref=dst, send_sem=send.at[p, kind], recv_sem=recv.at[p, kind], device_id=who, device_id_type=MESH)
-
-    locals_ = []
+        return pltpu.make_async_remote_copy(
+            src_ref=src, dst_ref=dst, send_sem=send.at[p, kind], recv_sem=recv.at[p, kind],
+            device_id=who, device_id_type=MESH,
+        )
+
     started = []
-    for p in range(len(plan)):
+
+    def go(one):
+        one.start()
+        started.append(one)
+
+    def start_own(p):
         for q in (0, 1):
-            a = copy(own(p, d, q), window(p, f, d, q), p, q, tox); a.start()
-            b = copy(own(p, d, 1 - q), window(p, f, d, 1 - q), p, 3 - q, toy); b.start()
-            started += [a, b]
-    for p in range(len(plan)):
+            go(copy(own(p, d, q), window(p, f, d, q), p, q, tox))
+            go(copy(own(p, d, 1 - q), window(p, f, d, 1 - q), p, 3 - q, toy))
+
+    def place_own(p):
         for half in (0, 1):
             for q in (0, 1):
-                c = pltpu.make_async_copy(own(p, half, q), window(p, f, half, q), local.at[p, half * 2 + q]); c.start(); locals_.append(c)
+                pltpu.make_async_copy(
+                    own(p, half, q), window(p, f, half, q), local.at[p, half * 2 + q]
+                ).start()
+
+    def own_ready(p):
+        for half in (0, 1):
+            for q in (0, 1):
+                pltpu.make_async_copy(
+                    own(p, half, q), window(p, f, half, q), local.at[p, half * 2 + q]
+                ).wait()
+
     def arrived(p, kind, owner, half, q):
         w = window(p, owner, half, q)
         copy(w, w, p, kind, sib).wait_recv()
         return w
-    for p in range(len(plan)):
-        for kind, owner, q in ((0, fx, 0), (3, fy, 1), (1, fx, 1), (2, fy, 0)):
+
+    near = ((0, fx, 0), (3, fy, 1), (1, fx, 1), (2, fy, 0))
+    diagonal = ((4, fd, 0), (5, fd, 1))
+
+    def serve_near(p):
+        for kind, owner, q in near:
             w = arrived(p, kind, owner, d, q)
             if kind == 0:
-                c = copy(w, w, p, 4, toy); c.start(); started.append(c)
+                go(copy(w, w, p, 4, toy))
             if kind == 3:
-                c = copy(w, w, p, 5, tox); c.start(); started.append(c)
-            c = copy(w, w, p, 6 + kind, sib); c.start(); started.append(c)
-    for p in range(len(plan)):
-        for kind, q in ((4, 0), (5, 1)):
-            w = arrived(p, kind, fd, d, q)
-            c = copy(w, w, p, 6 + kind, sib); c.start(); started.append(c)
-    for p in range(len(plan)):
-        for kind, owner, q in ((0, fx, 0), (3, fy, 1), (1, fx, 1), (2, fy, 0), (4, fd, 0), (5, fd, 1)):
+                go(copy(w, w, p, 5, tox))
+            go(copy(w, w, p, 6 + kind, sib))
+
+    def serve_far(p):
+        for kind, owner, q in diagonal:
+            w = arrived(p, kind, owner, d, q)
+            go(copy(w, w, p, 6 + kind, sib))
+
+    def near_ready(p):
+        for kind, owner, q in near:
             arrived(p, 6 + kind, owner, 1 - d, q)
-    for c in started: c.wait_send()
-    for c in locals_: c.wait()
-
-def gather(in_w, out_w, xp, dt, small):
-    ops = (in_w, out_w, xp, dt, small)
-    dims = (0, 0, 0, 1, 1)
-    half = in_w.shape[1] // 2
-    plan = ((0, 0, (0, half)), (2, 0, None), (3, 1, None), (4, 1, None), (0, 0, (half, 2 * half)), (1, 0, None))
-    def full(v, dim):
-        s = list(v.shape); s[dim] *= 4
-        return jax.ShapeDtypeStruct(tuple(s), v.dtype)
-    m = len(plan)
-    return pl.pallas_call(functools.partial(gather_kernel, plan),
-        in_specs=[pl.BlockSpec(memory_space=pltpu.VMEM)] * 5,
-        out_specs=[pl.BlockSpec(memory_space=pl.ANY)] * 5,
-        out_shape=[full(v, dm) for v, dm in zip(ops, dims)],
-        scratch_shapes=[pltpu.SemaphoreType.DMA((m, 12)), pltpu.SemaphoreType.DMA((m, 12)), pltpu.SemaphoreType.DMA((m, 4))],
-        compiler_params=pltpu.CompilerParams(collective_id=0, has_side_effects=True, vmem_limit_bytes=40<<20), name="gather")(*ops)
+
+    def far_ready(p):
+        for kind, owner, q in diagonal:
+            arrived(p, 6 + kind, owner, 1 - d, q)
+
+    for p in (SMALL, STREAM, PROJ, STEP):
+        start_own(p)
+    for p in range(6):
+        place_own(p)
+    def edges(c):
+        return pltpu.make_async_remote_copy(
+            src_ref=x.at[(c + 1) * ctx - GROUP : (c + 1) * ctx], dst_ref=hx.at[c],
+            send_sem=halo.at[0, c], recv_sem=halo.at[1, c],
+            device_id={"seq": jnp.minimum(s + 1, span - 1)}, device_id_type=MESH,
+        )
+
+    @pl.when(s < span - 1)
+    def _():
+        for c in range(seqs):
+            edges(c).start()
+
+    for c in range(seqs):
+        t = s * ctx + lax.broadcasted_iota(jnp.int32, (ctx, LANES), 0)
+        mask[c * ctx : (c + 1) * ctx] = (t < lengths[c]).astype(F32)
+
+    def mask_step(r, carry):
+        tok = pl.ds(pl.multiple_of(r * GROUP, GROUP), GROUP)
+        held = jnp.concatenate([mask[tok]] * (width // LANES), 1)
+        bg[tok] = (og[tok].astype(F32) * held).astype(BF16)
+        return carry
+
+    lax.fori_loop(0, rows // GROUP, mask_step, 0)
+
+    serve_near(SMALL)
+    serve_far(SMALL)
+    near_ready(SMALL)
+    far_ready(SMALL)
+    own_ready(SMALL)
+
+    @pl.when(s > 0)
+    def _():
+        for c in range(seqs):
+            edges(c).wait_recv()
+
+    gain_at = at_bias + 3
+    gain = jnp.concatenate(
+        [small[gain_at : gain_at + 1, j * share : j * share + width // 4] for j in range(4)], 1
+    )
+
+    def normalised(v):
+        v = v.astype(F32)
+        inverse = lax.rsqrt(jnp.mean(v * v, -1, keepdims=True) + EPS)
+        return (v * inverse * gain).astype(BF16)
+
+    def norm_step(r, carry):
+        tok = pl.ds(pl.multiple_of(r * GROUP, GROUP), GROUP)
+        normed[tok] = normalised(x[tok])
+        normed_out[tok] = normed[tok]
+        return carry
+
+    lax.fori_loop(0, rows // GROUP, norm_step, 0)
+    for c in range(seqs):
+        normed[rows + c * GROUP : rows + (c + 1) * GROUP] = normalised(hx[c])
+
+    def project(total, high, first, owner, fresh):
+        shard = pl.ds(pl.multiple_of(owner * (width // 4), width // 4), width // 4)
+        left = normed[:high, shard]
+
+        def one(t, carry):
+            cols = pl.ds(pl.multiple_of(t * CHUNK, CHUNK), CHUNK)
+            right = in_w[shard, pl.ds(pl.multiple_of(first + t * CHUNK, CHUNK), CHUNK)]
+            part = dot(left, right)
+            total[:, cols] = part if fresh else total[:, cols] + part
+            return carry
+
+        lax.fori_loop(0, inner // CHUNK, one, 0)
+
+    tall = rows + seqs * GROUP
+    own_ready(STREAM)
+    project(acc, tall, 0, f, True)
+    serve_near(STREAM)
+    start_own(GATE)
+    start_own(OUT)
+    near_ready(STREAM)
+    project(acc, tall, 0, fx, False)
+    project(acc, tall, 0, fy, False)
+    serve_far(STREAM)
+    for p in (PROJ, STEP):
+        serve_near(p)
+        serve_far(p)
+    far_ready(STREAM)
+    project(acc, tall, 0, fd, False)
+
+    tile = 2 * LANES
+
+    def columns(t, size=tile):
+        return pl.ds(pl.multiple_of(t * size, size), size)
+
+    def conv_step(t, carry):
+        cols = columns(t)
+        for c in range(seqs):
+            before = acc[rows + c * GROUP : rows + (c + 1) * GROUP, cols].astype(BF16)
+            stream = acc[c * ctx : (c + 1) * ctx, cols].astype(BF16)
+            lead[c, :GROUP, cols] = before
+            lead[c, GROUP:, cols] = stream
+            held = jnp.concatenate([before, stream], 0).astype(F32)
+            total = small[at_bias : at_bias + 1, cols]
+            for k in range(TAPS):
+                at = GROUP - TAPS + 1 + k
+                total = total + small[k : k + 1, cols] * held[at : at + ctx]
+            conv[c * ctx : (c + 1) * ctx, cols] = total
+            u[c * ctx : (c + 1) * ctx, cols] = (total * jax.nn.sigmoid(total)).astype(BF16)
+        return carry
+
+    lax.fori_loop(0, inner // tile, conv_step, 0)
+    for p in (PROJ, STEP):
+        near_ready(p)
+        far_ready(p)
+        own_ready(p)
+    proj[...] = dot(u[...], xp[...])
+    step_low[...] = proj[:, :rank].astype(BF16)
+
+    def wide_step(i, carry):
+        tok = pl.ds(pl.multiple_of(i * GROUP, GROUP), GROUP)
+        held = proj[tok]
+        for ref, first in ((bw, rank), (cw, rank + state)):
+            value = held[:, first : first + state]
+            c, at = i // groups, lax.rem(i, groups)
+            ref[c, pl.ds(pl.multiple_of(at * GROUP, GROUP), GROUP)] = jnp.broadcast_to(
+                value[:, :, None], (GROUP, state, LANES)
+            )
+        return carry
+
+    lax.fori_loop(0, rows // GROUP, wide_step, 0)
+    r = lax.broadcasted_iota(jnp.int32, (rows, GROUP * state), 0)
+    k = lax.broadcasted_iota(jnp.int32, (rows, GROUP * state), 1)
+    mine = lax.rem(r, GROUP) == k // state
+    at = lax.broadcasted_iota(jnp.int32, (proj.shape[1], GROUP * state), 0)
+    col = lax.rem(lax.broadcasted_iota(jnp.int32, (proj.shape[1], GROUP * state), 1), state)
+    for ref, first in ((bbd, rank), (cbd, rank + state)):
+        spread = (at == col + first).astype(F32).astype(BF16)
+        ref[...] = jnp.where(mine, dot(proj[...].astype(BF16), spread), 0.0).astype(BF16)
+
+    def delta_step(t, carry):
+        cols = columns(t)
+        for c in range(seqs):
+            tok = slice(c * ctx, (c + 1) * ctx)
+            value = dot(step_low[tok], dt[:, cols]) + small[at_bias + 1 : at_bias + 2, cols]
+            raw[tok, cols] = value
+            value = jnp.maximum(value, 0.0) + jnp.log1p(jnp.exp(-jnp.abs(value)))
+            for i in range(groups):
+                delta[c * groups + i, :, cols] = value[i * GROUP : (i + 1) * GROUP]
+            sums[c : c + 1, cols] = jnp.sum(value, 0, keepdims=True)
+            value = value * u[tok, cols].astype(F32)
+            for i in range(groups):
+                v[c * groups + i, :, cols] = value[i * GROUP : (i + 1) * GROUP]
+        return carry
+
+    sums[...] = jnp.zeros(sums.shape, F32)
+    lax.fori_loop(0, inner // tile, delta_step, 0)
+
+    def sums_copy(j):
+        return pltpu.make_async_remote_copy(
+            src_ref=sums, dst_ref=sums_in.at[s], send_sem=sums_send.at[j],
+            recv_sem=sums_recv.at[s], device_id={"seq": j}, device_id_type=MESH,
+        )
+
+    def sums_start(o, carry):
+        sums_copy(lax.rem(s + o, span)).start()
+        return carry
+
+    lax.fori_loop(1, span, sums_start, 0)
+
+    def ends_copy(j, way, c):
+        return pltpu.make_async_remote_copy(
+            src_ref=ends.at[way, c], dst_ref=ends_in.at[s, c], send_sem=relay_send.at[j, c],
+            recv_sem=relay_recv.at[s, c], device_id={"seq": j}, device_id_type=MESH,
+        )
+
+    def ends_start(first, count, way, c):
+        def one(j, carry):
+            ends_copy(j, way, c).start()
+            return carry
+
+        lax.fori_loop(first, count, one, 0)
+
+    def forward_ends(c):
+        for j in range(0, inner, CHUNK):
+            cuts = [slice(j + i, j + i + LANES) for i in range(0, CHUNK, LANES)]
+            rates = [-jnp.exp(small[at_state:at_bias, cut]) * LOG2E for cut in cuts]
+
+            def one(i, h):
+                h = list(h)
+                for k in range(GROUP):
+                    b = bw[c, i * GROUP + k]
+                    for n, cut in enumerate(cuts):
+                        step = delta[c * groups + i, k : k + 1, cut]
+                        factor = jnp.exp2(jnp.broadcast_to(step, (state, LANES)) * rates[n])
+                        row = jnp.broadcast_to(v[c * groups + i, k : k + 1, cut], (state, LANES))
+                        h[n] = factor * h[n] + row * b
+                return tuple(h)
+
+            zero = tuple(jnp.zeros((state, LANES), F32) for _ in cuts)
+            h = lax.fori_loop(0, groups, one, zero)
+            for n, cut in enumerate(cuts):
+                ends[0, c, :, cut] = h[n].astype(BF16)
+
+    def backward_ends(c):
+        for j in range(0, inner, CHUNK):
+            cuts = [slice(j + i, j + i + LANES) for i in range(0, CHUNK, LANES)]
+            rates = [-jnp.exp(small[at_state:at_bias, cut]) * LOG2E for cut in cuts]
+
+            def one(i, carry):
+                run, p = (list(value) for value in carry)
+                for k in range(GROUP):
+                    read = cw[c, i * GROUP + k]
+                    for n, cut in enumerate(cuts):
+                        step = delta[c * groups + i, k : k + 1, cut]
+                        factor = jnp.exp2(jnp.broadcast_to(step, (state, LANES)) * rates[n])
+                        row = dy[c * groups + i, k : k + 1, cut]
+                        run[n] = run[n] * factor
+                        p[n] = p[n] + run[n] * (read * jnp.broadcast_to(row, (state, LANES)))
+                return tuple(run), tuple(p)
+
+            one_s = tuple(jnp.ones((state, LANES), F32) for _ in cuts)
+            zero = tuple(jnp.zeros((state, LANES), F32) for _ in cuts)
+            _, p = lax.fori_loop(0, groups, one, (one_s, zero))
+            for n, cut in enumerate(cuts):
+                ends[1, c, :, cut] = p[n].astype(BF16)
+
+    forward_ends(0)
+    ends_start(s + 1, span, 0, 0)
+    serve_near(GATE)
+    own_ready(GATE)
+    project(zacc, rows, inner, f, True)
+    forward_ends(1)
+    ends_start(s + 1, span, 0, 1)
+    near_ready(GATE)
+    project(zacc, rows, inner, fx, False)
+    project(zacc, rows, inner, fy, False)
+
+    def grad_part(owner):
+        shard = pl.ds(pl.multiple_of(owner * share, share), share)
+        gg[:, shard] = dot(bg[...], out_w[shard], across)
+
+    own_ready(OUT)
+    grad_part(f)
+    serve_near(OUT)
+    serve_far(GATE)
+    far_ready(GATE)
+    project(zacc, rows, inner, fd, False)
+    near_ready(OUT)
+    grad_part(fx)
+    grad_part(fy)
+    serve_far(OUT)
+    far_ready(OUT)
+    grad_part(fd)
+
+    fulls = ((in_w, in_full), (out_w, out_full), (xp, xp_full), (dt, dt_full), (small, small_full))
+    kept = [pltpu.make_async_copy(a, b, keep.at[n]) for n, (a, b) in enumerate(fulls)]
+    for one in kept:
+        one.start()
+
+    def gate_step(t, carry):
+        cols = columns(t)
+        for c in range(seqs):
+            tok = slice(c * ctx, (c + 1) * ctx)
+            low = zacc[tok, cols].astype(BF16)
+            gate[tok, cols] = low
+            value = low.astype(F32)
+            value = gg[tok, cols] * (value * jax.nn.sigmoid(value))
+            for i in range(groups):
+                dy[c * groups + i, :, cols] = value[i * GROUP : (i + 1) * GROUP]
+        return carry
+
+    lax.fori_loop(0, inner // tile, gate_step, 0)
+    for c in range(seqs):
+        backward_ends(c)
+        ends_start(0, s, 1, c)
+
+    def sums_wait(o, carry):
+        j = lax.rem(s + o, span)
+        pltpu.make_async_remote_copy(
+            src_ref=sums, dst_ref=sums_in.at[j], send_sem=sums_send.at[j],
+            recv_sem=sums_recv.at[j], device_id={"seq": j}, device_id_type=MESH,
+        ).wait_recv()
+        return carry
+
+    lax.fori_loop(1, span, sums_wait, 0)
+
+    def ends_wait(j, c):
+        pltpu.make_async_remote_copy(
+            src_ref=ends.at[0, c], dst_ref=ends_in.at[j, c], send_sem=relay_send.at[j, c],
+            recv_sem=relay_recv.at[j, c], device_id={"seq": j}, device_id_type=MESH,
+        ).wait_recv()
+
+    start[...] = jnp.zeros(start.shape, F32)
+    final[...] = jnp.zeros(final.shape, F32)
+
+    def join(ref, j, c):
+        ends_wait(j, c)
+
+        def one(t, carry):
+            cols = columns(t, CHUNK)
+            rates = -jnp.exp(small[at_state:at_bias, cols]) * LOG2E
+            decay = jnp.exp2(sums_in[j, c : c + 1, cols] * rates)
+            ref[c, :, cols] = decay * ref[c, :, cols] + ends_in[j, c, :, cols].astype(F32)
+            return carry
+
+        lax.fori_loop(0, inner // CHUNK, one, 0)
+
+    def join_start(j, carry):
+        for c in range(seqs):
+            join(start, j, c)
+        return carry
+
+    def join_final(o, carry):
+        for c in range(seqs):
+            join(final, span - 1 - o, c)
+        return carry
+
+    lax.fori_loop(0, s, join_start, 0)
+    lax.fori_loop(0, span - 1 - s, join_final, 0)
+
+    for one in started:
+        one.wait_send()
+
+    @pl.when(s < span - 1)
+    def _():
+        for c in range(seqs):
+            edges(c).wait_send()
+
+    def sent(o, carry):
+        j = lax.rem(s + o, span)
+        sums_copy(j).wait_send()
+        for c in range(seqs):
+            ends_copy(j, 0, c).wait_send()
+        return carry
+
+    lax.fori_loop(1, span, sent, 0)
+    for one in kept:
+        one.wait()
+
+
+def front(x, og, lengths, taps, logs, cbias, dbias, skip, gain, in_own, out_own, xp_own, dt_own, seqs):
+    rows, width = x.shape
+    share, inner = taps.shape[1], 4 * taps.shape[1]
+    state, rank, used = logs.shape[0], dt_own.shape[0], xp_own.shape[1]
+    ctx = rows // seqs
+    span = lax.axis_size("seq")
+    vmem, dma = pltpu.VMEM, pltpu.SemaphoreType.DMA
+    whole, anywhere = pl.BlockSpec(memory_space=vmem), pl.BlockSpec(memory_space=pl.ANY)
+    shape = jax.ShapeDtypeStruct
+    return pl.pallas_call(
+        functools.partial(front_kernel, span),
+        in_specs=[whole, whole, pl.BlockSpec(memory_space=pltpu.SMEM)]
+        + [whole] * 6
+        + [anywhere] * 4,
+        out_specs=[whole] * 18 + [anywhere] * 5,
+        out_shape=[
+            shape((rows, width), BF16),
+            shape((rows, width), BF16),
+            shape((rows, LANES), F32),
+            shape((seqs, ctx + GROUP, inner), BF16),
+            shape((rows, inner), F32),
+            shape((rows, inner), BF16),
+            shape((rows, inner), BF16),
+            shape((rows, inner), F32),
+            shape((rows // GROUP, GROUP, inner), F32),
+            shape((seqs, ctx, state, LANES), F32),
+            shape((seqs, ctx, state, LANES), F32),
+            shape((rows, GROUP * state), BF16),
+            shape((rows, GROUP * state), BF16),
+            shape((rows, inner), F32),
+            shape((rows // GROUP, GROUP, inner), F32),
+            shape((rows, rank), BF16),
+            shape((seqs, state, inner), F32),
+            shape((seqs, state, inner), F32),
+            shape((width, 2 * inner), BF16),
+            shape((inner, width), BF16),
+            shape((inner, used), BF16),
+            shape((rank, inner), BF16),
+            shape((32, inner), F32),
+        ],
+        scratch_shapes=[
+            vmem((width, 2 * inner), BF16),
+            vmem((inner, width), BF16),
+            vmem((inner, used), BF16),
+            vmem((rank, inner), BF16),
+            vmem((32, inner), F32),
+            vmem((32, share), F32),
+            vmem((seqs, GROUP, width), BF16),
+            vmem((rows + seqs * GROUP, inner), F32),
+            vmem((rows, inner), F32),
+            vmem((rows + seqs * GROUP, width), BF16),
+            vmem((rows // GROUP, GROUP, inner), F32),
+            vmem((rows, used), F32),
+            vmem((2, seqs, state, inner), BF16),
+            vmem((8, inner), F32),
+            vmem((span, seqs, state, inner), BF16),
+            vmem((span, 8, inner), F32),
+            dma((6, 12)),
+            dma((6, 12)),
+            dma((2, seqs)),
+            dma((span, seqs)),
+            dma((span, seqs)),
+            dma((span,)),
+            dma((span,)),
+            dma((6, 4)),
+            dma((5,)),
+        ],
+        compiler_params=pltpu.CompilerParams(
+            collective_id=0, has_side_effects=True, vmem_limit_bytes=63 << 20
+        ),
+        name="front",
+    )(x, og, lengths, taps, logs, cbias, dbias, skip, gain, in_own, out_own, xp_own, dt_own)
 
 
 def back_kernel(
@@ -657,13 +1085,6 @@
     )(*args)
 
 
-def block_diagonal(v):
-    seqs, ctx, state = v.shape
-    eye = jnp.eye(GROUP, dtype=F32)[None, None, :, :, None]
-    spread = v.reshape(seqs, ctx // GROUP, GROUP, 1, state) * eye
-    return spread.reshape(seqs, ctx // GROUP, GROUP, GROUP * state).astype(BF16)
-
-
 def local_specs(seqs, ctx, inner, state, width):
     groups = ctx // GROUP
     tok = pl.BlockSpec((1, groups, GROUP, width), lambda c, j: (c, 0, 0, j))
@@ -674,29 +1095,13 @@
     return tok, wide, rate, end, diag
 
 
-def local_ends(delta, drive, dy, b_wide, c_wide, rates):
-    seqs, groups, _, inner = delta.shape
-    state = rates.shape[0]
-    width = 512
-    tok, wide, rate, end, _ = local_specs(seqs, groups * GROUP, inner, state, width)
-    return pl.pallas_call(
-        ends_kernel,
-        grid=(seqs, inner // width),
-        in_specs=[tok, tok, tok, wide, wide, rate],
-        out_specs=[end, end],
-        out_shape=[jax.ShapeDtypeStruct((seqs, state, inner), F32)] * 2,
-        compiler_params=pltpu.CompilerParams(vmem_limit_bytes=56 << 20),
-        name="ends",
-    )(delta, drive, dy, b_wide, c_wide, rates)
-
-
-def sweep(delta, u, dy, gated_grad, gate_in, raw, b_in, c_in, b_wide, c_wide, small, start, final):
+def sweep(delta, u, dy, gated_grad, gate_in, raw, b_wide, c_wide, bbd, cbd, small, start, final):
     seqs, groups, _, inner = delta.shape
     ctx = groups * GROUP
-    state = b_in.shape[2]
+    state = b_wide.shape[2]
     width = CHUNK
     tok, wide, _, end, diag = local_specs(seqs, ctx, inner, state, width)
-    ones = block_diagonal(jnp.ones((1, GROUP, state), F32))[0, 0]
+    ones = jnp.asarray(np.kron(np.eye(GROUP), np.ones((1, state))), BF16)
     token = lambda t: jax.ShapeDtypeStruct(delta.shape, t)
     diag_shape = jax.ShapeDtypeStruct((seqs, groups, GROUP, GROUP * state), F32)
     chunked = pl.BlockSpec((1, 1, groups, GROUP, width), lambda c, j: (j, c, 0, 0, 0))
@@ -726,7 +1131,7 @@
         name="sweep",
     )(
         delta, u, dy, gated_grad, gate_in, raw, b_wide, c_wide, small, start, final,
-        block_diagonal(c_in), block_diagonal(b_in), ones,
+        cbd.reshape(diag_shape.shape), bbd.reshape(diag_shape.shape), ones,
     )
 
 
@@ -738,91 +1143,26 @@
     taps, share = conv_weight.shape
     state = a_log.shape[0]
     rank = dt_weight.shape[0]
-    reach = taps - 1
     rows = ctx * seqs
-    groups = ctx // GROUP
-    small = jnp.concatenate(
-        [conv_weight, a_log, conv_bias[None], dt_bias[None], skip_gain[None]]
-        + [jnp.pad(norm_gain, (0, share - norm_gain.shape[0]))[None]],
-        0,
+    row = lambda v: v.reshape(1, -1)
+    x, og = hidden_in.reshape(rows, width), out_grad.reshape(rows, width)
+    (
+        normed, branch_grad, mask, lead, conv_out, u, gate_in, raw, delta, b_wide, c_wide, bbd, cbd,
+        gated_grad, y_grad, step_low, start, final,
+        in_matrix, out_matrix, proj_matrix, step_matrix, small,
+    ) = front(
+        x, og, lengths, conv_weight, a_log, row(conv_bias), row(dt_bias), row(skip_gain),
+        row(norm_gain), in_weight, out_weight, xproj_weight, dt_weight, seqs,
     )
-    used = small.shape[0]
-    small = jnp.pad(small, ((0, -used % 32), (0, 0)))
-    in_matrix, out_matrix, proj_matrix, step_matrix, small = gather(
-        in_weight, out_weight, xproj_weight, dt_weight, small
-    )
-    gain = small[used - 1].reshape(-1, share)[:, : norm_gain.shape[0]].reshape(-1)
-    conv_taps, log_rate = small[:taps], small[taps : taps + state]
-    conv_shift, step_bias, skip = (small[taps + state + i] for i in range(3))
-    inner = proj_matrix.shape[0]
-    dot = lambda a, b: jnp.dot(a, b, preferred_element_type=F32)
-
-    x_tok = hidden_in.astype(F32)
-    position = lax.axis_index("seq") * ctx + jnp.arange(ctx, dtype=jnp.int32)
-    mask = (position[None, :] < lengths[:, None]).astype(F32)[:, :, None]
-
-    def normalised(x):
-        inverse = lax.rsqrt(jnp.mean(x * x, -1, keepdims=True) + EPS)
-        return inverse, (x * inverse * gain).astype(BF16)
-
-    inverse, normed = normalised(x_tok)
-    normed = normed.reshape(rows, width)
-    mixed = dot(normed, in_matrix).astype(BF16)
-    stream = mixed[:, :inner].reshape(seqs, ctx, inner)
-    gate_in = mixed[:, inner:].astype(F32).reshape(seqs, ctx, inner)
-    before = passed_along(stream[:, ctx - reach :], "seq", 1)
-    extended = jnp.concatenate([before, stream], 1).astype(F32)
-    conv_out = conv_shift + sum(conv_taps[k] * extended[:, k : k + ctx] for k in range(taps))
-    u_low = jax.nn.silu(conv_out).astype(BF16)
-    u_rows = u_low.reshape(rows, inner)
-    proj = dot(u_rows, proj_matrix)
-    step_low = proj[:, :rank].astype(BF16)
-    b_in = proj[:, rank : rank + state].reshape(seqs, ctx, state)
-    c_in = proj[:, rank + state :].reshape(seqs, ctx, state)
-    raw = dot(step_low, step_matrix).reshape(seqs, ctx, inner) + step_bias
-    delta = jax.nn.softplus(raw)
-    rates = -jnp.exp(log_rate)
-    rates2 = rates * LOG2E
-    u_float = u_low.astype(F32)
-    drive = delta * u_float
-
-    cotangent = out_grad.astype(F32)
-    branch_grad = (cotangent * mask).astype(BF16).reshape(rows, width)
-    gated_grad = lax.dot_general(
-        branch_grad, out_matrix, (((1,), (1,)), ((), ())), preferred_element_type=F32
-    ).reshape(seqs, ctx, inner)
-    gate_act = jax.nn.silu(gate_in)
-    y_grad = gated_grad * gate_act
-
-    grouped = lambda v: v.reshape(seqs, groups, GROUP, inner)
-    b_wide = jnp.broadcast_to(b_in[..., None], (seqs, ctx, state, LANES))
-    c_wide = jnp.broadcast_to(c_in[..., None], (seqs, ctx, state, LANES))
-    scan_args = (grouped(delta), grouped(drive), grouped(y_grad))
-    local_end, local_back = local_ends(*scan_args, b_wide, c_wide, rates2)
-
-    blocks = lax.axis_size("seq")
-    me = lax.axis_index("seq")
-    ends = lax.all_gather(jnp.stack([local_end, local_back]).astype(BF16), "seq")
-    sums = lax.all_gather(jnp.sum(delta, 1), "seq")
-    start = jnp.zeros((seqs, state, inner), F32)
-    final = jnp.zeros((seqs, state, inner), F32)
-    for k in range(blocks):
-        decay = jnp.exp2(sums[k][:, None, :] * rates2)
-        start = jnp.where(k < me, decay * start + ends[k, 0].astype(F32), start)
-        r = blocks - 1 - k
-        decay = jnp.exp2(sums[r][:, None, :] * rates2)
-        final = jnp.where(r > me, decay * final + ends[r, 1].astype(F32), final)
-
+    grouped = lambda v: v.reshape(seqs, ctx // GROUP, GROUP, v.shape[-1])
     gated, z_grad, u_grad, raw_low, c_acc, b_acc, rate_grad, sums = sweep(
-        grouped(delta), grouped(u_low), grouped(y_grad), grouped(gated_grad),
-        grouped(mixed[:, inner:]), grouped(raw), b_in, c_in, b_wide, c_wide, small, start, final,
+        *map(grouped, (delta, u, y_grad, gated_grad, gate_in, raw)),
+        b_wide, c_wide, bbd, cbd, small, start, final,
     )
     flat = lambda v: v.reshape(rows, -1)
-    lead = jnp.concatenate([jnp.zeros((seqs, GROUP - reach, inner), BF16), before, stream], 1)
     hidden_out, input_grad, out_sum, in_sum, rest = back(
-        flat(gated), z_grad.reshape(-1, rows, CHUNK), flat(u_grad), flat(raw_low), u_rows,
-        flat(conv_out), lead, step_low, flat(c_acc), flat(b_acc), normed, flat(hidden_in),
-        flat(out_grad), branch_grad, jnp.broadcast_to(mask, (seqs, ctx, LANES)).reshape(rows, LANES),
+        flat(gated), z_grad.reshape(-1, rows, CHUNK), flat(u_grad), flat(raw_low), u, conv_out,
+        lead, step_low, flat(c_acc), flat(b_acc), normed, x, og, branch_grad, mask,
         in_matrix, out_matrix, proj_matrix, step_matrix, small, rate_grad, sums,
     )
     rest = rest.astype(F32)

time: 343 us -> 289 us (0.84)
  Pallas kernels: 236 us -> 272 us
  other arithmetic: 25.4 us -> 5.22 us
  local copies, waits for them, and re-layouts: 29.6 us -> 10.8 us
  matrix products: 15.6 us -> 0 us
  between operations: 14.4 us -> 0.69 us
  blocking collectives: 11 us -> 0 us
  waiting for transfers between devices: 8.13 us -> 0 us
    pallas_call x2 -> x1, Pallas kernels: 75.8 us -> 111 us  [front(): pl.pallas_call(functools.partial(front_kernel, span), in_specs=[whole, wh...]
    dot_general x4 -> x0, matrix products: 15.6 us -> none  [the longest x3 9.76 us: body(): dot = lambda a, b: jnp.dot(a, b, preferred_element_type=F32)]
    all_gather x1 -> x0, blocking collectives: 11 us -> none  [body(): sums = lax.all_gather(jnp.sum(delta, 1), 'seq')]
    all_gather x1 -> x0, waiting for transfers between devices: 8.11 us -> none  [body(): lax.all_gather(jnp.stack([local_end, local_back]).astype(BF16), 'seq')]
    convert_element_type x9 -> x0, other arithmetic: 7.36 us -> none  [the longest x1 2.64 us: body(): u_low = jax.nn.silu(conv_out).astype(BF16)]
    select_n x3 -> x0, other arithmetic: 7.25 us -> none  [the longest x1 3.09 us: body(): delta = jax.nn.softplus(raw)]
    unnamed x53 -> x11, local copies, waits for them, and re-layouts: 10.5 us -> 3.25 us
    broadcast_in_dim x6 -> x0, local copies, waits for them, and re-layouts: 4.84 us -> none  [the longest x2 2.06 us: body(): b_wide = jnp.broadcast_to(b_in[..., None], (seqs, ctx, state, LANES))]
  transfers between devices with their start and end apart: 2 -> 0, of which waited for: 1 -> 0; matrix products, arithmetic and copies ran while one was open for 5% -> 0% of each run, Pallas kernels for 0% -> 0%
where the time goes in v3:
time: 289 us
  Pallas kernels  272 us (94%)
  local copies, waits for them, and re-layouts  10.8 us (4%)
  other arithmetic  5.22 us (2%)
    pallas_call x1, Pallas kernels, front(): pl.pallas_call(functools.partial(front_kernel, span), in_specs=[whole, wh...  111 us
    pallas_call x1, Pallas kernels, back(): pl.pallas_call(functools.partial(back_kernel, span, state, rank), in_spec...  102 us
    pallas_call x1, Pallas kernels, sweep(): pl.pallas_call(sweep_kernel, grid=(seqs, inner // width), in_specs=[tok]...  59.3 us

profile of v3, /device:TPU:25, one launch (start us, length us, event | category | flops | bytes accessed | tf_op | source)
XLA Modules:
  0.0 288.8 jit_solution(11175601111563714288)
XLA Ops:
  0.6 1.7 copy.26.xp_own
  2.3 111.0 %front.1 = (bf16[256,1024]{1,0:T(8,128)(2,1)}, bf16[256,1024]{1,0:T(8,128)(2,1)}, f32[256,128]{1,0:T(8,128)}, bf16[2,144,2048]{2,1,0:T(8,128)(2,1)}, f32[256,204...) custom-call(bf16[256,1024]{1,0:T(8,128)(2,1)} %bitcast.34, ...), custom_call_target="tpu_custom_call" | custom-call | tf_op jit(solution)/shard_map/front/pallas_call | solution.py:599
  113.3 59.3 %sweep.1 = (bf16[2,8,16,2048]{3,2,1,0:T(8,128)(2,1)}, bf16[4,2,8,16,512]{4,3,2,1,0:T(8,128)(2,1)}, f32[2,8,16,2048]{3,2,1,0:T(8,128)}, bf16[2,8,16,2048]{3,2,1,0...) custom-call(f32[2,8,16,2048]{3,2,1,0:T(8,128)} %bitcast.31, ...), custom_call_target="tpu_custom_call" | custom-call | tf_op jit(solution)/shard_map/sweep/pallas_call | solution.py:1110
  172.6 101.8 %back.1 = (bf16[256,1024]{1,0:T(8,128)(2,1)}, bf16[256,1024]{1,0:T(8,128)(2,1)}, bf16[512,1024]{1,0:T(8,128)(2,1)}, bf16[256,4096]{1,0:T(8,128)(2,1)}, bf16[256,512]{1,0:T(8,128)(2,1)}) custom-call(bf16[256,2048]{1,0:T(8,128)(2,1)} %bitcast.38, bf16[4,256,512]{2,1,0:T(8,128)(2,1)} %bitcast.39, f32[256,2048]{1,0:T(8,128)} %bitcast.29, ...), custom_call_target="tpu_custom_call" | custom-call | tf_op jit(solution)/shard_map/back/pallas_call | solution.py:1052
  274.4 0.0 copy-start.1
  274.4 1.3 slice.32
  275.7 1.4 fusion
  277.1 1.3 slice.33
  278.4 1.4 slice.38
  279.8 1.5 slice.36
  281.3 0.0 copy-start
  281.3 1.1 convert_element_type.9
  282.5 0.7 slice_bitcast_fusion
  283.1 0.0 copy-done.1
  283.1 1.6 convert_element_type.11
  284.7 0.0 copy-done
  284.7 0.0 copy-start.3
  284.7 0.0 copy-start.2
  284.7 2.5 convert_element_type.10
  287.2 0.0 copy-done.3
  287.2 0.8 copy.29
  288.0 0.0 copy-done.2
  288.0 0.8 copy.30
Async XLA Ops:
  274.4 8.8 %copy-start.1 = (bf16[512,1024]{1,0:T(8,128)(2,1)S(1)}, bf16[512,1024]{1,0:T(8,128)(2,1)}, u32[]{:S(2)}) copy-start(bf16[512,1024]{1,0:T(8,128)(2,1)} %get-tuple-element.83) | copy-start | bytes 3145732
  281.3 3.4 %copy-start = (bf16[256,4096]{1,0:T(8,128)(2,1)S(1)}, bf16[256,4096]{1,0:T(8,128)(2,1)}, u32[]{:S(2)}) copy-start(bf16[256,4096]{1,0:T(8,128)(2,1)} %get-tuple-element.82) | copy-start | bytes 6291460
  284.7 2.5 copy-start.3
  284.7 3.3 %copy-start.2 = (bf16[256,1024]{1,0:T(8,128)(2,1)S(1)}, bf16[256,1024]{1,0:T(8,128)(2,1)}, u32[]{:S(2)}) copy-start(bf16[256,1024]{1,0:T(8,128)(2,1)} %get-tuple-element.80) | copy-start | bytes 1572868

commit v4 on v3

--- a/solution.py
+++ b/solution.py
@@ -27,100 +27,17 @@
     return v * s, s * (1.0 + v * (1.0 - s))
 
 
-def sweep_kernel(
-    d_ref, u_ref, dy_ref, gg_ref, z_ref, raw_ref, b_ref, c_ref, small_ref, h0_ref, p0_ref,
-    cbd_ref, bbd_ref, one_ref,
-    gated_ref, zg_ref, ug_ref, rl_ref, cacc_ref, bacc_ref, racc_ref, sums_ref,
-    v_s, y_s, h_s, a_s, g_s, w_s,
-):
-    groups, width = d_ref.shape[1], d_ref.shape[3]
-    state = b_ref.shape[2]
-    cuts = [slice(j, j + LANES) for j in range(0, width, LANES)]
-    all_rates = -jnp.exp(small_ref[TAPS : TAPS + state]) * LOG2E
-    rates = [all_rates[:, s] for s in cuts]
-    skip = small_ref[TAPS + state + 2 : TAPS + state + 3]
-    across = (((1,), (1,)), ((), ()))
-
-    @pl.when(pl.program_id(1) == 0)
-    def _():
-        cacc_ref[...] = jnp.zeros_like(cacc_ref)
-        bacc_ref[...] = jnp.zeros_like(bacc_ref)
-
-    h_s[0] = h0_ref[0]
-
-    def forward(i, h):
-        h = list(h)
-        u = u_ref[0, i].astype(F32)
-        v_s[i] = d_ref[0, i] * u
-        for k in range(GROUP):
-            t = i * GROUP + k
-            b = b_ref[0, t]
-            for j, s in enumerate(cuts):
-                factor = jnp.exp2(jnp.broadcast_to(d_ref[0, i, k : k + 1, s], (state, LANES)) * rates[j])
-                h[j] = factor * h[j] + jnp.broadcast_to(v_s[i, k : k + 1, s], (state, LANES)) * b
-                h_s[t + 1, :, s] = h[j]
-                a_s[t, :, s] = factor
-        held = h_s[pl.ds(i * GROUP + 1, GROUP)].reshape(GROUP * state, width).astype(BF16)
-        y = jnp.dot(cbd_ref[0, i], held, preferred_element_type=F32) + skip * u
-        cacc_ref[0, i] += lax.dot_general(
-            dy_ref[0, i].astype(BF16), held, across, preferred_element_type=F32
-        )
-        gate, slope = silu_parts(z_ref[0, i].astype(F32))
-        gated_ref[0, i] = (y * gate).astype(BF16)
-        zg_ref[0, 0, i] = (gg_ref[0, i] * y * slope).astype(BF16)
-        return tuple(h)
-
-    lax.fori_loop(0, groups, forward, tuple(h0_ref[0, :, s] for s in cuts))
-
-    def backward(turn, carry):
-        i = groups - 1 - turn
-        p, total, sums = (list(v) for v in carry)
-        for k in reversed(range(GROUP)):
-            t = i * GROUP + k
-            c = c_ref[0, t]
-            for j, s in enumerate(cuts):
-                row = lambda ref: jnp.broadcast_to(ref[0, i, k : k + 1, s], (state, LANES))
-                g = c * row(dy_ref) + p[j]
-                p[j] = a_s[t, :, s] * g
-                w = p[j] * h_s[t, :, s]
-                total[j] = total[j] + w * row(d_ref)
-                g_s[k, :, s] = g.astype(BF16)
-                w_s[k, :, s] = (w * rates[j]).astype(BF16)
-        g_all = g_s[...].reshape(GROUP * state, width)
-        drive_grad = jnp.dot(bbd_ref[0, i], g_all, preferred_element_type=F32)
-        delta_part = jnp.dot(
-            one_ref[...], w_s[...].reshape(GROUP * state, width), preferred_element_type=F32
-        )
-        bacc_ref[0, i] += lax.dot_general(
-            v_s[i].astype(BF16), g_all, across, preferred_element_type=F32
-        )
-        u, dy, delta = u_ref[0, i].astype(F32), dy_ref[0, i], d_ref[0, i]
-        raw_grad = (drive_grad * u + delta_part * (1.0 / LOG2E)) * jax.nn.sigmoid(raw_ref[0, i])
-        rl_ref[0, i] = raw_grad.astype(BF16)
-        ug_ref[0, i] = dy * skip + drive_grad * delta
-        sums[0] = sums[0] + (dy * u)[:8] + (dy * u)[8:]
-        sums[1] = sums[1] + raw_grad[:8] + raw_grad[8:]
-        return tuple(p), tuple(total), tuple(sums)
-
-    zero = tuple(jnp.zeros((state, LANES), F32) for _ in cuts)
-    start = tuple(p0_ref[0, :, s] for s in cuts)
-    none = jnp.zeros((8, width), F32)
-    _, total, sums = lax.fori_loop(0, groups, backward, (start, zero, (none, none)))
-    for j, s in enumerate(cuts):
-        racc_ref[0, :, s] = total[j]
-    sums_ref[0, 0] = sums[0]
-    sums_ref[0, 1] = sums[1]
-
-
 def front_kernel(
     span,
     x, og, lengths, taps_own, log_own, cbias_own, dbias_own, skip_own, gain_own,
     in_own, out_own, xp_own, dt_own,
-    normed_out, bg, mask, lead, conv, u, gate, raw, delta, bw, cw, bbd, cbd, gg, dy, step_low,
-    start, final, in_full, out_full, xp_full, dt_full, small_full,
+    hidden_out, step_low, final, bbd,
+    held_all, normed_full, bg_full, lead_full, slope_full, u_full, sig_full, delta_full,
+    cw_full, dy_full, gated_full, zg_full, in_full, xp_full, dt_full, small_full,
     in_w, out_w, xp, dt, small, small_own, hx, acc, zacc, normed, v, proj, ends, sums,
-    ends_in, sums_in,
-    send, recv, halo, relay_send, relay_recv, sums_send, sums_recv, local, keep,
+    ends_in, sums_in, bg, mask, lead, slope, u, sig, delta, bw, cw, cbd, gg, dy, y, gated, zg,
+    start, held,
+    send, recv, halo, relay_send, relay_recv, sums_send, sums_recv, local, keep, held_sem,
 ):
     d, s, f = (lax.axis_index(a) for a in ("dp", "seq", "fsdp"))
     fx, fy, fd = f ^ 1, f ^ 2, f ^ 3
@@ -300,7 +217,6 @@
     def norm_step(r, carry):
         tok = pl.ds(pl.multiple_of(r * GROUP, GROUP), GROUP)
         normed[tok] = normalised(x[tok])
-        normed_out[tok] = normed[tok]
         return carry
 
     lax.fori_loop(0, rows // GROUP, norm_step, 0)
@@ -353,8 +269,9 @@
             for k in range(TAPS):
                 at = GROUP - TAPS + 1 + k
                 total = total + small[k : k + 1, cols] * held[at : at + ctx]
-            conv[c * ctx : (c + 1) * ctx, cols] = total
-            u[c * ctx : (c + 1) * ctx, cols] = (total * jax.nn.sigmoid(total)).astype(BF16)
+            value, grad = silu_parts(total)
+            slope[c * ctx : (c + 1) * ctx, cols] = grad.astype(BF16)
+            u[c * ctx : (c + 1) * ctx, cols] = value.astype(BF16)
         return carry
 
     lax.fori_loop(0, inner // tile, conv_step, 0)
@@ -391,7 +308,7 @@
         for c in range(seqs):
             tok = slice(c * ctx, (c + 1) * ctx)
             value = dot(step_low[tok], dt[:, cols]) + small[at_bias + 1 : at_bias + 2, cols]
-            raw[tok, cols] = value
+            sig[tok, cols] = jax.nn.sigmoid(value).astype(BF16)
             value = jnp.maximum(value, 0.0) + jnp.log1p(jnp.exp(-jnp.abs(value)))
             for i in range(groups):
                 delta[c * groups + i, :, cols] = value[i * GROUP : (i + 1) * GROUP]
@@ -473,55 +390,46 @@
             for n, cut in enumerate(cuts):
                 ends[1, c, :, cut] = p[n].astype(BF16)
 
-    forward_ends(0)
-    ends_start(s + 1, span, 0, 0)
-    serve_near(GATE)
-    own_ready(GATE)
-    project(zacc, rows, inner, f, True)
-    forward_ends(1)
-    ends_start(s + 1, span, 0, 1)
-    near_ready(GATE)
-    project(zacc, rows, inner, fx, False)
-    project(zacc, rows, inner, fy, False)
-
-    def grad_part(owner):
-        shard = pl.ds(pl.multiple_of(owner * share, share), share)
-        gg[:, shard] = dot(bg[...], out_w[shard], across)
-
-    own_ready(OUT)
-    grad_part(f)
-    serve_near(OUT)
-    serve_far(GATE)
-    far_ready(GATE)
-    project(zacc, rows, inner, fd, False)
-    near_ready(OUT)
-    grad_part(fx)
-    grad_part(fy)
-    serve_far(OUT)
-    far_ready(OUT)
-    grad_part(fd)
-
-    fulls = ((in_w, in_full), (out_w, out_full), (xp, xp_full), (dt, dt_full), (small, small_full))
-    kept = [pltpu.make_async_copy(a, b, keep.at[n]) for n, (a, b) in enumerate(fulls)]
-    for one in kept:
-        one.start()
-
-    def gate_step(t, carry):
-        cols = columns(t)
+    def stash(*pairs):
+        for at, (src, dst) in pairs:
+            one = pltpu.make_async_copy(src, dst, keep.at[at])
+            one.start()
+            kept.append(one)
+
+    kept = []
+    stash(
+        (0, (normed.at[:rows], normed_full)), (1, (bg, bg_full)), (2, (lead, lead_full)),
+        (3, (slope, slope_full)), (4, (u, u_full)), (5, (sig, sig_full)), (6, (delta, delta_full)),
+        (7, (cw, cw_full)), (8, (xp, xp_full)), (9, (dt, dt_full)), (10, (small, small_full)),
+    )
+
+    def ends_wait(j, c):
+        pltpu.make_async_remote_copy(
+            src_ref=ends.at[0, c], dst_ref=ends_in.at[j, c], send_sem=relay_send.at[j, c],
+            recv_sem=relay_recv.at[j, c], device_id={"seq": j}, device_id_type=MESH,
+        ).wait_recv()
+
+    def join(ref, j, c):
+        ends_wait(j, c)
+
+        def one(t, carry):
+            cols = columns(t, CHUNK)
+            rates = -jnp.exp(small[at_state:at_bias, cols]) * LOG2E
+            decay = jnp.exp2(sums_in[j, c : c + 1, cols] * rates)
+            ref[c, :, cols] = decay * ref[c, :, cols] + ends_in[j, c, :, cols].astype(F32)
+            return carry
+
+        lax.fori_loop(0, inner // CHUNK, one, 0)
+
+    def join_start(j, carry):
         for c in range(seqs):
-            tok = slice(c * ctx, (c + 1) * ctx)
-            low = zacc[tok, cols].astype(BF16)
-            gate[tok, cols] = low
-            value = low.astype(F32)
-            value = gg[tok, cols] * (value * jax.nn.sigmoid(value))
-            for i in range(groups):
-                dy[c * groups + i, :, cols] = value[i * GROUP : (i + 1) * GROUP]
-        return carry
-
-    lax.fori_loop(0, inner // tile, gate_step, 0)
-    for c in range(seqs):
-        backward_ends(c)
-        ends_start(0, s, 1, c)
+            join(start, j, c)
+        return carry
+
+    def join_final(o, carry):
+        for c in range(seqs):
+            join(final, span - 1 - o, c)
+        return carry
 
     def sums_wait(o, carry):
         j = lax.rem(s + o, span)
@@ -531,40 +439,113 @@
         ).wait_recv()
         return carry
 
+    parts = inner // CHUNK
+    blocks = seqs * parts
+
+    def held_copy(b):
+        slot = lax.rem(b, 2)
+        return pltpu.make_async_copy(held.at[slot], held_all.at[b], held_sem.at[slot])
+
+    def sweep_block(b, carry):
+        c, slot = b // parts, lax.rem(b, 2)
+        first = lax.rem(b, parts) * CHUNK
+        cuts = [pl.ds(pl.multiple_of(first + n, LANES), LANES) for n in range(0, CHUNK, LANES)]
+        tiles = [slice(n, n + LANES) for n in range(0, CHUNK, LANES)]
+        all_cols = pl.ds(pl.multiple_of(first, CHUNK), CHUNK)
+        rates = [-jnp.exp(small[at_state:at_bias, cut]) * LOG2E for cut in cuts]
+        skip = small[at_bias + 2 : at_bias + 3, all_cols]
+
+        @pl.when(b >= 2)
+        def _():
+            held_copy(b - 2).wait()
+
+        h = tuple(start[c, :, cut] for cut in cuts)
+        for n, cut in enumerate(tiles):
+            held[slot, 0, :, cut] = h[n].astype(BF16)
+
+        def one(i, h):
+            h = list(h)
+            g = c * groups + i
+            for k in range(GROUP):
+                b_in = bw[c, i * GROUP + k]
+                for n, cut in enumerate(cuts):
+                    step = jnp.broadcast_to(delta[g, k : k + 1, cut], (state, LANES))
+                    row = jnp.broadcast_to(v[g, k : k + 1, cut], (state, LANES))
+                    h[n] = jnp.exp2(step * rates[n]) * h[n] + row * b_in
+                    held[slot, i * GROUP + k + 1, :, tiles[n]] = h[n].astype(BF16)
+            states = held[slot, pl.ds(i * GROUP + 1, GROUP)].reshape(GROUP * state, CHUNK)
+            tok = pl.ds(pl.multiple_of(g * GROUP, GROUP), GROUP)
+            y[g, :, all_cols] = dot(cbd[tok], states) + skip * u[tok, all_cols].astype(F32)
+            return tuple(h)
+
+        lax.fori_loop(0, groups, one, h)
+        held_copy(b).start()
+        return carry
+
+    def grad_part(owner):
+        shard = pl.ds(pl.multiple_of(owner * share, share), share)
+        gg[:, shard] = dot(bg[...], out_w[shard], across)
+
+    forward_ends(0)
+    ends_start(s + 1, span, 0, 0)
+    serve_near(GATE)
+    own_ready(GATE)
+    forward_ends(1)
+    ends_start(s + 1, span, 0, 1)
+    near_ready(GATE)
+    for owner, fresh in ((f, True), (fx, False), (fy, False)):
+        project(zacc, rows, inner, owner, fresh)
     lax.fori_loop(1, span, sums_wait, 0)
-
-    def ends_wait(j, c):
-        pltpu.make_async_remote_copy(
-            src_ref=ends.at[0, c], dst_ref=ends_in.at[j, c], send_sem=relay_send.at[j, c],
-            recv_sem=relay_recv.at[j, c], device_id={"seq": j}, device_id_type=MESH,
-        ).wait_recv()
-
     start[...] = jnp.zeros(start.shape, F32)
+    lax.fori_loop(0, s, join_start, 0)
+    lax.fori_loop(0, 2, sweep_block, 0)
+    serve_far(GATE)
+    lax.fori_loop(2, 4, sweep_block, 0)
+    serve_near(OUT)
+    far_ready(GATE)
+    project(zacc, rows, inner, fd, False)
+    lax.fori_loop(4, blocks - 1, sweep_block, 0)
+    serve_far(OUT)
+    stash((11, (in_w, in_full)))
+    lax.fori_loop(blocks - 1, blocks, sweep_block, 0)
+    own_ready(OUT)
+    near_ready(OUT)
+    for owner in (f, fx, fy):
+        grad_part(owner)
+    far_ready(OUT)
+    grad_part(fd)
+
+    def gate_step(t, carry):
+        cols = columns(t)
+        for c in range(seqs):
+            tok = slice(c * ctx, (c + 1) * ctx)
+            value, grad = silu_parts(zacc[tok, cols].astype(BF16).astype(F32))
+            back = gg[tok, cols]
+            pieces = [y[c * groups + i, :, cols] for i in range(groups)]
+            scanned = jnp.concatenate(pieces, 0)
+            gated[tok, cols] = (scanned * value).astype(BF16)
+            half = pl.ds(pl.multiple_of(lax.rem(t, 2) * tile, tile), tile)
+            zg[t // 2, tok, half] = (back * scanned * grad).astype(BF16)
+            value = back * value
+            for i in range(groups):
+                dy[c * groups + i, :, cols] = value[i * GROUP : (i + 1) * GROUP]
+        return carry
+
+    lax.fori_loop(0, inner // tile, gate_step, 0)
+    stash((12, (dy, dy_full)), (13, (gated, gated_full)), (14, (zg, zg_full)))
+    for c in range(seqs):
+        backward_ends(c)
+        ends_start(0, s, 1, c)
+
+    def hidden_step(t, carry):
+        cols = columns(t)
+        keep_rows = jnp.concatenate([mask[...]] * (tile // LANES), 1)
+        branch = dot(gated[...], out_w[:, cols])
+        hidden_out[:, cols] = (x[:, cols].astype(F32) + keep_rows * branch).astype(BF16)
+        return carry
+
+    lax.fori_loop(0, width // tile, hidden_step, 0)
     final[...] = jnp.zeros(final.shape, F32)
-
-    def join(ref, j, c):
-        ends_wait(j, c)
-
-        def one(t, carry):
-            cols = columns(t, CHUNK)
-            rates = -jnp.exp(small[at_state:at_bias, cols]) * LOG2E
-            decay = jnp.exp2(sums_in[j, c : c + 1, cols] * rates)
-            ref[c, :, cols] = decay * ref[c, :, cols] + ends_in[j, c, :, cols].astype(F32)
-            return carry
-
-        lax.fori_loop(0, inner // CHUNK, one, 0)
-
-    def join_start(j, carry):
-        for c in range(seqs):
-            join(start, j, c)
-        return carry
-
-    def join_final(o, carry):
-        for c in range(seqs):
-            join(final, span - 1 - o, c)
-        return carry
-
-    lax.fori_loop(0, s, join_start, 0)
     lax.fori_loop(0, span - 1 - s, join_final, 0)
 
     for one in started:
@@ -585,6 +566,8 @@
     lax.fori_loop(1, span, sent, 0)
     for one in kept:
         one.wait()
+    for b in range(max(blocks - 2, 0), blocks):
+        held_copy(b).wait()
 
 
 def front(x, og, lengths, taps, logs, cbias, dbias, skip, gain, in_own, out_own, xp_own, dt_own, seqs):
@@ -593,40 +576,43 @@
     state, rank, used = logs.shape[0], dt_own.shape[0], xp_own.shape[1]
     ctx = rows // seqs
     span = lax.axis_size("seq")
+    parts = inner // CHUNK
     vmem, dma = pltpu.VMEM, pltpu.SemaphoreType.DMA
     whole, anywhere = pl.BlockSpec(memory_space=vmem), pl.BlockSpec(memory_space=pl.ANY)
     shape = jax.ShapeDtypeStruct
+    grouped = (rows // GROUP, GROUP, inner)
+    kept = [
+        ((rows, width), BF16),
+        ((rows, width), BF16),
+        ((seqs, ctx + GROUP, inner), BF16),
+        ((rows, inner), BF16),
+        ((rows, inner), BF16),
+        ((rows, inner), BF16),
+        (grouped, F32),
+        ((seqs, ctx, state, LANES), F32),
+        (grouped, F32),
+        ((rows, inner), BF16),
+        ((parts, rows, CHUNK), BF16),
+        ((width, 2 * inner), BF16),
+        ((inner, used), BF16),
+        ((rank, inner), BF16),
+        ((32, inner), F32),
+    ]
+    held = (ctx + 1, state, CHUNK)
     return pl.pallas_call(
         functools.partial(front_kernel, span),
         in_specs=[whole, whole, pl.BlockSpec(memory_space=pltpu.SMEM)]
         + [whole] * 6
         + [anywhere] * 4,
-        out_specs=[whole] * 18 + [anywhere] * 5,
+        out_specs=[whole] * 4 + [anywhere] * (1 + len(kept)),
         out_shape=[
             shape((rows, width), BF16),
-            shape((rows, width), BF16),
-            shape((rows, LANES), F32),
-            shape((seqs, ctx + GROUP, inner), BF16),
-            shape((rows, inner), F32),
-            shape((rows, inner), BF16),
-            shape((rows, inner), BF16),
-            shape((rows, inner), F32),
-            shape((rows // GROUP, GROUP, inner), F32),
-            shape((seqs, ctx, state, LANES), F32),
-            shape((seqs, ctx, state, LANES), F32),
-            shape((rows, GROUP * state), BF16),
-            shape((rows, GROUP * state), BF16),
-            shape((rows, inner), F32),
-            shape((rows // GROUP, GROUP, inner), F32),
             shape((rows, rank), BF16),
             shape((seqs, state, inner), F32),
-            shape((seqs, state, inner), F32),
-            shape((width, 2 * inner), BF16),
-            shape((inner, width), BF16),
-            shape((inner, used), BF16),
-            shape((rank, inner), BF16),
-            shape((32, inner), F32),
-        ],
+            shape((rows, GROUP * state), BF16),
+            shape((seqs * parts,) + held, BF16),
+        ]
+        + [shape(*k) for k in kept],
         scratch_shapes=[
             vmem((width, 2 * inner), BF16),
             vmem((inner, width), BF16),
@@ -638,12 +624,29 @@
             vmem((rows + seqs * GROUP, inner), F32),
             vmem((rows, inner), F32),
             vmem((rows + seqs * GROUP, width), BF16),
-            vmem((rows // GROUP, GROUP, inner), F32),
+            vmem(grouped, F32),
             vmem((rows, used), F32),
             vmem((2, seqs, state, inner), BF16),
             vmem((8, inner), F32),
             vmem((span, seqs, state, inner), BF16),
             vmem((span, 8, inner), F32),
+            vmem((rows, width), BF16),
+            vmem((rows, LANES), F32),
+            vmem((seqs, ctx + GROUP, inner), BF16),
+            vmem((rows, inner), BF16),
+            vmem((rows, inner), BF16),
+            vmem((rows, inner), BF16),
+            vmem(grouped, F32),
+            vmem((seqs, ctx, state, LANES), F32),
+            vmem((seqs, ctx, state, LANES), F32),
+            vmem((rows, GROUP * state), BF16),
+            vmem((rows, inner), F32),
+            vmem(grouped, F32),
+            vmem(grouped, F32),
+            vmem((rows, inner), BF16),
+            vmem((parts, rows, CHUNK), BF16),
+            vmem((seqs, state, inner), F32),
+            vmem((2,) + held, BF16),
             dma((6, 12)),
             dma((6, 12)),
             dma((2, seqs)),
@@ -652,7 +655,8 @@
             dma((span,)),
             dma((span,)),
             dma((6, 4)),
-            dma((5,)),
+            dma((len(kept),)),
+            dma((2,)),
         ],
         compiler_params=pltpu.CompilerParams(
             collective_id=0, has_side_effects=True, vmem_limit_bytes=63 << 20
@@ -663,10 +667,14 @@
 
 def back_kernel(
     span, state, rank,
-    gated, zg, ug, rl, u, conv, lead, step_low, cacc, bacc, normed, x, og, bg, mask,
-    in_w, out_w, xp, dt, small, racc, sums,
-    hidden_out, input_grad, out_sum, in_sum, rest_sum,
-    pg, mixed, cg, ng, rest, g, ra, rx, ry, zlo, zhi, tot, send, recv, halo, local,
+    gated, bg, step_low, final, bbd, ones, small, x, og,
+    held_all, normed_full, lead_full, slope_full, u_full, sig_full, delta_full,
+    cw_full, dy_full, zg_full, in_full, xp_full, dt_full,
+    input_grad, out_sum, in_sum, rest_sum,
+    normed, lead, slope, u, sig, delta, cw, dy, mixed, xp, dt, in_w, held, gs, ws, rl, cacc,
+    bacc, logs, sums,
+    pg, cg, ng, rest, g, ra, rx, ry, zlo, zhi, tot,
+    send, recv, halo, local, load, held_sem, in_sem,
 ):
     d, s, f = (lax.axis_index(a) for a in ("dp", "seq", "fsdp"))
     fx, fy, fd = f ^ 1, f ^ 2, f ^ 3
@@ -690,6 +698,28 @@
         a, b, dims, preferred_element_type=F32
     )
 
+    loads = (
+        (mixed.at[:parts], zg_full), (normed, normed_full), (delta, delta_full), (dy, dy_full),
+        (u, u_full), (cw, cw_full), (sig, sig_full), (slope, slope_full),
+        (lead, lead_full), (xp, xp_full), (dt, dt_full),
+    )
+    loads = [pltpu.make_async_copy(src, dst, load.at[n]) for n, (dst, src) in enumerate(loads)]
+
+    def held_copy(b):
+        slot = lax.rem(b, 2)
+        return pltpu.make_async_copy(held_all.at[b], held.at[slot], held_sem.at[slot])
+
+    def in_copy(k):
+        slot = lax.rem(k, 2)
+        first = pl.multiple_of(lax.rem(k + parts, 2 * parts) * CHUNK, CHUNK)
+        return pltpu.make_async_copy(in_full.at[:, pl.ds(first, CHUNK)], in_w.at[slot], in_sem.at[slot])
+
+    held_copy(0).start()
+    for one in loads[2:6]:
+        one.start()
+    held_copy(1).start()
+    for one in loads[:2] + loads[6:]:
+        one.start()
     cg[:, ctx:] = jnp.zeros((seqs, cg.shape[1] - ctx, inner), F32)
     barrier = pltpu.get_barrier_semaphore()
     for who in (tox, toy, sib):
@@ -844,6 +874,62 @@
     def columns(t, size=tile):
         return pl.ds(pl.multiple_of(t * size, size), size)
 
+    def back_block(b):
+        c, slot = b // parts, lax.rem(b, 2)
+        groups = ctx // GROUP
+        first = lax.rem(b, parts) * CHUNK
+        cuts = [pl.ds(pl.multiple_of(first + n, LANES), LANES) for n in range(0, CHUNK, LANES)]
+        tiles = [slice(n, n + LANES) for n in range(0, CHUNK, LANES)]
+        cols = pl.ds(pl.multiple_of(first, CHUNK), CHUNK)
+        rates = [-jnp.exp(small[TAPS : TAPS + state, cut]) * LOG2E for cut in cuts]
+        skip = small[TAPS + state + 2 : TAPS + state + 3, cols]
+        held_copy(b).wait()
+
+        def one(turn, carry):
+            i = groups - 1 - turn
+            at = c * groups + i
+            tok = pl.ds(pl.multiple_of(at * GROUP, GROUP), GROUP)
+            p, total, kept = (list(value) for value in carry)
+            for k in reversed(range(GROUP)):
+                t = i * GROUP + k
+                read = cw[c, t]
+                for n, cut in enumerate(cuts):
+                    row = lambda ref: jnp.broadcast_to(ref[at, k : k + 1, cut], (state, LANES))
+                    step = row(delta)
+                    grad = read * row(dy) + p[n]
+                    p[n] = jnp.exp2(step * rates[n]) * grad
+                    w = p[n] * held[slot, t, :, tiles[n]].astype(F32)
+                    total[n] = total[n] + w * step
+                    gs[k, :, tiles[n]] = grad.astype(BF16)
+                    ws[k, :, tiles[n]] = (w * rates[n]).astype(BF16)
+            grads = gs[...].reshape(GROUP * state, CHUNK)
+            states = held[slot, pl.ds(i * GROUP + 1, GROUP)].reshape(GROUP * state, CHUNK)
+            drive_grad = dot(bbd[tok], grads)
+            delta_part = dot(ones[...], ws[...].reshape(GROUP * state, CHUNK))
+            value, out, gain = u[tok, cols].astype(F32), dy[at, :, cols], delta[at, :, cols]
+            bacc[tok] += dot((gain * value).astype(BF16), grads, across)
+            cacc[tok] += dot(out.astype(BF16), states, across)
+            raw_grad = drive_grad * value + delta_part * (1.0 / LOG2E)
+            raw_grad = raw_grad * sig[tok, cols].astype(F32)
+            rl[tok, cols] = raw_grad.astype(BF16)
+            dy[at, :, cols] = out * skip + drive_grad * gain
+            kept[0] = kept[0] + (out * value)[:8] + (out * value)[8:]
+            kept[1] = kept[1] + raw_grad[:8] + raw_grad[8:]
+            return tuple(p), tuple(total), tuple(kept)
+
+        zero = tuple(jnp.zeros((state, LANES), F32) for _ in cuts)
+        none = jnp.zeros((8, CHUNK), F32)
+        begin = tuple(final[c, :, cut] for cut in cuts)
+        _, total, kept = lax.fori_loop(0, groups, one, (begin, zero, (none, none)))
+        for n, cut in enumerate(cuts):
+            logs[:, cut] += total[n]
+        sums[0, :, cols] += kept[0]
+        sums[1, :, cols] += kept[1]
+
+        @pl.when(b + 2 < blocks)
+        def _():
+            held_copy(b + 2).start()
+
     def proj_work():
         step_grad = dot(rl[...], dt[...], across)
         r = lax.broadcasted_iota(jnp.int32, (rows, GROUP * state), 0)
@@ -856,7 +942,8 @@
         grads = jnp.concatenate([step_grad, jnp.zeros((rows, LANES - rank), F32)], 1)
         grads = grads + dot(pick(bacc), fold(rank)) + dot(pick(cacc), fold(rank + state))
         pg[...] = grads.astype(BF16)
-        rest[...] = jnp.zeros(rest.shape, F32)
+
+    def weight_work():
         first = TAPS + state + 4
         used = rank + 2 * state
 
@@ -864,15 +951,11 @@
             cols = columns(t)
             rest[first : first + rank, cols] = dot(step_low[...], rl[:, cols], contract)
             rest[first + rank : first + rank + used, cols] = dot(pg[...], u[:, cols], contract)[:used]
-            logs = racc[0, :, cols]
-            kept = sums[0, :, :, cols]
-            for c in range(1, seqs):
-                logs = logs + racc[c, :, cols]
-                kept = kept + sums[c, :, :, cols]
-            rest[TAPS : TAPS + state, cols] = -logs * jnp.exp(small[TAPS : TAPS + state, cols])
+            kept = -logs[:, cols] * jnp.exp(small[TAPS : TAPS + state, cols])
+            rest[TAPS : TAPS + state, cols] = kept
             at = TAPS + state
-            rest[at + 1 : at + 2, cols] = jnp.sum(kept[1], 0, keepdims=True)
-            rest[at + 2 : at + 3, cols] = jnp.sum(kept[0], 0, keepdims=True)
+            rest[at + 1 : at + 2, cols] = jnp.sum(sums[1, :, cols], 0, keepdims=True)
+            rest[at + 2 : at + 3, cols] = jnp.sum(sums[0, :, cols], 0, keepdims=True)
             return carry
 
         lax.fori_loop(0, inner // tile, weights, 0)
@@ -886,8 +969,9 @@
                 tok = slice(c * ctx, (c + 1) * ctx)
                 weight = xp[columns(t)]
                 back = dot(pg[tok, : weight.shape[1]], weight, across)
-                _, slope = silu_parts(conv[tok, cols])
-                grad = (ug[tok, cols] + back) * slope
+                own = range(c * ctx // GROUP, (c + 1) * ctx // GROUP)
+                grad = jnp.concatenate([dy[at, :, cols] for at in own], 0) + back
+                grad = grad * slope[tok, cols].astype(F32)
                 cg[c, :ctx, cols] = grad
                 before = lead[c, :, cols].astype(F32)
                 shift = shift + jnp.sum(grad, 0, keepdims=True)
@@ -927,21 +1011,15 @@
         lax.fori_loop(0, inner // tile, one, 0)
         pl.when(s > 0)(lambda: H().wait_send())
 
-    def hidden_work():
-        def one(t, carry):
-            cols = columns(t)
-            branch = dot(gated[...], out_w[:, cols])
-            keep = mask[...]
-            keep = jnp.concatenate([keep] * (tile // LANES), 1)
-            hidden_out[:, cols] = (x[:, cols].astype(F32) + keep * branch).astype(BF16)
-            return carry
-
-        lax.fori_loop(0, width // tile, one, 0)
-
     def norm_work(first, count):
         def one(k, carry):
-            cols = columns(lax.rem(k + parts, 2 * parts), CHUNK)
-            ng[...] += dot(mixed[k], in_w[:, cols], across)
+            in_copy(k).wait()
+            ng[...] += dot(mixed[k], in_w[lax.rem(k, 2)], across)
+
+            @pl.when(k + 2 < 2 * parts)
+            def _():
+                in_copy(k + 2).start()
+
             return carry
 
         if first == 0:
@@ -971,34 +1049,61 @@
         for j in range(4):
             rest[at : at + 1, j * CHUNK : j * CHUNK + share] = total[:, j * share : (j + 1) * share]
 
-    mixed[:parts] = zg[...]
+    blocks = seqs * parts
     tiles = inner // tile
-    work = {
-        0: proj_work,
-        1: lambda: conv_work(0, tiles // 2),
-        2: lambda: conv_work(tiles // 2, tiles // 2),
-        3: halo_send,
-        4: hidden_work,
-        5: stream_work,
-        last - 4: lambda: norm_work(0, parts),
-        last - 3: lambda: norm_work(parts, parts),
-        last - 2: input_work,
-    }
+    pause = 3
+    held_back = out_chunks + parts
     base = 1 + 2 * SLACK + 1
 
+    def prepare():
+        for ref in (cacc, bacc, logs, sums, rest):
+            ref[...] = jnp.zeros(ref.shape, F32)
+        for one in loads[2:]:
+            one.wait()
+
+    def blocks_work(i):
+        pl.when(i == 0)(prepare)
+        pl.when(i < blocks)(lambda: back_block(i))
+
+    def late_work(i):
+        at = held_back
+
+        @pl.when(i == at)
+        def _():
+            proj_work()
+            conv_work(0, tiles)
+            halo_send()
+            in_copy(0).start()
+            in_copy(1).start()
+
+        pl.when(i == at + 1)(weight_work)
+        pl.when(i == at + 2)(stream_work)
+        pl.when(i == at + 4)(lambda: norm_work(0, parts))
+        pl.when(i == at + 5)(lambda: norm_work(parts, parts))
+        pl.when(i == at + 6)(input_work)
+
     def step(i, carry):
-        stage(i, produce)
-        stage(i - 1, first_sum)
-        stage(i - 1 - SLACK, second_sum)
-        stage(i - 1 - 2 * SLACK, third_sum)
-        pl.when(s != root)(lambda: stage(i - base - SLACK * spot, inward))
-        pl.when(s == root)(lambda: stage(i - base - SLACK * most, at_root))
-        pl.when(s != root)(lambda: stage(i - base - SLACK * most - SLACK * far, outward))
-        for at, run in work.items():
-            pl.when(i == at)(run)
-        return carry
-
-    lax.fori_loop(0, chunks + base + 2 * SLACK * most + 1, step, 0)
+        def at(offset):
+            k = i - offset
+            return jnp.where(k < held_back, k, jnp.where(k < held_back + pause, -1, k - pause))
+
+        @pl.when(i == out_chunks)
+        def _():
+            for one in loads[:2]:
+                one.wait()
+
+        stage(at(0), produce)
+        stage(at(1), first_sum)
+        stage(at(1 + SLACK), second_sum)
+        stage(at(1 + 2 * SLACK), third_sum)
+        pl.when(s != root)(lambda: stage(at(base + SLACK * spot), inward))
+        pl.when(s == root)(lambda: stage(at(base + SLACK * most), at_root))
+        pl.when(s != root)(lambda: stage(at(base + SLACK * most + SLACK * far), outward))
+        blocks_work(i)
+        late_work(i)
+        return carry
+
+    lax.fori_loop(0, chunks + pause + base + 2 * SLACK * most + 1, step, 0)
 
     def finish(c, carry):
         pl.when(c >= chunks - slots)(lambda: A(c).wait_send())
@@ -1034,36 +1139,47 @@
         one.wait()
 
 
-def back(*args):
-    gated, zg, _, _, _, _, _, step_low, cacc, _, _, x = args[:12]
-    in_w, out_w = args[15:17]
+def back(gated, bg, step_low, final, bbd, small, x, og, far):
     rows, inner = gated.shape
     width = x.shape[1]
-    state = cacc.shape[1] // GROUP
-    rank = step_low.shape[1]
-    seqs = args[20].shape[0]
+    seqs, state = final.shape[:2]
+    ctx, rank, parts = rows // seqs, step_low.shape[1], inner // CHUNK
     span = lax.axis_size("seq")
-    out_chunks, in_chunks = 2 * width // CHUNK, 2 * inner // CHUNK
+    out_chunks, in_chunks = 2 * width // CHUNK, 2 * parts
     n = out_chunks + in_chunks + 1
+    ones = jnp.asarray(np.kron(np.eye(GROUP), np.ones((1, state))), BF16)
     vmem, dma = pltpu.VMEM, pltpu.SemaphoreType.DMA
-    any_space = pl.BlockSpec(memory_space=pl.ANY)
+    anywhere = pl.BlockSpec(memory_space=pl.ANY)
     whole = pl.BlockSpec(memory_space=vmem)
     shape = jax.ShapeDtypeStruct
+    like = lambda v: vmem(v.shape, v.dtype)
+    (held, normed, lead, slope, u, sig, delta, cw, dy, zg, in_full, xp, dt) = far
     return pl.pallas_call(
         functools.partial(back_kernel, span, state, rank),
-        in_specs=[whole] * len(args),
-        out_specs=[whole, whole, any_space, any_space, any_space],
+        in_specs=[whole] * 9 + [anywhere] * len(far),
+        out_specs=[whole, anywhere, anywhere, anywhere],
         out_shape=[
-            shape((rows, width), BF16),
             shape((rows, width), BF16),
             shape((inner // 4, width), BF16),
             shape((width // 4, 2 * inner), BF16),
             shape((2 * HR, CHUNK), BF16),
         ],
         scratch_shapes=[
+            *map(like, (normed, lead, slope, u, sig, delta, cw, dy)),
+            vmem((in_chunks, rows, CHUNK), BF16),
+            like(xp),
+            like(dt),
+            vmem((2, width, CHUNK), BF16),
+            vmem((2,) + held.shape[1:], BF16),
+            vmem((GROUP, state, CHUNK), BF16),
+            vmem((GROUP, state, CHUNK), BF16),
+            vmem((rows, inner), BF16),
+            vmem((rows, GROUP * state), F32),
+            vmem((rows, GROUP * state), F32),
+            vmem((state, inner), F32),
+            vmem((2, 8, inner), F32),
             vmem((rows, LANES), BF16),
-            vmem((in_chunks, rows, CHUNK), BF16),
-            vmem((seqs, rows // seqs + 8, inner), F32),
+            vmem((seqs, ctx + 8, inner), F32),
             vmem((rows, width), F32),
             vmem((2 * HR, inner), F32),
             vmem((4, 4, 2, HR, CHUNK), BF16),
@@ -1077,62 +1193,15 @@
             dma((12, n)),
             dma((2,)),
             dma((n, 2)),
+            dma((11,)),
+            dma((2,)),
+            dma((2,)),
         ],
         compiler_params=pltpu.CompilerParams(
             collective_id=1, has_side_effects=True, vmem_limit_bytes=63 << 20
         ),
         name="back",
-    )(*args)
-
-
-def local_specs(seqs, ctx, inner, state, width):
-    groups = ctx // GROUP
-    tok = pl.BlockSpec((1, groups, GROUP, width), lambda c, j: (c, 0, 0, j))
-    wide = pl.BlockSpec((1, ctx, state, LANES), lambda c, j: (c, 0, 0, 0))
-    rate = pl.BlockSpec((state, width), lambda c, j: (0, j))
-    end = pl.BlockSpec((1, state, width), lambda c, j: (c, 0, j))
-    diag = pl.BlockSpec((1, groups, GROUP, GROUP * state), lambda c, j: (c, 0, 0, 0))
-    return tok, wide, rate, end, diag
-
-
-def sweep(delta, u, dy, gated_grad, gate_in, raw, b_wide, c_wide, bbd, cbd, small, start, final):
-    seqs, groups, _, inner = delta.shape
-    ctx = groups * GROUP
-    state = b_wide.shape[2]
-    width = CHUNK
-    tok, wide, _, end, diag = local_specs(seqs, ctx, inner, state, width)
-    ones = jnp.asarray(np.kron(np.eye(GROUP), np.ones((1, state))), BF16)
-    token = lambda t: jax.ShapeDtypeStruct(delta.shape, t)
-    diag_shape = jax.ShapeDtypeStruct((seqs, groups, GROUP, GROUP * state), F32)
-    chunked = pl.BlockSpec((1, 1, groups, GROUP, width), lambda c, j: (j, c, 0, 0, 0))
-    chunked_shape = jax.ShapeDtypeStruct((inner // width, seqs, groups, GROUP, width), BF16)
-    vmem = pltpu.VMEM
-    return pl.pallas_call(
-        sweep_kernel,
-        grid=(seqs, inner // width),
-        in_specs=[tok] * 6
-        + [wide, wide, pl.BlockSpec((small.shape[0], width), lambda c, j: (0, j)), end, end]
-        + [diag, diag, pl.BlockSpec(ones.shape, lambda c, j: (0, 0))],
-        out_specs=[tok, chunked, tok, tok, diag, diag, end]
-        + [pl.BlockSpec((1, 2, 8, width), lambda c, j: (c, 0, 0, j))],
-        out_shape=[token(BF16), chunked_shape, token(F32), token(BF16)]
-        + [diag_shape] * 2
-        + [jax.ShapeDtypeStruct((seqs, state, inner), F32)]
-        + [jax.ShapeDtypeStruct((seqs, 2, 8, inner), F32)],
-        scratch_shapes=[
-            vmem((groups, GROUP, width), F32),
-            vmem((groups, GROUP, width), F32),
-            vmem((ctx + 1, state, width), F32),
-            vmem((ctx, state, width), F32),
-            vmem((GROUP, state, width), BF16),
-            vmem((GROUP, state, width), BF16),
-        ],
-        compiler_params=pltpu.CompilerParams(vmem_limit_bytes=56 << 20),
-        name="sweep",
-    )(
-        delta, u, dy, gated_grad, gate_in, raw, b_wide, c_wide, small, start, final,
-        cbd.reshape(diag_shape.shape), bbd.reshape(diag_shape.shape), ones,
-    )
+    )(gated, bg, step_low, final, bbd, ones, small, x, og, *far)
 
 
 def body(
@@ -1147,23 +1216,18 @@
     row = lambda v: v.reshape(1, -1)
     x, og = hidden_in.reshape(rows, width), out_grad.reshape(rows, width)
     (
-        normed, branch_grad, mask, lead, conv_out, u, gate_in, raw, delta, b_wide, c_wide, bbd, cbd,
-        gated_grad, y_grad, step_low, start, final,
-        in_matrix, out_matrix, proj_matrix, step_matrix, small,
+        hidden_out, step_low, final, bbd, held, normed, branch_grad, lead, slope, u, sig, delta,
+        c_wide, y_grad, gated, z_grad, in_matrix, proj_matrix, step_matrix, small,
     ) = front(
         x, og, lengths, conv_weight, a_log, row(conv_bias), row(dt_bias), row(skip_gain),
         row(norm_gain), in_weight, out_weight, xproj_weight, dt_weight, seqs,
     )
-    grouped = lambda v: v.reshape(seqs, ctx // GROUP, GROUP, v.shape[-1])
-    gated, z_grad, u_grad, raw_low, c_acc, b_acc, rate_grad, sums = sweep(
-        *map(grouped, (delta, u, y_grad, gated_grad, gate_in, raw)),
-        b_wide, c_wide, bbd, cbd, small, start, final,
+    far = (
+        held, normed, lead, slope, u, sig, delta, c_wide, y_grad, z_grad, in_matrix,
+        proj_matrix, step_matrix,
     )
-    flat = lambda v: v.reshape(rows, -1)
-    hidden_out, input_grad, out_sum, in_sum, rest = back(
-        flat(gated), z_grad.reshape(-1, rows, CHUNK), flat(u_grad), flat(raw_low), u, conv_out,
-        lead, step_low, flat(c_acc), flat(b_acc), normed, x, og, branch_grad, mask,
-        in_matrix, out_matrix, proj_matrix, step_matrix, small, rate_grad, sums,
+    input_grad, out_sum, in_sum, rest = back(
+        gated, branch_grad, step_low, final, bbd, small, x, og, far
     )
     rest = rest.astype(F32)
     shards = lax.axis_size("fsdp")

time: 289 us -> 290 us (level)
    pallas_call x1 -> x0, Pallas kernels: 59.3 us -> none  [sweep(): pl.pallas_call(sweep_kernel, grid=(seqs, inner // width), in_specs=[tok]...]
    pallas_call x1, Pallas kernels: 102 us -> 141 us  [back(): pl.pallas_call(functools.partial(back_kernel, span, state, rank), in_spec...]
    pallas_call x1, Pallas kernels: 111 us -> 132 us  [front(): pl.pallas_call(functools.partial(front_kernel, span), in_specs=[whole, wh...]
where the time goes in v4:
time: 290 us
  Pallas kernels  273 us (94%)
  local copies, waits for them, and re-layouts  10.8 us (4%)
  other arithmetic  5.22 us (2%)
    pallas_call x1, Pallas kernels, back(): pl.pallas_call(functools.partial(back_kernel, span, state, rank), in_spec...  141 us
    pallas_call x1, Pallas kernels, front(): pl.pallas_call(functools.partial(front_kernel, span), in_specs=[whole, wh...  132 us

profile of v4, /device:TPU:25, one launch (start us, length us, event | category | flops | bytes accessed | tf_op | source)
XLA Modules:
  0.0 289.8 jit_solution(7562607221375005949)
XLA Ops:
  0.6 1.7 copy.26.xp_own
  2.3 132.2 %front.1 = (bf16[256,1024]{1,0:T(8,128)(2,1)}, bf16[256,64]{1,0:T(8,128)(2,1)}, f32[2,16,2048]{2,1,0:T(8,128)}, bf16[256,256]{1,0:T(8,128)(2,1)}, bf16[8,129,16,...) custom-call(bf16[256,1024]{1,0:T(8,128)(2,1)} %bitcast.14, ...), custom_call_target="tpu_custom_call" | custom-call | tf_op jit(solution)/shard_map/front/pallas_call | solution.py:602
  134.5 140.8 %back.1 = (bf16[256,1024]{1,0:T(8,128)(2,1)}, bf16[512,1024]{1,0:T(8,128)(2,1)}, bf16[256,4096]{1,0:T(8,128)(2,1)}, bf16[256,512]{1,0:T(8,128)(2,1)}) custom-call(bf16[256,2048]{1,0:T(8,128)(2,1)} %get-tuple-element.37.gated, bf16[256,1024]{1,0:T(8,128)(2,1)} %get-tuple-element.38.bg, bf16[256,64]{1,0:T(8,128)(2,1)} %get-tuple-element.39.step_low, ...), custom_call_target="tpu_custom_call" | custom-call | tf_op jit(solution)/shard_map/back/pallas_call | solution.py:1157
  275.4 0.0 copy-start.1
  275.4 1.3 slice.32
  276.7 1.4 fusion
  278.1 1.3 slice.33
  279.4 1.4 slice.38
  280.8 1.5 slice.36
  282.3 0.0 copy-start
  282.3 1.1 convert_element_type.9
  283.4 0.7 slice_bitcast_fusion
  284.1 0.0 copy-done.1
  284.1 1.6 convert_element_type.11
  285.7 0.0 copy-done
  285.7 0.0 copy-start.2
  285.7 0.0 copy-start.3
  285.7 2.5 convert_element_type.10
  288.2 0.0 copy-done.2
  288.2 0.8 copy.29
  289.0 0.0 copy-done.3
  289.0 0.8 copy.30
Async XLA Ops:
  275.4 8.7 %copy-start.1 = (bf16[512,1024]{1,0:T(8,128)(2,1)S(1)}, bf16[512,1024]{1,0:T(8,128)(2,1)}, u32[]{:S(2)}) copy-start(bf16[512,1024]{1,0:T(8,128)(2,1)} %get-tuple-element.59) | copy-start | bytes 3145732
  282.3 3.4 %copy-start = (bf16[256,4096]{1,0:T(8,128)(2,1)S(1)}, bf16[256,4096]{1,0:T(8,128)(2,1)}, u32[]{:S(2)}) copy-start(bf16[256,4096]{1,0:T(8,128)(2,1)} %get-tuple-element.58) | copy-start | bytes 6291460
  285.7 2.5 copy-start.2
  285.7 3.3 %copy-start.3 = (bf16[256,1024]{1,0:T(8,128)(2,1)S(1)}, bf16[256,1024]{1,0:T(8,128)(2,1)}, u32[]{:S(2)}) copy-start(bf16[256,1024]{1,0:T(8,128)(2,1)} %get-tuple-element.56) | copy-start | bytes 1572868

commit v5 on v4

--- a/solution.py
+++ b/solution.py
@@ -27,15 +27,28 @@
     return v * s, s * (1.0 + v * (1.0 - s))
 
 
+def rows_sum(stack, value, rising):
+    row = lax.broadcasted_iota(jnp.int32, value.shape, 0)
+    level = 0
+    while stack and stack[-1][0] == level:
+        _, other = stack.pop()
+        first, second = (other, value) if rising else (value, other)
+        low = (row & (1 << level)) == 0
+        turned = pltpu.roll(jnp.where(low, second, first), 1 << level, 0)
+        value = jnp.where(low, first, second) + turned
+        level += 1
+    stack.append((level, value))
+
+
 def front_kernel(
     span,
     x, og, lengths, taps_own, log_own, cbias_own, dbias_own, skip_own, gain_own,
     in_own, out_own, xp_own, dt_own,
-    hidden_out, step_low, final, bbd,
-    held_all, normed_full, bg_full, lead_full, slope_full, u_full, sig_full, delta_full,
+    hidden_out, step_low, final,
+    held_all, normed_full, bg_full, lead_full, slope_full, u_full, sig_full, delta_full, bw_full,
     cw_full, dy_full, gated_full, zg_full, in_full, xp_full, dt_full, small_full,
     in_w, out_w, xp, dt, small, small_own, hx, acc, zacc, normed, v, proj, ends, sums,
-    ends_in, sums_in, bg, mask, lead, slope, u, sig, delta, bw, cw, cbd, gg, dy, y, gated, zg,
+    ends_in, sums_in, bg, mask, lead, slope, u, sig, delta, bw, cw, gg, dy, y, gated, zg,
     start, held,
     send, recv, halo, relay_send, relay_recv, sums_send, sums_recv, local, keep, held_sem,
 ):
@@ -294,15 +307,6 @@
         return carry
 
     lax.fori_loop(0, rows // GROUP, wide_step, 0)
-    r = lax.broadcasted_iota(jnp.int32, (rows, GROUP * state), 0)
-    k = lax.broadcasted_iota(jnp.int32, (rows, GROUP * state), 1)
-    mine = lax.rem(r, GROUP) == k // state
-    at = lax.broadcasted_iota(jnp.int32, (proj.shape[1], GROUP * state), 0)
-    col = lax.rem(lax.broadcasted_iota(jnp.int32, (proj.shape[1], GROUP * state), 1), state)
-    for ref, first in ((bbd, rank), (cbd, rank + state)):
-        spread = (at == col + first).astype(F32).astype(BF16)
-        ref[...] = jnp.where(mine, dot(proj[...].astype(BF16), spread), 0.0).astype(BF16)
-
     def delta_step(t, carry):
         cols = columns(t)
         for c in range(seqs):
@@ -401,6 +405,7 @@
         (0, (normed.at[:rows], normed_full)), (1, (bg, bg_full)), (2, (lead, lead_full)),
         (3, (slope, slope_full)), (4, (u, u_full)), (5, (sig, sig_full)), (6, (delta, delta_full)),
         (7, (cw, cw_full)), (8, (xp, xp_full)), (9, (dt, dt_full)), (10, (small, small_full)),
+        (15, (bw, bw_full)),
     )
 
     def ends_wait(j, c):
@@ -466,16 +471,21 @@
         def one(i, h):
             h = list(h)
             g = c * groups + i
-            for k in range(GROUP):
-                b_in = bw[c, i * GROUP + k]
+            for first_row in range(0, GROUP, 8):
+                stacks = [[] for _ in cuts]
+                for k in range(first_row, first_row + 8):
+                    b_in, read = bw[c, i * GROUP + k], cw[c, i * GROUP + k]
+                    for n, cut in enumerate(cuts):
+                        step = jnp.broadcast_to(delta[g, k : k + 1, cut], (state, LANES))
+                        row = jnp.broadcast_to(v[g, k : k + 1, cut], (state, LANES))
+                        h[n] = jnp.exp2(step * rates[n]) * h[n] + row * b_in
+                        held[slot, i * GROUP + k + 1, :, tiles[n]] = h[n].astype(BF16)
+                        part = h[n] * read
+                        rows_sum(stacks[n], part[:8] + part[8:], True)
                 for n, cut in enumerate(cuts):
-                    step = jnp.broadcast_to(delta[g, k : k + 1, cut], (state, LANES))
-                    row = jnp.broadcast_to(v[g, k : k + 1, cut], (state, LANES))
-                    h[n] = jnp.exp2(step * rates[n]) * h[n] + row * b_in
-                    held[slot, i * GROUP + k + 1, :, tiles[n]] = h[n].astype(BF16)
-            states = held[slot, pl.ds(i * GROUP + 1, GROUP)].reshape(GROUP * state, CHUNK)
+                    y[g, first_row : first_row + 8, cut] = stacks[n][0][1]
             tok = pl.ds(pl.multiple_of(g * GROUP, GROUP), GROUP)
-            y[g, :, all_cols] = dot(cbd[tok], states) + skip * u[tok, all_cols].astype(F32)
+            y[g, :, all_cols] += skip * u[tok, all_cols].astype(F32)
             return tuple(h)
 
         lax.fori_loop(0, groups, one, h)
@@ -590,6 +600,7 @@
         ((rows, inner), BF16),
         (grouped, F32),
         ((seqs, ctx, state, LANES), F32),
+        ((seqs, ctx, state, LANES), F32),
         (grouped, F32),
         ((rows, inner), BF16),
         ((parts, rows, CHUNK), BF16),
@@ -604,12 +615,11 @@
         in_specs=[whole, whole, pl.BlockSpec(memory_space=pltpu.SMEM)]
         + [whole] * 6
         + [anywhere] * 4,
-        out_specs=[whole] * 4 + [anywhere] * (1 + len(kept)),
+        out_specs=[whole] * 3 + [anywhere] * (1 + len(kept)),
         out_shape=[
             shape((rows, width), BF16),
             shape((rows, rank), BF16),
             shape((seqs, state, inner), F32),
-            shape((rows, GROUP * state), BF16),
             shape((seqs * parts,) + held, BF16),
         ]
         + [shape(*k) for k in kept],
@@ -639,7 +649,6 @@
             vmem(grouped, F32),
             vmem((seqs, ctx, state, LANES), F32),
             vmem((seqs, ctx, state, LANES), F32),
-            vmem((rows, GROUP * state), BF16),
             vmem((rows, inner), F32),
             vmem(grouped, F32),
             vmem(grouped, F32),
@@ -667,13 +676,13 @@
 
 def back_kernel(
     span, state, rank,
-    gated, bg, step_low, final, bbd, ones, small, x, og,
-    held_all, normed_full, lead_full, slope_full, u_full, sig_full, delta_full,
+    gated, bg, step_low, final, small, x, og,
+    held_all, normed_full, lead_full, slope_full, u_full, sig_full, delta_full, bw_full,
     cw_full, dy_full, zg_full, in_full, xp_full, dt_full,
     input_grad, out_sum, in_sum, rest_sum,
-    normed, lead, slope, u, sig, delta, cw, dy, mixed, xp, dt, in_w, held, gs, ws, rl, cacc,
+    normed, lead, slope, u, sig, delta, bw, cw, dy, mixed, xp, dt, in_w, held, v, rl, cacc,
     bacc, logs, sums,
-    pg, cg, ng, rest, g, ra, rx, ry, zlo, zhi, tot,
+    pg, pg_full, cg, ng, rest, g, ra, rx, ry, zlo, zhi, tot,
     send, recv, halo, local, load, held_sem, in_sem,
 ):
     d, s, f = (lax.axis_index(a) for a in ("dp", "seq", "fsdp"))
@@ -700,7 +709,7 @@
 
     loads = (
         (mixed.at[:parts], zg_full), (normed, normed_full), (delta, delta_full), (dy, dy_full),
-        (u, u_full), (cw, cw_full), (sig, sig_full), (slope, slope_full),
+        (u, u_full), (cw, cw_full), (bw, bw_full), (sig, sig_full), (slope, slope_full),
         (lead, lead_full), (xp, xp_full), (dt, dt_full),
     )
     loads = [pltpu.make_async_copy(src, dst, load.at[n]) for n, (dst, src) in enumerate(loads)]
@@ -715,10 +724,10 @@
         return pltpu.make_async_copy(in_full.at[:, pl.ds(first, CHUNK)], in_w.at[slot], in_sem.at[slot])
 
     held_copy(0).start()
-    for one in loads[2:6]:
+    for one in loads[2:7]:
         one.start()
     held_copy(1).start()
-    for one in loads[:2] + loads[6:]:
+    for one in loads[:2] + loads[7:]:
         one.start()
     cg[:, ctx:] = jnp.zeros((seqs, cg.shape[1] - ctx, inner), F32)
     barrier = pltpu.get_barrier_semaphore()
@@ -890,25 +899,39 @@
             at = c * groups + i
             tok = pl.ds(pl.multiple_of(at * GROUP, GROUP), GROUP)
             p, total, kept = (list(value) for value in carry)
-            for k in reversed(range(GROUP)):
-                t = i * GROUP + k
-                read = cw[c, t]
-                for n, cut in enumerate(cuts):
-                    row = lambda ref: jnp.broadcast_to(ref[at, k : k + 1, cut], (state, LANES))
-                    step = row(delta)
-                    grad = read * row(dy) + p[n]
-                    p[n] = jnp.exp2(step * rates[n]) * grad
-                    w = p[n] * held[slot, t, :, tiles[n]].astype(F32)
-                    total[n] = total[n] + w * step
-                    gs[k, :, tiles[n]] = grad.astype(BF16)
-                    ws[k, :, tiles[n]] = (w * rates[n]).astype(BF16)
-            grads = gs[...].reshape(GROUP * state, CHUNK)
-            states = held[slot, pl.ds(i * GROUP + 1, GROUP)].reshape(GROUP * state, CHUNK)
-            drive_grad = dot(bbd[tok], grads)
-            delta_part = dot(ones[...], ws[...].reshape(GROUP * state, CHUNK))
             value, out, gain = u[tok, cols].astype(F32), dy[at, :, cols], delta[at, :, cols]
-            bacc[tok] += dot((gain * value).astype(BF16), grads, across)
-            cacc[tok] += dot(out.astype(BF16), states, across)
+            v[...] = gain * value
+            drive_parts, delta_parts = [[], []], [[], []]
+            for pair in range(0, len(cuts), 2):
+                which = range(pair, pair + 2)
+                after = {n: held[slot, (i + 1) * GROUP, :, tiles[n]].astype(F32) for n in which}
+                for half in (1, 0):
+                    drives, deltas = ({n: [] for n in which} for _ in range(2))
+                    for k in reversed(range(half * 8, half * 8 + 8)):
+                        t = i * GROUP + k
+                        b_in, read = bw[c, t], cw[c, t]
+                        b_part = c_part = 0.0
+                        for n in which:
+                            row = lambda tile: jnp.broadcast_to(tile, (state, LANES))
+                            step, back = row(delta[at, k : k + 1, cuts[n]]), row(dy[at, k : k + 1, cuts[n]])
+                            grad = read * back + p[n]
+                            p[n] = jnp.exp2(step * rates[n]) * grad
+                            before = held[slot, t, :, tiles[n]].astype(F32)
+                            w = p[n] * before
+                            total[n] = total[n] + w * step
+                            part = w * rates[n]
+                            rows_sum(deltas[n], part[:8] + part[8:], False)
+                            part = grad * b_in
+                            rows_sum(drives[n], part[:8] + part[8:], False)
+                            b_part = b_part + grad * row(v[k : k + 1, tiles[n]])
+                            c_part = c_part + after[n] * back
+                            after[n] = before
+                        bacc[c * ctx + t] += b_part
+                        cacc[c * ctx + t] += c_part
+                    drive_parts[half] += [drives[n][0][1] for n in which]
+                    delta_parts[half] += [deltas[n][0][1] for n in which]
+            joined = lambda halves: jnp.concatenate([jnp.concatenate(h, 1) for h in halves], 0)
+            drive_grad, delta_part = joined(drive_parts), joined(delta_parts)
             raw_grad = drive_grad * value + delta_part * (1.0 / LOG2E)
             raw_grad = raw_grad * sig[tok, cols].astype(F32)
             rl[tok, cols] = raw_grad.astype(BF16)
@@ -932,16 +955,22 @@
 
     def proj_work():
         step_grad = dot(rl[...], dt[...], across)
-        r = lax.broadcasted_iota(jnp.int32, (rows, GROUP * state), 0)
-        k = lax.broadcasted_iota(jnp.int32, (rows, GROUP * state), 1)
-        own = lax.rem(r, GROUP) == k // state
-        pick = lambda v: jnp.where(own, v[...], 0.0).astype(BF16)
-        at = lax.rem(lax.broadcasted_iota(jnp.int32, (GROUP * state, LANES), 0), state)
-        col = lax.broadcasted_iota(jnp.int32, (GROUP * state, LANES), 1)
-        fold = lambda first: (col == at + first).astype(F32).astype(BF16)
-        grads = jnp.concatenate([step_grad, jnp.zeros((rows, LANES - rank), F32)], 1)
-        grads = grads + dot(pick(bacc), fold(rank)) + dot(pick(cacc), fold(rank + state))
-        pg[...] = grads.astype(BF16)
+        col = lax.broadcasted_iota(jnp.int32, (state, LANES), 1)
+        n = lax.broadcasted_iota(jnp.int32, (state, LANES), 0)
+        ones = jnp.ones((LANES, LANES), BF16)
+
+        def one(r, carry):
+            tok = pl.ds(pl.multiple_of(r * GROUP, GROUP), GROUP)
+            total = pg_full[tok]
+            for ref, first in ((bacc, rank), (cacc, rank + state)):
+                value = dot(ref[tok].reshape(GROUP * state, LANES).astype(BF16), ones)
+                keep = jnp.where(col == n + first, value.reshape(GROUP, state, LANES), 0.0)
+                total = total + jnp.sum(keep, 1)
+            pg[tok] = total.astype(BF16)
+            return carry
+
+        pg_full[...] = jnp.concatenate([step_grad, jnp.zeros((rows, LANES - rank), F32)], 1)
+        lax.fori_loop(0, rows // GROUP, one, 0)
 
     def weight_work():
         first = TAPS + state + 4
@@ -968,7 +997,7 @@
             for c in range(seqs):
                 tok = slice(c * ctx, (c + 1) * ctx)
                 weight = xp[columns(t)]
-                back = dot(pg[tok, : weight.shape[1]], weight, across)
+                back = dot(pg[tok], weight, across)
                 own = range(c * ctx // GROUP, (c + 1) * ctx // GROUP)
                 grad = jnp.concatenate([dy[at, :, cols] for at in own], 0) + back
                 grad = grad * slope[tok, cols].astype(F32)
@@ -1139,7 +1168,7 @@
         one.wait()
 
 
-def back(gated, bg, step_low, final, bbd, small, x, og, far):
+def back(gated, bg, step_low, final, small, x, og, far):
     rows, inner = gated.shape
     width = x.shape[1]
     seqs, state = final.shape[:2]
@@ -1147,16 +1176,15 @@
     span = lax.axis_size("seq")
     out_chunks, in_chunks = 2 * width // CHUNK, 2 * parts
     n = out_chunks + in_chunks + 1
-    ones = jnp.asarray(np.kron(np.eye(GROUP), np.ones((1, state))), BF16)
     vmem, dma = pltpu.VMEM, pltpu.SemaphoreType.DMA
     anywhere = pl.BlockSpec(memory_space=pl.ANY)
     whole = pl.BlockSpec(memory_space=vmem)
     shape = jax.ShapeDtypeStruct
     like = lambda v: vmem(v.shape, v.dtype)
-    (held, normed, lead, slope, u, sig, delta, cw, dy, zg, in_full, xp, dt) = far
+    (held, normed, lead, slope, u, sig, delta, bw, cw, dy, zg, in_full, xp, dt) = far
     return pl.pallas_call(
         functools.partial(back_kernel, span, state, rank),
-        in_specs=[whole] * 9 + [anywhere] * len(far),
+        in_specs=[whole] * 7 + [anywhere] * len(far),
         out_specs=[whole, anywhere, anywhere, anywhere],
         out_shape=[
             shape((rows, width), BF16),
@@ -1165,20 +1193,20 @@
             shape((2 * HR, CHUNK), BF16),
         ],
         scratch_shapes=[
-            *map(like, (normed, lead, slope, u, sig, delta, cw, dy)),
+            *map(like, (normed, lead, slope, u, sig, delta, bw, cw, dy)),
             vmem((in_chunks, rows, CHUNK), BF16),
             like(xp),
             like(dt),
             vmem((2, width, CHUNK), BF16),
             vmem((2,) + held.shape[1:], BF16),
-            vmem((GROUP, state, CHUNK), BF16),
-            vmem((GROUP, state, CHUNK), BF16),
+            vmem((GROUP, CHUNK), F32),
             vmem((rows, inner), BF16),
-            vmem((rows, GROUP * state), F32),
-            vmem((rows, GROUP * state), F32),
+            vmem((rows, state, LANES), F32),
+            vmem((rows, state, LANES), F32),
             vmem((state, inner), F32),
             vmem((2, 8, inner), F32),
             vmem((rows, LANES), BF16),
+            vmem((rows, LANES), F32),
             vmem((seqs, ctx + 8, inner), F32),
             vmem((rows, width), F32),
             vmem((2 * HR, inner), F32),
@@ -1193,7 +1221,7 @@
             dma((12, n)),
             dma((2,)),
             dma((n, 2)),
-            dma((11,)),
+            dma((12,)),
             dma((2,)),
             dma((2,)),
         ],
@@ -1201,7 +1229,43 @@
             collective_id=1, has_side_effects=True, vmem_limit_bytes=63 << 20
         ),
         name="back",
-    )(gated, bg, step_low, final, bbd, ones, small, x, og, *far)
+    )(gated, bg, step_low, final, small, x, og, *far)
+
+
+def finish_kernel(state, rank, used, in_sum, out_sum, rest, gain, in_w, taps, cbias, xp, dt, dbias, logs, skip, out_w):
+    in_w[...] = in_sum[...].astype(F32)
+    out_w[...] = out_sum[...].astype(F32)
+    at = TAPS + state
+    row = lambda first, count=1: rest[...].astype(F32)[first : first + count]
+    taps[...] = row(0, TAPS)
+    logs[...] = row(TAPS, state)
+    cbias[...] = row(at)
+    dbias[...] = row(at + 1)
+    skip[...] = row(at + 2)
+    gain[...] = row(at + 3)[:, : gain.shape[1]]
+    dt[...] = row(at + 4, rank)
+    xp[...] = row(at + 4 + rank, used).T
+
+
+def finish(in_sum, out_sum, rest, state, rank, used):
+    steps = 4
+    share = rest.shape[1]
+    tall = lambda v: pl.BlockSpec((v.shape[0] // steps, v.shape[1]), lambda i: (i, 0))
+    fixed = lambda *v: pl.BlockSpec(v, lambda i: (0, 0))
+    small = [(1, in_sum.shape[0]), (TAPS, share), (1, share), (share, used), (rank, share)]
+    small += [(1, share), (state, share), (1, share)]
+    shape = lambda v: jax.ShapeDtypeStruct(v, F32)
+    return pl.pallas_call(
+        functools.partial(finish_kernel, state, rank, used),
+        grid=(steps,),
+        in_specs=[tall(in_sum), tall(out_sum), fixed(*rest.shape)],
+        out_specs=[fixed(*small[0]), tall(in_sum)] + [fixed(*v) for v in small[1:]] + [tall(out_sum)],
+        out_shape=[shape(small[0]), shape(in_sum.shape)]
+        + [shape(v) for v in small[1:]]
+        + [shape(out_sum.shape)],
+        compiler_params=pltpu.CompilerParams(vmem_limit_bytes=32 << 20),
+        name="finish",
+    )(in_sum, out_sum, rest)
 
 
 def body(
@@ -1215,28 +1279,29 @@
     rows = ctx * seqs
     row = lambda v: v.reshape(1, -1)
     x, og = hidden_in.reshape(rows, width), out_grad.reshape(rows, width)
+    used = xproj_weight.shape[1]
+    xp_own = jnp.pad(xproj_weight, ((0, 0), (0, LANES - used)))
     (
-        hidden_out, step_low, final, bbd, held, normed, branch_grad, lead, slope, u, sig, delta,
-        c_wide, y_grad, gated, z_grad, in_matrix, proj_matrix, step_matrix, small,
+        hidden_out, step_low, final, held, normed, branch_grad, lead, slope, u, sig, delta,
+        b_wide, c_wide, y_grad, gated, z_grad, in_matrix, proj_matrix, step_matrix, small,
     ) = front(
         x, og, lengths, conv_weight, a_log, row(conv_bias), row(dt_bias), row(skip_gain),
-        row(norm_gain), in_weight, out_weight, xproj_weight, dt_weight, seqs,
+        row(norm_gain), in_weight, out_weight, xp_own, dt_weight, seqs,
     )
     far = (
-        held, normed, lead, slope, u, sig, delta, c_wide, y_grad, z_grad, in_matrix,
+        held, normed, lead, slope, u, sig, delta, b_wide, c_wide, y_grad, z_grad, in_matrix,
         proj_matrix, step_matrix,
     )
     input_grad, out_sum, in_sum, rest = back(
-        gated, branch_grad, step_low, final, bbd, small, x, og, far
+        gated, branch_grad, step_low, final, small, x, og, far
     )
-    rest = rest.astype(F32)
-    shards = lax.axis_size("fsdp")
-    at = taps + state
+    gain, in_w, taps_grad, cbias, proj_w, step_w, dbias, logs, skip, out_w = finish(
+        in_sum, out_sum, rest, state, rank, used
+    )
+    flat = lambda v: v.reshape(-1)
     return (
-        hidden_out.reshape(seqs, ctx, width), input_grad.reshape(seqs, ctx, width),
-        rest[at + 3, : width // shards], in_sum.astype(F32), rest[:taps], rest[at],
-        rest[at + 4 + rank : at + 4 + rank + proj_matrix.shape[1]].T, rest[at + 4 : at + 4 + rank],
-        rest[at + 1], rest[taps:at], rest[at + 2], out_sum.astype(F32),
+        hidden_out.reshape(seqs, ctx, width), input_grad.reshape(seqs, ctx, width), flat(gain), in_w,
+        taps_grad, flat(cbias), proj_w, step_w, flat(dbias), logs, flat(skip), out_w,
     )
 
 

time: 290 us -> 269 us (0.928)
  Pallas kernels: 273 us -> 260 us
  other arithmetic: 5.22 us -> 0 us
  local copies, waits for them, and re-layouts: 10.8 us -> 7.85 us
    pallas_call x1, Pallas kernels: 141 us -> 128 us  [back(): pl.pallas_call(functools.partial(back_kernel, span, state, rank), in_spec...]
    slice x5 -> x0, local copies, waits for them, and re-layouts: 6.88 us -> none  [the longest x1 1.5 us: body(): rest[at + 4:at + 4 + rank]]
    convert_element_type x3 -> x0, other arithmetic: 5.22 us -> none  [the longest x1 2.5 us: body(): in_sum.astype(F32)]
    unnamed x11 -> x14, local copies, waits for them, and re-layouts: 3.25 us -> 7.16 us
    pallas_call x1, Pallas kernels: 132 us -> 129 us  [front(): pl.pallas_call(functools.partial(front_kernel, span), in_specs=[whole, wh...]
    pallas_call x0 -> x1, Pallas kernels: none -> 3.02 us  [finish(): pl.pallas_call(functools.partial(finish_kernel, state, rank, used), grid=...]
where the time goes in v5:
time: 269 us; the launch traced here: 268 us
  Pallas kernels  260 us (97%)
  local copies, waits for them, and re-layouts  7.85 us (3%)
    pallas_call x1, Pallas kernels, front(): pl.pallas_call(functools.partial(front_kernel, span), in_specs=[whole, wh...  129 us
    pallas_call x1, Pallas kernels, back(): pl.pallas_call(functools.partial(back_kernel, span, state, rank), in_spec...  128 us
    unnamed x14, local copies, waits for them, and re-layouts  7.16 us

profile of v5, /device:TPU:25, one launch (start us, length us, event | category | flops | bytes accessed | tf_op | source)
XLA Modules:
  0.0 268.3 jit_solution(1002954649838090047)
XLA Ops:
  0.6 1.0 copy.25
  1.7 0.7 pad.4.xp_own
  2.3 128.8 %front.1 = (bf16[256,1024]{1,0:T(8,128)(2,1)}, bf16[256,64]{1,0:T(8,128)(2,1)}, f32[2,16,2048]{2,1,0:T(8,128)}, bf16[8,129,16,512]{3,2,1,0:T(8,128)(2,1)}, bf16[...) custom-call(bf16[256,1024]{1,0:T(8,128)(2,1)} %bitcast.12, ...), custom_call_target="tpu_custom_call" | custom-call | tf_op jit(solution)/shard_map/front/pallas_call | solution.py:613
  131.1 0.0 copy-start.3
  131.1 127.9 %back.1 = (bf16[256,1024]{1,0:T(8,128)(2,1)}, bf16[512,1024]{1,0:T(8,128)(2,1)}, bf16[256,4096]{1,0:T(8,128)(2,1)}, bf16[256,512]{1,0:T(8,128)(2,1)}) custom-call(bf16[256,2048]{1,0:T(8,128)(2,1)} %get-tuple-element.47.gated, bf16[256,1024]{1,0:T(8,128)(2,1)} %get-tuple-element.48.bg, bf16[256,64]{1,0:T(8,128)(2,1)} %get-tuple-element.49.step_low, ...), custom_call_target="tpu_custom_call" | custom-call | tf_op jit(solution)/shard_map/back/pallas_call | solution.py:1185
  259.1 0.0 copy-start
  259.1 1.6 copy-done
  260.7 0.0 copy-start.1
  260.7 1.2 copy-done.1
  261.9 0.0 copy-start.2
  261.9 0.9 copy-done.2
  262.8 0.0 copy-start.4
  262.8 3.0 %finish.1 = (f32[1,256]{1,0:T(1,128)}, f32[256,4096]{1,0:T(8,128)}, f32[4,512]{1,0:T(4,128)}, f32[1,512]{1,0:T(1,128)}, f32[512,96]{1,0:T(8,128)S(1)}, /*index=5...) custom-call(bf16[256,4096]{1,0:T(8,128)(2,1)S(1)} %copy-done, ...), custom_call_target="tpu_custom_call" | custom-call | tf_op jit(solution)/shard_map/finish/pallas_call | solution.py:1258
  265.9 0.8 copy.26
  266.7 0.0 copy-done.3
  266.7 0.8 copy.29
  267.5 0.0 copy-done.4
  267.5 0.8 copy.30
Async XLA Ops:
  131.1 135.5 %copy-start.3 = (bf16[256,1024]{1,0:T(8,128)(2,1)S(1)}, bf16[256,1024]{1,0:T(8,128)(2,1)}, u32[]{:S(2)}) copy-start(bf16[256,1024]{1,0:T(8,128)(2,1)} %get-tuple-element.46) | copy-start | bytes 1572868
  259.1 1.6 copy-start
  260.7 1.2 copy-start.1
  261.9 0.9 copy-start.2
  262.8 4.6 %copy-start.4 = (bf16[256,1024]{1,0:T(8,128)(2,1)S(1)}, bf16[256,1024]{1,0:T(8,128)(2,1)}, u32[]{:S(2)}) copy-start(bf16[256,1024]{1,0:T(8,128)(2,1)} %get-tuple-element.66) | copy-start | bytes 1572868

commit v6 on v5

--- a/solution.py
+++ b/solution.py
@@ -20,6 +20,7 @@
 CHUNK = 512
 SLACK = 1
 TAPS = 4
+HELD = 3
 
 
 def silu_parts(v):
@@ -54,7 +55,7 @@
 ):
     d, s, f = (lax.axis_index(a) for a in ("dp", "seq", "fsdp"))
     fx, fy, fd = f ^ 1, f ^ 2, f ^ 3
-    tox, toy, sib = {"fsdp": fx}, {"fsdp": fy}, {"dp": 1 - d}
+    tox, toy, tod, sib = {"fsdp": fx}, {"fsdp": fy}, {"fsdp": fd}, {"dp": 1 - d}
     rows, width = x.shape
     inner = u.shape[1]
     seqs = bw.shape[0]
@@ -71,7 +72,7 @@
     for c in range(seqs):
         hx[c] = jnp.zeros((GROUP, width), BF16)
     barrier = pltpu.get_barrier_semaphore()
-    for who in (tox, toy, sib):
+    for who in (tox, toy, tod, sib):
         pl.semaphore_signal(barrier, inc=1, device_id=who, device_id_type=MESH)
 
     def greet(o, carry):
@@ -87,7 +88,7 @@
     small_own[at_bias + 1 : at_bias + 2] = dbias_own[...]
     small_own[at_bias + 2 : at_bias + 3] = skip_own[...]
     small_own[at_bias + 3 : at_bias + 4, : width // 4] = gain_own[...]
-    pl.semaphore_wait(barrier, 2 + span)
+    pl.semaphore_wait(barrier, 3 + span)
 
     SMALL, STREAM, PROJ, STEP, GATE, OUT = range(6)
     plan = (
@@ -129,10 +130,30 @@
         one.start()
         started.append(one)
 
-    def start_own(p):
+    def start_own(p, routed=False):
         for q in (0, 1):
             go(copy(own(p, d, q), window(p, f, d, q), p, q, tox))
             go(copy(own(p, d, 1 - q), window(p, f, d, 1 - q), p, 3 - q, toy))
+        if routed:
+            for q in (0, 1):
+                go(copy(own(p, d, q), window(p, f, d, q), p, 4 + q, tod))
+
+    def small_copy(at, owner, part, who):
+        rows_of = slice(*((at_bias - at_bias % 8, at_bias + 4), (0, at_bias - at_bias % 8))[part])
+        cols = pl.ds(pl.multiple_of(owner * share, share), share)
+        return pltpu.make_async_remote_copy(
+            src_ref=small_own.at[rows_of], dst_ref=small.at[rows_of, cols],
+            send_sem=send.at[SMALL, 3 * part + at], recv_sem=recv.at[SMALL, 3 * part + at],
+            device_id=who, device_id_type=MESH,
+        )
+
+    def small_start(part):
+        for at, who in enumerate((tox, toy, tod)):
+            go(small_copy(at, f, part, who))
+
+    def small_ready(part):
+        for at, owner in enumerate((fx, fy, fd)):
+            small_copy(at, owner, part, sib).wait_recv()
 
     def place_own(p):
         for half in (0, 1):
@@ -156,12 +177,12 @@
     near = ((0, fx, 0), (3, fy, 1), (1, fx, 1), (2, fy, 0))
     diagonal = ((4, fd, 0), (5, fd, 1))
 
-    def serve_near(p):
+    def serve_near(p, routed=False):
         for kind, owner, q in near:
             w = arrived(p, kind, owner, d, q)
-            if kind == 0:
+            if kind == 0 and not routed:
                 go(copy(w, w, p, 4, toy))
-            if kind == 3:
+            if kind == 3 and not routed:
                 go(copy(w, w, p, 5, tox))
             go(copy(w, w, p, 6 + kind, sib))
 
@@ -178,10 +199,13 @@
         for kind, owner, q in diagonal:
             arrived(p, 6 + kind, owner, 1 - d, q)
 
-    for p in (SMALL, STREAM, PROJ, STEP):
-        start_own(p)
-    for p in range(6):
+    small_start(0)
+    start_own(STREAM)
+    for p in (STREAM, PROJ, STEP, GATE, OUT):
         place_own(p)
+    pltpu.make_async_copy(
+        small_own, small.at[:, pl.ds(pl.multiple_of(f * share, share), share)], local.at[SMALL, 0]
+    ).start()
     def edges(c):
         return pltpu.make_async_remote_copy(
             src_ref=x.at[(c + 1) * ctx - GROUP : (c + 1) * ctx], dst_ref=hx.at[c],
@@ -206,11 +230,10 @@
 
     lax.fori_loop(0, rows // GROUP, mask_step, 0)
 
-    serve_near(SMALL)
-    serve_far(SMALL)
-    near_ready(SMALL)
-    far_ready(SMALL)
-    own_ready(SMALL)
+    pltpu.make_async_copy(
+        small_own, small.at[:, pl.ds(pl.multiple_of(f * share, share), share)], local.at[SMALL, 0]
+    ).wait()
+    small_ready(0)
 
     @pl.when(s > 0)
     def _():
@@ -253,17 +276,17 @@
     own_ready(STREAM)
     project(acc, tall, 0, f, True)
     serve_near(STREAM)
+    small_start(1)
+    start_own(PROJ, True)
+    start_own(STEP, True)
     start_own(GATE)
-    start_own(OUT)
     near_ready(STREAM)
     project(acc, tall, 0, fx, False)
     project(acc, tall, 0, fy, False)
     serve_far(STREAM)
-    for p in (PROJ, STEP):
-        serve_near(p)
-        serve_far(p)
     far_ready(STREAM)
     project(acc, tall, 0, fd, False)
+    small_ready(1)
 
     tile = 2 * LANES
 
@@ -289,6 +312,9 @@
 
     lax.fori_loop(0, inner // tile, conv_step, 0)
     for p in (PROJ, STEP):
+        serve_near(p, True)
+        serve_far(p)
+    for p in (PROJ, STEP):
         near_ready(p)
         far_ready(p)
         own_ready(p)
@@ -426,10 +452,12 @@
 
         lax.fori_loop(0, inner // CHUNK, one, 0)
 
-    def join_start(j, carry):
-        for c in range(seqs):
+    def join_start(c):
+        def one(j, carry):
             join(start, j, c)
-        return carry
+            return carry
+
+        lax.fori_loop(0, s, one, 0)
 
     def join_final(o, carry):
         for c in range(seqs):
@@ -448,11 +476,11 @@
     blocks = seqs * parts
 
     def held_copy(b):
-        slot = lax.rem(b, 2)
+        slot = lax.rem(b, HELD)
         return pltpu.make_async_copy(held.at[slot], held_all.at[b], held_sem.at[slot])
 
     def sweep_block(b, carry):
-        c, slot = b // parts, lax.rem(b, 2)
+        c, slot = b // parts, lax.rem(b, HELD)
         first = lax.rem(b, parts) * CHUNK
         cuts = [pl.ds(pl.multiple_of(first + n, LANES), LANES) for n in range(0, CHUNK, LANES)]
         tiles = [slice(n, n + LANES) for n in range(0, CHUNK, LANES)]
@@ -460,9 +488,9 @@
         rates = [-jnp.exp(small[at_state:at_bias, cut]) * LOG2E for cut in cuts]
         skip = small[at_bias + 2 : at_bias + 3, all_cols]
 
-        @pl.when(b >= 2)
+        @pl.when(b >= HELD)
         def _():
-            held_copy(b - 2).wait()
+            held_copy(b - HELD).wait()
 
         h = tuple(start[c, :, cut] for cut in cuts)
         for n, cut in enumerate(tiles):
@@ -499,25 +527,29 @@
     forward_ends(0)
     ends_start(s + 1, span, 0, 0)
     serve_near(GATE)
+    start_own(OUT)
     own_ready(GATE)
     forward_ends(1)
     ends_start(s + 1, span, 0, 1)
-    near_ready(GATE)
-    for owner, fresh in ((f, True), (fx, False), (fy, False)):
-        project(zacc, rows, inner, owner, fresh)
     lax.fori_loop(1, span, sums_wait, 0)
     start[...] = jnp.zeros(start.shape, F32)
-    lax.fori_loop(0, s, join_start, 0)
-    lax.fori_loop(0, 2, sweep_block, 0)
+    join_start(0)
     serve_far(GATE)
-    lax.fori_loop(2, 4, sweep_block, 0)
+    lax.fori_loop(0, parts // 2, sweep_block, 0)
+    near_ready(GATE)
+    far_ready(GATE)
+    stash((11, (in_w, in_full)))
+
+    def gate_project(t, carry):
+        cols = columns(t, CHUNK)
+        right = in_w[:, pl.ds(pl.multiple_of(inner + t * CHUNK, CHUNK), CHUNK)]
+        zacc[:, cols] = dot(normed[:rows], right)
+        return carry
+
+    lax.fori_loop(0, parts, gate_project, 0)
     serve_near(OUT)
-    far_ready(GATE)
-    project(zacc, rows, inner, fd, False)
-    lax.fori_loop(4, blocks - 1, sweep_block, 0)
+    lax.fori_loop(parts // 2, parts, sweep_block, 0)
     serve_far(OUT)
-    stash((11, (in_w, in_full)))
-    lax.fori_loop(blocks - 1, blocks, sweep_block, 0)
     own_ready(OUT)
     near_ready(OUT)
     for owner in (f, fx, fy):
@@ -530,22 +562,33 @@
         for c in range(seqs):
             tok = slice(c * ctx, (c + 1) * ctx)
             value, grad = silu_parts(zacc[tok, cols].astype(BF16).astype(F32))
-            back = gg[tok, cols]
             pieces = [y[c * groups + i, :, cols] for i in range(groups)]
             scanned = jnp.concatenate(pieces, 0)
             gated[tok, cols] = (scanned * value).astype(BF16)
             half = pl.ds(pl.multiple_of(lax.rem(t, 2) * tile, tile), tile)
-            zg[t // 2, tok, half] = (back * scanned * grad).astype(BF16)
-            value = back * value
+            zg[t // 2, tok, half] = (gg[tok, cols] * scanned * grad).astype(BF16)
+        return carry
+
+    def back_step(t, carry):
+        cols = columns(t)
+        for c in range(seqs):
+            tok = slice(c * ctx, (c + 1) * ctx)
+            value = zacc[tok, cols].astype(BF16).astype(F32)
+            value = gg[tok, cols] * (value * jax.nn.sigmoid(value))
             for i in range(groups):
                 dy[c * groups + i, :, cols] = value[i * GROUP : (i + 1) * GROUP]
         return carry
 
-    lax.fori_loop(0, inner // tile, gate_step, 0)
-    stash((12, (dy, dy_full)), (13, (gated, gated_full)), (14, (zg, zg_full)))
+    lax.fori_loop(0, inner // tile, back_step, 0)
+    stash((12, (dy, dy_full)))
     for c in range(seqs):
         backward_ends(c)
         ends_start(0, s, 1, c)
+    for c in range(1, seqs):
+        join_start(c)
+    lax.fori_loop(parts, blocks, sweep_block, 0)
+    lax.fori_loop(0, inner // tile, gate_step, 0)
+    stash((13, (gated, gated_full)), (14, (zg, zg_full)))
 
     def hidden_step(t, carry):
         cols = columns(t)
@@ -576,7 +619,7 @@
     lax.fori_loop(1, span, sent, 0)
     for one in kept:
         one.wait()
-    for b in range(max(blocks - 2, 0), blocks):
+    for b in range(max(blocks - HELD, 0), blocks):
         held_copy(b).wait()
 
 
@@ -655,7 +698,7 @@
             vmem((rows, inner), BF16),
             vmem((parts, rows, CHUNK), BF16),
             vmem((seqs, state, inner), F32),
-            vmem((2,) + held, BF16),
+            vmem((HELD,) + held, BF16),
             dma((6, 12)),
             dma((6, 12)),
             dma((2, seqs)),
@@ -665,7 +708,7 @@
             dma((span,)),
             dma((6, 4)),
             dma((len(kept),)),
-            dma((2,)),
+            dma((HELD,)),
         ],
         compiler_params=pltpu.CompilerParams(
             collective_id=0, has_side_effects=True, vmem_limit_bytes=63 << 20

time: 269 us -> 238 us (0.88)
  Pallas kernels: 260 us -> 229 us
    pallas_call x1, Pallas kernels: 129 us -> 98.8 us  [front(): pl.pallas_call(functools.partial(front_kernel, span), in_specs=[whole, wh...]
where the time goes in v6:
time: 238 us
  Pallas kernels  229 us (96%)
  local copies, waits for them, and re-layouts  7.85 us (3%)
    pallas_call x1, Pallas kernels, back(): pl.pallas_call(functools.partial(back_kernel, span, state, rank), in_spec...  128 us
    pallas_call x1, Pallas kernels, front(): pl.pallas_call(functools.partial(front_kernel, span), in_specs=[whole, wh...  98.8 us
    unnamed x14, local copies, waits for them, and re-layouts  7.16 us

profile of v6, /device:TPU:25, one launch (start us, length us, event | category | flops | bytes accessed | tf_op | source)
XLA Modules:
  0.0 237.9 jit_solution(16986699342680176524)
XLA Ops:
  0.6 1.0 copy.25
  1.7 0.7 pad.4.xp_own
  2.3 98.8 %front.1 = (bf16[256,1024]{1,0:T(8,128)(2,1)}, bf16[256,64]{1,0:T(8,128)(2,1)}, f32[2,16,2048]{2,1,0:T(8,128)}, bf16[8,129,16,512]{3,2,1,0:T(8,128)(2,1)}, bf16[...) custom-call(bf16[256,1024]{1,0:T(8,128)(2,1)} %bitcast.12, ...), custom_call_target="tpu_custom_call" | custom-call | tf_op jit(solution)/shard_map/front/pallas_call | solution.py:656
  101.2 0.0 copy-start.3
  101.2 127.5 %back.1 = (bf16[256,1024]{1,0:T(8,128)(2,1)}, bf16[512,1024]{1,0:T(8,128)(2,1)}, bf16[256,4096]{1,0:T(8,128)(2,1)}, bf16[256,512]{1,0:T(8,128)(2,1)}) custom-call(bf16[256,2048]{1,0:T(8,128)(2,1)} %get-tuple-element.47.gated, bf16[256,1024]{1,0:T(8,128)(2,1)} %get-tuple-element.48.bg, bf16[256,64]{1,0:T(8,128)(2,1)} %get-tuple-element.49.step_low, ...), custom_call_target="tpu_custom_call" | custom-call | tf_op jit(solution)/shard_map/back/pallas_call | solution.py:1228
  228.8 0.0 copy-start
  228.8 1.6 copy-done
  230.3 0.0 copy-start.1
  230.3 1.2 copy-done.1
  231.6 0.0 copy-start.2
  231.6 0.9 copy-done.2
  232.5 0.0 copy-start.4
  232.5 3.0 %finish.1 = (f32[1,256]{1,0:T(1,128)}, f32[256,4096]{1,0:T(8,128)}, f32[4,512]{1,0:T(4,128)}, f32[1,512]{1,0:T(1,128)}, f32[512,96]{1,0:T(8,128)S(1)}, /*index=5...) custom-call(bf16[256,4096]{1,0:T(8,128)(2,1)S(1)} %copy-done, ...), custom_call_target="tpu_custom_call" | custom-call | tf_op jit(solution)/shard_map/finish/pallas_call | solution.py:1301
  235.5 0.8 copy.26
  236.3 0.0 copy-done.3
  236.3 0.8 copy.29
  237.1 0.0 copy-done.4
  237.1 0.8 copy.30
Async XLA Ops:
  101.2 135.1 %copy-start.3 = (bf16[256,1024]{1,0:T(8,128)(2,1)S(1)}, bf16[256,1024]{1,0:T(8,128)(2,1)}, u32[]{:S(2)}) copy-start(bf16[256,1024]{1,0:T(8,128)(2,1)} %get-tuple-element.46) | copy-start | bytes 1572868
  228.8 1.6 copy-start
  230.3 1.2 copy-start.1
  231.6 0.9 copy-start.2
  232.5 4.6 %copy-start.4 = (bf16[256,1024]{1,0:T(8,128)(2,1)S(1)}, bf16[256,1024]{1,0:T(8,128)(2,1)}, u32[]{:S(2)}) copy-start(bf16[256,1024]{1,0:T(8,128)(2,1)} %get-tuple-element.66) | copy-start | bytes 1572868

commit v7 on v6

--- a/solution.py
+++ b/solution.py
@@ -18,7 +18,7 @@
 MESH = pl.DeviceIdType.MESH
 HR = 128
 CHUNK = 512
-SLACK = 1
+SLACK = 2
 TAPS = 4
 HELD = 3
 
@@ -63,7 +63,7 @@
     state, rank = log_own.shape[0], dt_own.shape[0]
     groups = ctx // GROUP
     share = inner // 4
-    at_state, at_bias = TAPS, TAPS + state
+    at_bias = state + TAPS
     across = (((1,), (1,)), ((), ()))
     dot = lambda a, b, dims=(((1,), (0,)), ((), ())): lax.dot_general(
         a, b, dims, preferred_element_type=F32
@@ -82,8 +82,8 @@
 
     lax.fori_loop(1, span, greet, 0)
     small_own[...] = jnp.zeros(small_own.shape, F32)
-    small_own[:TAPS] = taps_own[...]
-    small_own[at_state:at_bias] = log_own[...]
+    small_own[:state] = log_own[...]
+    small_own[state:at_bias] = taps_own[...]
     small_own[at_bias : at_bias + 1] = cbias_own[...]
     small_own[at_bias + 1 : at_bias + 2] = dbias_own[...]
     small_own[at_bias + 2 : at_bias + 3] = skip_own[...]
@@ -139,7 +139,7 @@
                 go(copy(own(p, d, q), window(p, f, d, q), p, 4 + q, tod))
 
     def small_copy(at, owner, part, who):
-        rows_of = slice(*((at_bias - at_bias % 8, at_bias + 4), (0, at_bias - at_bias % 8))[part])
+        rows_of = slice(*((state, at_bias + 4), (0, state))[part])
         cols = pl.ds(pl.multiple_of(owner * share, share), share)
         return pltpu.make_async_remote_copy(
             src_ref=small_own.at[rows_of], dst_ref=small.at[rows_of, cols],
@@ -304,7 +304,7 @@
             total = small[at_bias : at_bias + 1, cols]
             for k in range(TAPS):
                 at = GROUP - TAPS + 1 + k
-                total = total + small[k : k + 1, cols] * held[at : at + ctx]
+                total = total + small[state + k : state + k + 1, cols] * held[at : at + ctx]
             value, grad = silu_parts(total)
             slope[c * ctx : (c + 1) * ctx, cols] = grad.astype(BF16)
             u[c * ctx : (c + 1) * ctx, cols] = value.astype(BF16)
@@ -379,7 +379,7 @@
     def forward_ends(c):
         for j in range(0, inner, CHUNK):
             cuts = [slice(j + i, j + i + LANES) for i in range(0, CHUNK, LANES)]
-            rates = [-jnp.exp(small[at_state:at_bias, cut]) * LOG2E for cut in cuts]
+            rates = [-jnp.exp(small[:state, cut]) * LOG2E for cut in cuts]
 
             def one(i, h):
                 h = list(h)
@@ -400,7 +400,7 @@
     def backward_ends(c):
         for j in range(0, inner, CHUNK):
             cuts = [slice(j + i, j + i + LANES) for i in range(0, CHUNK, LANES)]
-            rates = [-jnp.exp(small[at_state:at_bias, cut]) * LOG2E for cut in cuts]
+            rates = [-jnp.exp(small[:state, cut]) * LOG2E for cut in cuts]
 
             def one(i, carry):
                 run, p = (list(value) for value in carry)
@@ -445,7 +445,7 @@
 
         def one(t, carry):
             cols = columns(t, CHUNK)
-            rates = -jnp.exp(small[at_state:at_bias, cols]) * LOG2E
+            rates = -jnp.exp(small[:state, cols]) * LOG2E
             decay = jnp.exp2(sums_in[j, c : c + 1, cols] * rates)
             ref[c, :, cols] = decay * ref[c, :, cols] + ends_in[j, c, :, cols].astype(F32)
             return carry
@@ -485,7 +485,7 @@
         cuts = [pl.ds(pl.multiple_of(first + n, LANES), LANES) for n in range(0, CHUNK, LANES)]
         tiles = [slice(n, n + LANES) for n in range(0, CHUNK, LANES)]
         all_cols = pl.ds(pl.multiple_of(first, CHUNK), CHUNK)
-        rates = [-jnp.exp(small[at_state:at_bias, cut]) * LOG2E for cut in cuts]
+        rates = [-jnp.exp(small[:state, cut]) * LOG2E for cut in cuts]
         skip = small[at_bias + 2 : at_bias + 3, all_cols]
 
         @pl.when(b >= HELD)
@@ -741,7 +741,8 @@
     last = out_chunks + in_chunks
     slots = g.shape[0]
     q = HR // 2
-    root = (span - 1) // 2
+    roots = ((span - 1) // 2, span // 2)
+    most = span // 2
     tox, toy, sib = {"fsdp": fx}, {"fsdp": fy}, {"dp": 1 - d}
     up, down = {"seq": jnp.minimum(s + 1, span - 1)}, {"seq": jnp.maximum(s - 1, 0)}
     contract = (((0,), (0,)), ((), ()))
@@ -750,12 +751,17 @@
         a, b, dims, preferred_element_type=F32
     )
 
-    loads = (
-        (mixed.at[:parts], zg_full), (normed, normed_full), (delta, delta_full), (dy, dy_full),
-        (u, u_full), (cw, cw_full), (bw, bw_full), (sig, sig_full), (slope, slope_full),
-        (lead, lead_full), (xp, xp_full), (dt, dt_full),
-    )
-    loads = [pltpu.make_async_copy(src, dst, load.at[n]) for n, (dst, src) in enumerate(loads)]
+    parts_of = lambda v, c: v.at[pl.ds(c * (v.shape[0] // seqs), v.shape[0] // seqs)]
+    by_context = ((delta, delta_full), (dy, dy_full), (u, u_full), (cw, cw_full), (bw, bw_full), (sig, sig_full))
+    pairs = [
+        (parts_of(dst, c), parts_of(src, c)) for c in range(seqs) for dst, src in by_context
+    ]
+    first_loads = len(pairs)
+    pairs += [
+        (mixed.at[:parts], zg_full), (normed, normed_full), (slope, slope_full), (lead, lead_full),
+        (xp, xp_full), (dt, dt_full),
+    ]
+    loads = [pltpu.make_async_copy(src, dst, load.at[n]) for n, (dst, src) in enumerate(pairs)]
 
     def held_copy(b):
         slot = lax.rem(b, 2)
@@ -767,10 +773,10 @@
         return pltpu.make_async_copy(in_full.at[:, pl.ds(first, CHUNK)], in_w.at[slot], in_sem.at[slot])
 
     held_copy(0).start()
-    for one in loads[2:7]:
+    for one in loads[: len(by_context)]:
         one.start()
     held_copy(1).start()
-    for one in loads[:2] + loads[7:]:
+    for one in loads[len(by_context) :]:
         one.start()
     cg[:, ctx:] = jnp.zeros((seqs, cg.shape[1] - ctx, inner), F32)
     barrier = pltpu.get_barrier_semaphore()
@@ -802,15 +808,17 @@
     Y0 = lambda c: copy(4, c, ra.at[c, fd, hi], ry.at[c, 0], toy)
     Y2 = lambda c: copy(5, c, ra.at[c, fy, hi], ry.at[c, 2], toy)
     Y1 = lambda c: copy(6, c, ra.at[c, fy, lo], ry.at[c, 1], toy)
-    ZU = lambda c: copy(7, c, ra.at[c, f], zlo.at[c], up)
-    ZD = lambda c: copy(8, c, ra.at[c, f], zhi.at[c], down)
-    TU = lambda c: copy(9, c, tot.at[c, d], tot.at[c, d], up)
-    TD = lambda c: copy(10, c, tot.at[c, d], tot.at[c, d], down)
-    D = lambda c: copy(11, c, tot.at[c, d], tot.at[c, d], sib)
-    below, above = s < root, s > root
-    spot = jnp.where(below, s, jnp.where(above, span - 1 - s, 0))
-    far = jnp.abs(s - root)
-    most = max(root, span - 1 - root)
+    part = (lo, hi)
+    ZU = lambda c, h: copy(7 + h, c, ra.at[c, f, part[h]], zlo.at[c, part[h]], up)
+    ZD = lambda c, h: copy(9 + h, c, ra.at[c, f, part[h]], zhi.at[c, part[h]], down)
+    TU = lambda c, h: copy(11 + h, c, tot.at[c, d, part[h]], tot.at[c, d, part[h]], up)
+    TD = lambda c, h: copy(13 + h, c, tot.at[c, d, part[h]], tot.at[c, d, part[h]], down)
+    D = lambda c, h: copy(15 + h, c, tot.at[c, d, part[h]], tot.at[c, d, part[h]], sib)
+    below, above = [s < r for r in roots], [s > r for r in roots]
+    spot = [
+        jnp.where(below[h], s, jnp.where(above[h], span - 1 - s, 0)) for h in range(2)
+    ]
+    far = [jnp.abs(s - r) for r in roots]
 
     def stage(c, run):
         @pl.when((c >= 0) & (c < chunks))
@@ -856,7 +864,7 @@
         A(c).wait_recv()
         for j in range(4):
             own = g[lax.rem(c, slots), j, d]
-            ra[c, j] = (ra[c, j].astype(F32) + own.astype(F32)).astype(BF16)
+            ra[c, j] = ra[c, j] + own
         X0(c).start()
         Y0(c).start()
         X1(c).start()
@@ -864,10 +872,10 @@
 
     def second_sum(c):
         X0(c).wait_recv()
-        ra[c, fy, lo] = (ra[c, fy, lo].astype(F32) + rx[c, 0].astype(F32)).astype(BF16)
+        ra[c, fy, lo] = ra[c, fy, lo] + rx[c, 0]
         Y1(c).start()
         Y0(c).wait_recv()
-        ra[c, fx, hi] = (ra[c, fx, hi].astype(F32) + ry[c, 0].astype(F32)).astype(BF16)
+        ra[c, fx, hi] = ra[c, fx, hi] + ry[c, 0]
         X2(c).start()
 
     def third_sum(c):
@@ -875,51 +883,51 @@
         Y2(c).wait_recv()
         X2(c).wait_recv()
         Y1(c).wait_recv()
-        for k, part in enumerate((lo, hi)):
-            total = ra[c, f, part].astype(F32) + rx[c, 1 + k].astype(F32) + ry[c, 1 + k].astype(F32)
-            ra[c, f, part] = total.astype(BF16)
-
-    def inward(c):
-        @pl.when(below & (s > 0))
+        for k, piece in enumerate((lo, hi)):
+            total = ra[c, f, piece].astype(F32) + rx[c, 1 + k].astype(F32) + ry[c, 1 + k].astype(F32)
+            ra[c, f, piece] = total.astype(BF16)
+
+    def inward(c, h):
+        @pl.when(below[h] & (s > 0))
         def _():
-            ZU(c).wait_recv()
-            ra[c, f] = (ra[c, f].astype(F32) + zlo[c].astype(F32)).astype(BF16)
-
-        @pl.when(above & (s < span - 1))
+            ZU(c, h).wait_recv()
+            ra[c, f, part[h]] = ra[c, f, part[h]] + zlo[c, part[h]]
+
+        @pl.when(above[h] & (s < span - 1))
         def _():
-            ZD(c).wait_recv()
-            ra[c, f] = (ra[c, f].astype(F32) + zhi[c].astype(F32)).astype(BF16)
-
-        pl.when(below)(lambda: ZU(c).start())
-        pl.when(above)(lambda: ZD(c).start())
-
-    def at_root(c):
-        total = ra[c, f].astype(F32)
-        if root > 0:
-            ZU(c).wait_recv()
-            total = total + zlo[c].astype(F32)
-        if span - 1 > root:
-            ZD(c).wait_recv()
-            total = total + zhi[c].astype(F32)
-        tot[c, d] = total.astype(BF16)
-        if root > 0:
-            TD(c).start()
-        if span - 1 > root:
-            TU(c).start()
-        D(c).start()
-
-    def outward(c):
-        @pl.when(above)
+            ZD(c, h).wait_recv()
+            ra[c, f, part[h]] = ra[c, f, part[h]] + zhi[c, part[h]]
+
+        pl.when(below[h])(lambda: ZU(c, h).start())
+        pl.when(above[h])(lambda: ZD(c, h).start())
+
+    def at_root(c, h):
+        total = ra[c, f, part[h]].astype(F32)
+        if roots[h] > 0:
+            ZU(c, h).wait_recv()
+            total = total + zlo[c, part[h]].astype(F32)
+        if span - 1 > roots[h]:
+            ZD(c, h).wait_recv()
+            total = total + zhi[c, part[h]].astype(F32)
+        tot[c, d, part[h]] = total.astype(BF16)
+        if roots[h] > 0:
+            TD(c, h).start()
+        if span - 1 > roots[h]:
+            TU(c, h).start()
+        D(c, h).start()
+
+    def outward(c, h):
+        @pl.when(above[h])
         def _():
-            TU(c).wait_recv()
-            pl.when(s < span - 1)(lambda: TU(c).start())
-
-        @pl.when(below)
+            TU(c, h).wait_recv()
+            pl.when(s < span - 1)(lambda: TU(c, h).start())
+
+        @pl.when(below[h])
         def _():
-            TD(c).wait_recv()
-            pl.when(s > 0)(lambda: TD(c).start())
-
-        D(c).start()
+            TD(c, h).wait_recv()
+            pl.when(s > 0)(lambda: TD(c, h).start())
+
+        D(c, h).start()
 
     tile = 2 * LANES
 
@@ -933,7 +941,7 @@
         cuts = [pl.ds(pl.multiple_of(first + n, LANES), LANES) for n in range(0, CHUNK, LANES)]
         tiles = [slice(n, n + LANES) for n in range(0, CHUNK, LANES)]
         cols = pl.ds(pl.multiple_of(first, CHUNK), CHUNK)
-        rates = [-jnp.exp(small[TAPS : TAPS + state, cut]) * LOG2E for cut in cuts]
+        rates = [-jnp.exp(small[:state, cut]) * LOG2E for cut in cuts]
         skip = small[TAPS + state + 2 : TAPS + state + 3, cols]
         held_copy(b).wait()
 
@@ -953,7 +961,7 @@
                     for k in reversed(range(half * 8, half * 8 + 8)):
                         t = i * GROUP + k
                         b_in, read = bw[c, t], cw[c, t]
-                        b_part = c_part = 0.0
+                        b_parts, c_parts = [], []
                         for n in which:
                             row = lambda tile: jnp.broadcast_to(tile, (state, LANES))
                             step, back = row(delta[at, k : k + 1, cuts[n]]), row(dy[at, k : k + 1, cuts[n]])
@@ -966,11 +974,11 @@
                             rows_sum(deltas[n], part[:8] + part[8:], False)
                             part = grad * b_in
                             rows_sum(drives[n], part[:8] + part[8:], False)
-                            b_part = b_part + grad * row(v[k : k + 1, tiles[n]])
-                            c_part = c_part + after[n] * back
+                            b_parts.append(grad * row(v[k : k + 1, tiles[n]]))
+                            c_parts.append(after[n] * back)
                             after[n] = before
-                        bacc[c * ctx + t] += b_part
-                        cacc[c * ctx + t] += c_part
+                        bacc[c * ctx + t] += b_parts[0] + b_parts[1]
+                        cacc[c * ctx + t] += c_parts[0] + c_parts[1]
                     drive_parts[half] += [drives[n][0][1] for n in which]
                     delta_parts[half] += [deltas[n][0][1] for n in which]
             joined = lambda halves: jnp.concatenate([jnp.concatenate(h, 1) for h in halves], 0)
@@ -1023,8 +1031,8 @@
             cols = columns(t)
             rest[first : first + rank, cols] = dot(step_low[...], rl[:, cols], contract)
             rest[first + rank : first + rank + used, cols] = dot(pg[...], u[:, cols], contract)[:used]
-            kept = -logs[:, cols] * jnp.exp(small[TAPS : TAPS + state, cols])
-            rest[TAPS : TAPS + state, cols] = kept
+            kept = -logs[:, cols] * jnp.exp(small[:state, cols])
+            rest[:state, cols] = kept
             at = TAPS + state
             rest[at + 1 : at + 2, cols] = jnp.sum(sums[1, :, cols], 0, keepdims=True)
             rest[at + 2 : at + 3, cols] = jnp.sum(sums[0, :, cols], 0, keepdims=True)
@@ -1051,7 +1059,7 @@
                     at = GROUP - TAPS + 1 + k
                     taps[k] = taps[k] + jnp.sum(grad * before[at : at + ctx], 0, keepdims=True)
             for k in range(TAPS):
-                rest[k : k + 1, cols] = taps[k]
+                rest[state + k : state + k + 1, cols] = taps[k]
             rest[TAPS + state : TAPS + state + 1, cols] = shift
             return carry
 
@@ -1075,7 +1083,7 @@
                 total = 0.0
                 for k in range(TAPS):
                     at = TAPS - 1 - k
-                    total = total + small[k : k + 1, cols] * cg[c, at : at + ctx, cols]
+                    total = total + small[state + k : state + k + 1, cols] * cg[c, at : at + ctx, cols]
                 half = pl.ds(pl.multiple_of(lax.rem(t, 2) * tile, tile), tile)
                 mixed[parts + t // 2, c * ctx : (c + 1) * ctx, half] = total.astype(BF16)
             return carry
@@ -1130,11 +1138,16 @@
     def prepare():
         for ref in (cacc, bacc, logs, sums, rest):
             ref[...] = jnp.zeros(ref.shape, F32)
-        for one in loads[2:]:
-            one.wait()
 
     def blocks_work(i):
         pl.when(i == 0)(prepare)
+        for c in range(seqs):
+
+            @pl.when(i == c * parts)
+            def _():
+                for one in loads[c * len(by_context) : (c + 1) * len(by_context)]:
+                    one.wait()
+
         pl.when(i < blocks)(lambda: back_block(i))
 
     def late_work(i):
@@ -1161,16 +1174,19 @@
 
         @pl.when(i == out_chunks)
         def _():
-            for one in loads[:2]:
+            for one in loads[first_loads:]:
                 one.wait()
 
+        for h in range(2):
+            run = lambda f: lambda c: f(c, h)
+            away = s != roots[h]
+            pl.when(away)(lambda: stage(at(base + SLACK * (most + far[h])), run(outward)))
+            pl.when(~away)(lambda: stage(at(base + SLACK * most), run(at_root)))
+            pl.when(away)(lambda: stage(at(base + SLACK * spot[h]), run(inward)))
+        stage(at(1 + 2 * SLACK), third_sum)
+        stage(at(1 + SLACK), second_sum)
+        stage(at(1), first_sum)
         stage(at(0), produce)
-        stage(at(1), first_sum)
-        stage(at(1 + SLACK), second_sum)
-        stage(at(1 + 2 * SLACK), third_sum)
-        pl.when(s != root)(lambda: stage(at(base + SLACK * spot), inward))
-        pl.when(s == root)(lambda: stage(at(base + SLACK * most), at_root))
-        pl.when(s != root)(lambda: stage(at(base + SLACK * most + SLACK * far), outward))
         blocks_work(i)
         late_work(i)
         return carry
@@ -1181,14 +1197,15 @@
         pl.when(c >= chunks - slots)(lambda: A(c).wait_send())
         for t in (X0, X1, X2, Y0, Y1, Y2):
             t(c).wait_send()
-        pl.when(below)(lambda: ZU(c).wait_send())
-        pl.when(above)(lambda: ZD(c).wait_send())
-        if root > 0:
-            pl.when((s <= root) & (s > 0))(lambda: TD(c).wait_send())
-        if span - 1 > root:
-            pl.when((s >= root) & (s < span - 1))(lambda: TU(c).wait_send())
-        D(c).wait_send()
-        D(c).wait_recv()
+        for h, root in enumerate(roots):
+            pl.when(below[h])(lambda: ZU(c, h).wait_send())
+            pl.when(above[h])(lambda: ZD(c, h).wait_send())
+            if root > 0:
+                pl.when((s <= root) & (s > 0))(lambda: TD(c, h).wait_send())
+            if span - 1 > root:
+                pl.when((s >= root) & (s < span - 1))(lambda: TU(c, h).wait_send())
+            D(c, h).wait_send()
+            D(c, h).wait_recv()
         return carry
 
     lax.fori_loop(0, chunks, finish, 0)
@@ -1260,11 +1277,11 @@
             vmem((n, HR, CHUNK), BF16),
             vmem((n, HR, CHUNK), BF16),
             vmem((n, 2, HR, CHUNK), BF16),
-            dma((12, n)),
-            dma((12, n)),
+            dma((17, n)),
+            dma((17, n)),
             dma((2,)),
             dma((n, 2)),
-            dma((12,)),
+            dma((12 + 6,)),
             dma((2,)),
             dma((2,)),
         ],
@@ -1280,8 +1297,8 @@
     out_w[...] = out_sum[...].astype(F32)
     at = TAPS + state
     row = lambda first, count=1: rest[...].astype(F32)[first : first + count]
-    taps[...] = row(0, TAPS)
-    logs[...] = row(TAPS, state)
+    logs[...] = row(0, state)
+    taps[...] = row(state, TAPS)
     cbias[...] = row(at)
     dbias[...] = row(at + 1)
     skip[...] = row(at + 2)

time: 238 us -> 204 us (0.86); the launches traced: 238 us -> 200 us
  Pallas kernels: 229 us -> 192 us
    pallas_call x1, Pallas kernels: 128 us -> 102 us  [back(): pl.pallas_call(functools.partial(back_kernel, span, state, rank), in_spec...]
    pallas_call x1, Pallas kernels: 98.8 us -> 86.7 us  [front(): pl.pallas_call(functools.partial(front_kernel, span), in_specs=[whole, wh...]
where the time goes in v7:
time: 204 us; the launch traced here: 200 us
  Pallas kernels  192 us (94%)
  local copies, waits for them, and re-layouts  7.85 us (4%)
    pallas_call x1, Pallas kernels, back(): pl.pallas_call(functools.partial(back_kernel, span, state, rank), in_spec...  102 us
    pallas_call x1, Pallas kernels, front(): pl.pallas_call(functools.partial(front_kernel, span), in_specs=[whole, wh...  86.7 us
    unnamed x14, local copies, waits for them, and re-layouts  7.16 us

profile of v7, /device:TPU:25, one launch (start us, length us, event | category | flops | bytes accessed | tf_op | source)
XLA Modules:
  0.0 200.4 jit_solution(9151058939050527624)
XLA Ops:
  0.6 1.0 copy.25
  1.7 0.7 pad.4.xp_own
  2.3 86.7 %front.1 = (bf16[256,1024]{1,0:T(8,128)(2,1)}, bf16[256,64]{1,0:T(8,128)(2,1)}, f32[2,16,2048]{2,1,0:T(8,128)}, bf16[8,129,16,512]{3,2,1,0:T(8,128)(2,1)}, bf16[...) custom-call(bf16[256,1024]{1,0:T(8,128)(2,1)} %bitcast.12, ...), custom_call_target="tpu_custom_call" | custom-call | tf_op jit(solution)/shard_map/front/pallas_call | solution.py:656
  89.1 0.0 copy-start.3
  89.1 102.1 %back.1 = (bf16[256,1024]{1,0:T(8,128)(2,1)}, bf16[512,1024]{1,0:T(8,128)(2,1)}, bf16[256,4096]{1,0:T(8,128)(2,1)}, bf16[256,512]{1,0:T(8,128)(2,1)}) custom-call(bf16[256,2048]{1,0:T(8,128)(2,1)} %get-tuple-element.47.gated, bf16[256,1024]{1,0:T(8,128)(2,1)} %get-tuple-element.48.bg, bf16[256,64]{1,0:T(8,128)(2,1)} %get-tuple-element.49.step_low, ...), custom_call_target="tpu_custom_call" | custom-call | tf_op jit(solution)/shard_map/back/pallas_call | solution.py:1245
  191.2 0.0 copy-start
  191.2 1.6 copy-done
  192.8 0.0 copy-start.1
  192.8 1.2 copy-done.1
  194.0 0.0 copy-start.2
  194.0 0.9 copy-done.2
  195.0 0.0 copy-start.4
  195.0 3.0 %finish.1 = (f32[1,256]{1,0:T(1,128)}, f32[256,4096]{1,0:T(8,128)}, f32[4,512]{1,0:T(4,128)}, f32[1,512]{1,0:T(1,128)}, f32[512,96]{1,0:T(8,128)S(1)}, /*index=5...) custom-call(bf16[256,4096]{1,0:T(8,128)(2,1)S(1)} %copy-done, ...), custom_call_target="tpu_custom_call" | custom-call | tf_op jit(solution)/shard_map/finish/pallas_call | solution.py:1318
  198.0 0.8 copy.26
  198.8 0.0 copy-done.3
  198.8 0.8 copy.29
  199.6 0.0 copy-done.4
  199.6 0.8 copy.30
Async XLA Ops:
  89.1 109.7 %copy-start.3 = (bf16[256,1024]{1,0:T(8,128)(2,1)S(1)}, bf16[256,1024]{1,0:T(8,128)(2,1)}, u32[]{:S(2)}) copy-start(bf16[256,1024]{1,0:T(8,128)(2,1)} %get-tuple-element.46) | copy-start | bytes 1572868
  191.2 1.6 copy-start
  192.8 1.2 copy-start.1
  194.0 0.9 copy-start.2
  195.0 4.6 %copy-start.4 = (bf16[256,1024]{1,0:T(8,128)(2,1)S(1)}, bf16[256,1024]{1,0:T(8,128)(2,1)}, u32[]{:S(2)}) copy-start(bf16[256,1024]{1,0:T(8,128)(2,1)} %get-tuple-element.66) | copy-start | bytes 1572868

commit v8 on v7

--- a/solution.py
+++ b/solution.py
@@ -44,11 +44,11 @@
 def front_kernel(
     span,
     x, og, lengths, taps_own, log_own, cbias_own, dbias_own, skip_own, gain_own,
-    in_own, out_own, xp_own, dt_own,
+    xp_tall, in_own, out_own, dt_own,
     hidden_out, step_low, final,
     held_all, normed_full, bg_full, lead_full, slope_full, u_full, sig_full, delta_full, bw_full,
     cw_full, dy_full, gated_full, zg_full, in_full, xp_full, dt_full, small_full,
-    in_w, out_w, xp, dt, small, small_own, hx, acc, zacc, normed, v, proj, ends, sums,
+    in_w, out_w, xp, dt, small, small_own, xp_own, hx, acc, zacc, normed, v, proj, ends, sums,
     ends_in, sums_in, bg, mask, lead, slope, u, sig, delta, bw, cw, gg, dy, y, gated, zg,
     start, held,
     send, recv, halo, relay_send, relay_recv, sums_send, sums_recv, local, keep, held_sem,
@@ -81,6 +81,8 @@
         return carry
 
     lax.fori_loop(1, span, greet, 0)
+    blank = jnp.zeros((LANES - xp_tall.shape[0], share), BF16)
+    xp_own[...] = jnp.concatenate([xp_tall[...], blank], 0).T
     small_own[...] = jnp.zeros(small_own.shape, F32)
     small_own[:state] = log_own[...]
     small_own[state:at_bias] = taps_own[...]
@@ -199,8 +201,55 @@
         for kind, owner, q in diagonal:
             arrived(p, 6 + kind, owner, 1 - d, q)
 
+    odd = lax.rem(s, 2)
+    across_seq = {"seq": s + 1 - 2 * odd}
+    owners = (fx, fx, fy, fy, fd, fd, fx, fy, fd)
+    thirds = (0, 1, 0, 1, 0, 1, 2, 2, 2)
+
+    def third(ref, p, base, half, which):
+        _, _, _, cols = plan[p]
+        high = plan[p][0].shape[0]
+        tall = high // 2
+        wide = tall if cols is None else cols[1] - cols[0]
+        side = wide * 5 // 16
+        first = (odd * (wide - side), side, (1 - odd) * (wide - side))[which]
+        size = (side, wide - 2 * side, side)[which]
+        row = base + half * tall
+        if cols is None:
+            return ref.at[pl.ds(pl.multiple_of(row + first, GROUP), size)]
+        col = pl.ds(pl.multiple_of(cols[0] + first, LANES), size)
+        return ref.at[pl.ds(pl.multiple_of(row, tall), tall), col]
+
+    def place(p, kind, half):
+        high = plan[p][0].shape[0]
+        return third(plan[p][1], p, owners[kind] * high, half, thirds[kind])
+
+    def start_thirds(p):
+        for kind, which, who in ((0, 0, tox), (3, 1, toy), (1, 1, tox), (2, 0, toy)):
+            to = third(plan[p][1], p, f * plan[p][0].shape[0], d, which)
+            go(copy(third(plan[p][0], p, 0, d, which), to, p, kind, who))
+
+    def serve(p, kinds):
+        onward = {0: ((4, toy), (6, across_seq)), 2: ((7, across_seq),), 3: ((5, tox),)}
+        onward[4] = ((8, across_seq),)
+        for kind in kinds:
+            w = place(p, kind, d)
+            copy(w, w, p, kind, sib).wait_recv()
+            for to, who in onward.get(kind, ()):
+                go(copy(w, w, p, to, who))
+            go(copy(w, w, p, 9 + kind, sib))
+
+    serve_first = lambda p: serve(p, (0, 3, 1, 2))
+    serve_rest = lambda p: serve(p, (4, 5, 6, 7, 8))
+
+    def ready(p):
+        own_ready(p)
+        for kind in range(9):
+            w = place(p, kind, 1 - d)
+            copy(w, w, p, 9 + kind, sib).wait_recv()
+
     small_start(0)
-    start_own(STREAM)
+    start_thirds(STREAM)
     for p in (STREAM, PROJ, STEP, GATE, OUT):
         place_own(p)
     pltpu.make_async_copy(
@@ -259,33 +308,24 @@
     for c in range(seqs):
         normed[rows + c * GROUP : rows + (c + 1) * GROUP] = normalised(hx[c])
 
-    def project(total, high, first, owner, fresh):
-        shard = pl.ds(pl.multiple_of(owner * (width // 4), width // 4), width // 4)
-        left = normed[:high, shard]
-
+    def project(total, high, first):
         def one(t, carry):
             cols = pl.ds(pl.multiple_of(t * CHUNK, CHUNK), CHUNK)
-            right = in_w[shard, pl.ds(pl.multiple_of(first + t * CHUNK, CHUNK), CHUNK)]
-            part = dot(left, right)
-            total[:, cols] = part if fresh else total[:, cols] + part
+            right = in_w[:, pl.ds(pl.multiple_of(first + t * CHUNK, CHUNK), CHUNK)]
+            total[:, cols] = dot(normed[:high], right)
             return carry
 
         lax.fori_loop(0, inner // CHUNK, one, 0)
 
     tall = rows + seqs * GROUP
-    own_ready(STREAM)
-    project(acc, tall, 0, f, True)
-    serve_near(STREAM)
+    serve_first(STREAM)
     small_start(1)
     start_own(PROJ, True)
     start_own(STEP, True)
     start_own(GATE)
-    near_ready(STREAM)
-    project(acc, tall, 0, fx, False)
-    project(acc, tall, 0, fy, False)
-    serve_far(STREAM)
-    far_ready(STREAM)
-    project(acc, tall, 0, fd, False)
+    serve_rest(STREAM)
+    ready(STREAM)
+    project(acc, tall, 0)
     small_ready(1)
 
     tile = 2 * LANES
@@ -540,13 +580,7 @@
     far_ready(GATE)
     stash((11, (in_w, in_full)))
 
-    def gate_project(t, carry):
-        cols = columns(t, CHUNK)
-        right = in_w[:, pl.ds(pl.multiple_of(inner + t * CHUNK, CHUNK), CHUNK)]
-        zacc[:, cols] = dot(normed[:rows], right)
-        return carry
-
-    lax.fori_loop(0, parts, gate_project, 0)
+    project(zacc, rows, inner)
     serve_near(OUT)
     lax.fori_loop(parts // 2, parts, sweep_block, 0)
     serve_far(OUT)
@@ -623,10 +657,10 @@
         held_copy(b).wait()
 
 
-def front(x, og, lengths, taps, logs, cbias, dbias, skip, gain, in_own, out_own, xp_own, dt_own, seqs):
+def front(x, og, lengths, taps, logs, cbias, dbias, skip, gain, xp_tall, in_own, out_own, dt_own, seqs):
     rows, width = x.shape
     share, inner = taps.shape[1], 4 * taps.shape[1]
-    state, rank, used = logs.shape[0], dt_own.shape[0], xp_own.shape[1]
+    state, rank, used = logs.shape[0], dt_own.shape[0], LANES
     ctx = rows // seqs
     span = lax.axis_size("seq")
     parts = inner // CHUNK
@@ -656,8 +690,8 @@
     return pl.pallas_call(
         functools.partial(front_kernel, span),
         in_specs=[whole, whole, pl.BlockSpec(memory_space=pltpu.SMEM)]
-        + [whole] * 6
-        + [anywhere] * 4,
+        + [whole] * 7
+        + [anywhere] * 3,
         out_specs=[whole] * 3 + [anywhere] * (1 + len(kept)),
         out_shape=[
             shape((rows, width), BF16),
@@ -673,6 +707,7 @@
             vmem((rank, inner), BF16),
             vmem((32, inner), F32),
             vmem((32, share), F32),
+            vmem((share, LANES), BF16),
             vmem((seqs, GROUP, width), BF16),
             vmem((rows + seqs * GROUP, inner), F32),
             vmem((rows, inner), F32),
@@ -699,8 +734,8 @@
             vmem((parts, rows, CHUNK), BF16),
             vmem((seqs, state, inner), F32),
             vmem((HELD,) + held, BF16),
-            dma((6, 12)),
-            dma((6, 12)),
+            dma((6, 18)),
+            dma((6, 18)),
             dma((2, seqs)),
             dma((span, seqs)),
             dma((span, seqs)),
@@ -714,7 +749,7 @@
             collective_id=0, has_side_effects=True, vmem_limit_bytes=63 << 20
         ),
         name="front",
-    )(x, og, lengths, taps, logs, cbias, dbias, skip, gain, in_own, out_own, xp_own, dt_own)
+    )(x, og, lengths, taps, logs, cbias, dbias, skip, gain, xp_tall, in_own, out_own, dt_own)
 
 
 def back_kernel(
@@ -1292,7 +1327,12 @@
     )(gated, bg, step_low, final, small, x, og, *far)
 
 
-def finish_kernel(state, rank, used, in_sum, out_sum, rest, gain, in_w, taps, cbias, xp, dt, dbias, logs, skip, out_w):
+def finish_kernel(
+    state, rank, used, in_sum, out_sum, rest, hidden, grad,
+    gain, in_w, taps, cbias, xp, dt, dbias, logs, skip, out_w, hidden_out, grad_out,
+):
+    hidden_out[...] = hidden[...]
+    grad_out[...] = grad[...]
     in_w[...] = in_sum[...].astype(F32)
     out_w[...] = out_sum[...].astype(F32)
     at = TAPS + state
@@ -1304,28 +1344,31 @@
     skip[...] = row(at + 2)
     gain[...] = row(at + 3)[:, : gain.shape[1]]
     dt[...] = row(at + 4, rank)
-    xp[...] = row(at + 4 + rank, used).T
-
-
-def finish(in_sum, out_sum, rest, state, rank, used):
-    steps = 4
+    xp[...] = row(at + 4 + rank, used)
+
+
+def finish(in_sum, out_sum, rest, hidden, grad, state, rank, used):
+    steps = 2
     share = rest.shape[1]
     tall = lambda v: pl.BlockSpec((v.shape[0] // steps, v.shape[1]), lambda i: (i, 0))
     fixed = lambda *v: pl.BlockSpec(v, lambda i: (0, 0))
-    small = [(1, in_sum.shape[0]), (TAPS, share), (1, share), (share, used), (rank, share)]
+    small = [(1, in_sum.shape[0]), (TAPS, share), (1, share), (used, share), (rank, share)]
     small += [(1, share), (state, share), (1, share)]
     shape = lambda v: jax.ShapeDtypeStruct(v, F32)
     return pl.pallas_call(
         functools.partial(finish_kernel, state, rank, used),
         grid=(steps,),
-        in_specs=[tall(in_sum), tall(out_sum), fixed(*rest.shape)],
-        out_specs=[fixed(*small[0]), tall(in_sum)] + [fixed(*v) for v in small[1:]] + [tall(out_sum)],
+        in_specs=[tall(in_sum), tall(out_sum), fixed(*rest.shape), tall(hidden), tall(grad)],
+        out_specs=[fixed(*small[0]), tall(in_sum)]
+        + [fixed(*v) for v in small[1:]]
+        + [tall(out_sum), tall(hidden), tall(grad)],
         out_shape=[shape(small[0]), shape(in_sum.shape)]
         + [shape(v) for v in small[1:]]
-        + [shape(out_sum.shape)],
-        compiler_params=pltpu.CompilerParams(vmem_limit_bytes=32 << 20),
+        + [shape(out_sum.shape)]
+        + [jax.ShapeDtypeStruct(v.shape, v.dtype) for v in (hidden, grad)],
+        compiler_params=pltpu.CompilerParams(vmem_limit_bytes=63 << 20),
         name="finish",
-    )(in_sum, out_sum, rest)
+    )(in_sum, out_sum, rest, hidden, grad)
 
 
 def body(
@@ -1340,13 +1383,12 @@
     row = lambda v: v.reshape(1, -1)
     x, og = hidden_in.reshape(rows, width), out_grad.reshape(rows, width)
     used = xproj_weight.shape[1]
-    xp_own = jnp.pad(xproj_weight, ((0, 0), (0, LANES - used)))
     (
         hidden_out, step_low, final, held, normed, branch_grad, lead, slope, u, sig, delta,
         b_wide, c_wide, y_grad, gated, z_grad, in_matrix, proj_matrix, step_matrix, small,
     ) = front(
         x, og, lengths, conv_weight, a_log, row(conv_bias), row(dt_bias), row(skip_gain),
-        row(norm_gain), in_weight, out_weight, xp_own, dt_weight, seqs,
+        row(norm_gain), xproj_weight.T, in_weight, out_weight, dt_weight, seqs,
     )
     far = (
         held, normed, lead, slope, u, sig, delta, b_wide, c_wide, y_grad, z_grad, in_matrix,
@@ -1355,13 +1397,13 @@
     input_grad, out_sum, in_sum, rest = back(
         gated, branch_grad, step_low, final, small, x, og, far
     )
-    gain, in_w, taps_grad, cbias, proj_w, step_w, dbias, logs, skip, out_w = finish(
-        in_sum, out_sum, rest, state, rank, used
-    )
+    (
+        gain, in_w, taps_grad, cbias, proj_w, step_w, dbias, logs, skip, out_w, hidden_out, input_grad,
+    ) = finish(in_sum, out_sum, rest, hidden_out, input_grad, state, rank, used)
     flat = lambda v: v.reshape(-1)
     return (
         hidden_out.reshape(seqs, ctx, width), input_grad.reshape(seqs, ctx, width), flat(gain), in_w,
-        taps_grad, flat(cbias), proj_w, step_w, flat(dbias), logs, flat(skip), out_w,
+        taps_grad, flat(cbias), proj_w.T, step_w, flat(dbias), logs, flat(skip), out_w,
     )
 
 

time: 204 us -> 196 us (0.961)
  local copies, waits for them, and re-layouts: 7.85 us -> 0 us
    unnamed x14 -> x0, local copies, waits for them, and re-layouts: 7.16 us -> none
    pallas_call x1, Pallas kernels: 3.01 us -> 5.41 us  [finish(): pl.pallas_call(functools.partial(finish_kernel, state, rank, used), grid=...]
where the time goes in v8:
time: 196 us; the launch traced here: 193 us
  Pallas kernels  192 us (98%)
    pallas_call x1, Pallas kernels, back(): pl.pallas_call(functools.partial(back_kernel, span, state, rank), in_spec...  101 us
    pallas_call x1, Pallas kernels, front(): pl.pallas_call(functools.partial(front_kernel, span), in_specs=[whole, wh...  85.5 us
    pallas_call x1, Pallas kernels, finish(): pl.pallas_call(functools.partial(finish_kernel, state, rank, used), grid=...  5.41 us

profile of v8, /device:TPU:25, one launch (start us, length us, event | category | flops | bytes accessed | tf_op | source)
XLA Modules:
  0.0 193.1 jit_solution(6261974790255493308)
XLA Ops:
  0.6 85.5 %front.1 = (bf16[256,1024]{1,0:T(8,128)(2,1)}, bf16[256,64]{1,0:T(8,128)(2,1)}, f32[2,16,2048]{2,1,0:T(8,128)}, bf16[8,129,16,512]{3,2,1,0:T(8,128)(2,1)}, bf16[...) custom-call(bf16[256,1024]{1,0:T(8,128)(2,1)} %bitcast.14, ...), custom_call_target="tpu_custom_call" | custom-call | tf_op jit(solution)/shard_map/front/pallas_call | solution.py:690
  86.2 101.4 %back.1 = (bf16[256,1024]{1,0:T(8,128)(2,1)}, bf16[512,1024]{1,0:T(8,128)(2,1)}, bf16[256,4096]{1,0:T(8,128)(2,1)}, bf16[256,512]{1,0:T(8,128)(2,1)}) custom-call(bf16[256,2048]{1,0:T(8,128)(2,1)} %get-tuple-element.48.gated, bf16[256,1024]{1,0:T(8,128)(2,1)} %get-tuple-element.49.bg, bf16[256,64]{1,0:T(8,128)(2,1)} %get-tuple-element.50.step_low, ...), custom_call_target="tpu_custom_call" | custom-call | tf_op jit(solution)/shard_map/back/pallas_call | solution.py:1280
  187.5 5.4 %finish.1 = (f32[1,256]{1,0:T(1,128)}, f32[256,4096]{1,0:T(8,128)}, f32[4,512]{1,0:T(4,128)}, f32[1,512]{1,0:T(1,128)}, f32[96,512]{1,0:T(8,128)}, /*index=5*/f3...) custom-call(bf16[256,4096]{1,0:T(8,128)(2,1)} %get-tuple-element.67., ...), custom_call_target="tpu_custom_call" | custom-call | tf_op jit(solution)/shard_map/finish/pallas_call | solution.py:1358

commit v9 on v8

--- a/solution.py
+++ b/solution.py
@@ -754,12 +754,12 @@
 
 def back_kernel(
     span, state, rank,
-    gated, bg, step_low, final, small, x, og,
+    gated, bg, step_low, final, small, x_full, og_full,
     held_all, normed_full, lead_full, slope_full, u_full, sig_full, delta_full, bw_full,
     cw_full, dy_full, zg_full, in_full, xp_full, dt_full,
     input_grad, out_sum, in_sum, rest_sum,
     normed, lead, slope, u, sig, delta, bw, cw, dy, mixed, xp, dt, in_w, held, v, rl, cacc,
-    bacc, logs, sums,
+    bacc, logs, sums, x, og,
     pg, pg_full, cg, ng, rest, g, ra, rx, ry, zlo, zhi, tot,
     send, recv, halo, local, load, held_sem, in_sem,
 ):
@@ -794,7 +794,7 @@
     first_loads = len(pairs)
     pairs += [
         (mixed.at[:parts], zg_full), (normed, normed_full), (slope, slope_full), (lead, lead_full),
-        (xp, xp_full), (dt, dt_full),
+        (xp, xp_full), (dt, dt_full), (x, x_full), (og, og_full),
     ]
     loads = [pltpu.make_async_copy(src, dst, load.at[n]) for n, (dst, src) in enumerate(pairs)]
 
@@ -1279,7 +1279,7 @@
     (held, normed, lead, slope, u, sig, delta, bw, cw, dy, zg, in_full, xp, dt) = far
     return pl.pallas_call(
         functools.partial(back_kernel, span, state, rank),
-        in_specs=[whole] * 7 + [anywhere] * len(far),
+        in_specs=[whole] * 5 + [anywhere] * (2 + len(far)),
         out_specs=[whole, anywhere, anywhere, anywhere],
         out_shape=[
             shape((rows, width), BF16),
@@ -1300,6 +1300,8 @@
             vmem((rows, state, LANES), F32),
             vmem((state, inner), F32),
             vmem((2, 8, inner), F32),
+            like(x),
+            like(og),
             vmem((rows, LANES), BF16),
             vmem((rows, LANES), F32),
             vmem((seqs, ctx + 8, inner), F32),
@@ -1316,7 +1318,7 @@
             dma((17, n)),
             dma((2,)),
             dma((n, 2)),
-            dma((12 + 6,)),
+            dma((12 + 8,)),
             dma((2,)),
             dma((2,)),
         ],

time: 196 us -> 196 us (level)
  no operation moved by 1% of the time
where the time goes in v9:
time: 196 us; the launch traced here: 193 us
  Pallas kernels  192 us (98%)
    pallas_call x1, Pallas kernels, back(): pl.pallas_call(functools.partial(back_kernel, span, state, rank), in_spec...  101 us
    pallas_call x1, Pallas kernels, front(): pl.pallas_call(functools.partial(front_kernel, span), in_specs=[whole, wh...  85.5 us
    pallas_call x1, Pallas kernels, finish(): pl.pallas_call(functools.partial(finish_kernel, state, rank, used), grid=...  5.41 us

profile of v9, /device:TPU:25, one launch (start us, length us, event | category | flops | bytes accessed | tf_op | source)
XLA Modules:
  0.0 193.1 jit_solution(1425763072145370486)
XLA Ops:
  0.6 85.5 %front.1 = (bf16[256,1024]{1,0:T(8,128)(2,1)}, bf16[256,64]{1,0:T(8,128)(2,1)}, f32[2,16,2048]{2,1,0:T(8,128)}, bf16[8,129,16,512]{3,2,1,0:T(8,128)(2,1)}, bf16[...) custom-call(bf16[256,1024]{1,0:T(8,128)(2,1)} %bitcast.14, ...), custom_call_target="tpu_custom_call" | custom-call | tf_op jit(solution)/shard_map/front/pallas_call | solution.py:690
  86.2 101.3 %back.1 = (bf16[256,1024]{1,0:T(8,128)(2,1)}, bf16[512,1024]{1,0:T(8,128)(2,1)}, bf16[256,4096]{1,0:T(8,128)(2,1)}, bf16[256,512]{1,0:T(8,128)(2,1)}) custom-call(bf16[256,2048]{1,0:T(8,128)(2,1)} %get-tuple-element.48.gated, bf16[256,1024]{1,0:T(8,128)(2,1)} %get-tuple-element.49.bg, bf16[256,64]{1,0:T(8,128)(2,1)} %get-tuple-element.50.step_low, ...), custom_call_target="tpu_custom_call" | custom-call | tf_op jit(solution)/shard_map/back/pallas_call | solution.py:1280
  187.5 5.4 %finish.1 = (f32[1,256]{1,0:T(1,128)}, f32[256,4096]{1,0:T(8,128)}, f32[4,512]{1,0:T(4,128)}, f32[1,512]{1,0:T(1,128)}, f32[96,512]{1,0:T(8,128)}, /*index=5*/f3...) custom-call(bf16[256,4096]{1,0:T(8,128)(2,1)} %get-tuple-element.67., ...), custom_call_target="tpu_custom_call" | custom-call | tf_op jit(solution)/shard_map/finish/pallas_call | solution.py:1360
